TPU v7x, 768 devices: a whole 4x8x12 slice. The times are simulated.
768 devices in a mesh: row: 32 (over z_hi, y, core), col: 24 (over z_lo, x).
Axes of the slice: x: 4, y: 8, z: 12 (z_hi: 2, z_lo: 6; z = z_hi * 6 + z_lo), core: 2. Of those that a mesh axis runs over, the one named last changes fastest.
Arguments:
- amplitudes: bfloat16 [36864, 256], P(('row', 'col')), may hold values from -6 to 6
- residual_in: float32 [36864, 256], P(('row', 'col')), may hold values from -6 to 6
- v_tiles: bfloat16 [32, 24, 385, 2304], P('row', 'col'), as said below
- tile_map: int32 [32, 24, 385, 2], P('row', 'col'), may hold values from 0 to 767, as said below
Outputs:
- residual_out: float32 [36864, 256], P(('row', 'col'))
Inputs may be any that keep to these rules, and one draw needn't show every extreme that they name: `tile_map`: slot k of device (r, c) names tile row I = r * 24 + i and tile column J = j * 24 + c with 0 <= i < 24, 0 <= j < 32. Slot 0 is the diagonal tile I = J = r * 24 + c. Over all devices each unordered pair of distinct tiles is named in exactly one slot. Slots past a device's stored tiles repeat its diagonal tile; some devices use all 385 slots. `v_tiles`: slot 0 of every device is a symmetric tile; slots that repeat the diagonal tile past the first are zero.
All inputs are finite; a program needn't handle non-finite values.
Results may differ from a plain program's by a relative error of at most 0.0003.
Values may be sent and summed in bfloat16 or wider, within the bound.
No kernel may reach another device: no remote copies, remote signals or barrier semaphores. Data moves between devices by JAX's collectives and lax.ppermute only.
A program may use at most 64 MiB of HBM per device.

v0:
```python
import jax
import jax.numpy as jnp
from jax import lax
from jax.sharding import PartitionSpec as P


def per_device(amplitudes, residual_in, v_tiles, tile_map):
    ncols = lax.axis_size("col")
    nrows = lax.axis_size("row")
    my_row = lax.axis_index("row")
    my_col = lax.axis_index("col")
    width = amplitudes.shape[0]
    pairs = amplitudes.shape[1]
    slots = v_tiles.shape[2]
    tiles = v_tiles[0, 0].reshape(slots, width, width)
    entries = tile_map[0, 0]
    row_group = lax.all_gather(amplitudes, "col", axis=0, tiled=True)
    col_group = lax.all_gather(amplitudes, "row", axis=0, tiled=True)
    local_row = entries[:, 0] - my_row * ncols
    local_col = entries[:, 1] // ncols
    off_diag = entries[:, 0] != entries[:, 1]
    kept = jnp.where(off_diag[:, None, None], tiles, jnp.zeros_like(tiles))
    placed = (
        jnp.zeros((ncols, nrows, width, width), jnp.bfloat16).at[local_row, local_col].add(kept)
    )
    dense = placed.transpose(0, 2, 1, 3).reshape(ncols * width, nrows * width)
    diag_tile = tiles[0]
    direct = jnp.dot(dense, col_group, preferred_element_type=jnp.float32)
    own_cols = lax.dynamic_slice_in_dim(col_group, my_row * width, width, 0)
    own = jnp.dot(diag_tile, own_cols, preferred_element_type=jnp.float32)
    row_total = lax.psum_scatter(
        direct.reshape(ncols, width, pairs).at[my_col].add(own).reshape(ncols * width, pairs),
        "col",
        scatter_dimension=0,
        tiled=True,
    )
    mirror = lax.dot_general(
        dense, row_group, (((0,), (0,)), ((), ())), preferred_element_type=jnp.float32
    )
    col_total = lax.psum_scatter(
        mirror.reshape(nrows, width, pairs).reshape(nrows * width, pairs),
        "row",
        scatter_dimension=0,
        tiled=True,
    )
    return residual_in + row_total + col_total


def solution(mesh):
    return jax.shard_map(
        per_device,
        mesh=mesh,
        in_specs=(
            P(("row", "col"), None),
            P(("row", "col"), None),
            P("row", "col", None, None),
            P("row", "col", None, None),
        ),
        out_specs=P(("row", "col"), None),
        check_vma=False,
    )
```

profile of v0, /device:TPU:8, one launch (start us, length us, event | category | flops | bytes accessed | tf_op | source)
XLA Modules:
  0.0 519.2 jit_solution(15735935563187239824)
XLA Ops:
  6.5 0.0 reduce-scatter.5.cloned.1.call-start
  6.5 0.8 compare_reduce_fusion
  7.3 0.8 or_select_fusion
  8.1 2.7 copy.7
  10.8 1.6 broadcast_select_fusion
  12.4 6.9 %copy.8 = bf16[385,48,48]{2,1,0:T(8,128)(2,1)} copy(bf16[385,48,48]{0,2,1:T(8,128)(2,1)} %broadcast_select_fusion) | data formatting | bytes 3548160 | tf_op jit(solution)/shard_map/jit(_where)/select_n | solution.py:22
  19.4 5.7 %broadcast_in_dim.18 = bf16[24,32,48,48]{3,2,1,0:T(8,128)(2,1)} broadcast(bf16[]{:T(256)} %constant.39.clone.1), dimensions={} | broadcast | bytes 3538946 | tf_op jit(solution)/shard_map/broadcast_in_dim | solution.py:24
  25.0 59.2 %scatter_fusion = bf16[24,32,48,48]{3,2,1,0:T(8,128)(2,1)} fusion(bf16[24,32,48,48]{3,2,1,0:T(8,128)(2,1)} %broadcast_in_dim.18, s32[385]{0:T(512)S(1)} %bitcast.28, bf16[385,48,48]{2,1,0:T(8,128)(2,1)} %copy.8), kind=kCustom, calls=%fused_computation | custom fusion | flops 887040 | bytes 5325320 | tf_op jit(solution)/shard_map/scatter-add | solution.py:24
  84.2 9.7 %copy.9 = bf16[24,48,32,48]{3,2,1,0:T(8,128)(2,1)} copy(bf16[24,48,32,48]{3,1,2,0:T(8,128)(2,1)} %bitcast.27) | data formatting | bytes 7077888 | tf_op jit(solution)/shard_map/transpose | solution.py:26
  93.9 17.4 %reshape.57 = bf16[1152,1536]{1,0:T(8,128)(2,1)S(1)} reshape(bf16[24,48,32,48]{3,2,1,0:T(8,128)(2,1)} %copy.9) | data formatting | bytes 7077888 | tf_op jit(solution)/shard_map/reshape | solution.py:26
  111.4 89.2 %all_gather.7 = bf16[1152,256]{1,0:T(8,128)(2,1)S(1)} all-gather(bf16[48,256]{1,0:T(8,128)(2,1)} %param.6), channel_id=1, replica_groups=mesh['row'=32,'col'=24] {'col'}, dimensions={0}, use_global_device_ids=true | all-gather | bytes 614400 | tf_op jit(solution)/shard_map/all_gather | solution.py:17
  200.6 2.4 fusion.8
  203.0 0.0 reduce-scatter.5.cloned.1.call-update
  203.0 0.0 copy-start
  203.0 0.0 reduce-scatter.3.cloned.1.call-start
  203.0 17.4 %dot_general.11 = bf16[24,48,1536]{2,1,0:T(8,128)(2,1)S(1)} reshape(bf16[24,48,32,48]{3,2,1,0:T(8,128)(2,1)} %copy.9) | data formatting | bytes 7077888 | tf_op jit(solution)/shard_map/dot_general | solution.py:28
  220.5 1.4 slice_reduce_fusion
  221.9 0.8 squeeze.5
  222.7 0.0 copy-done
  222.7 0.8 and_reduce_fusion
  223.5 67.7 %all_gather.6 = bf16[1536,256]{1,0:T(8,128)(2,1)S(1)} all-gather(bf16[48,256]{1,0:T(8,128)(2,1)} %param.6), channel_id=1, replica_groups=mesh['row'=32,'col'=24] {'row'}, dimensions={0}, use_global_device_ids=true | all-gather | bytes 811008 | tf_op jit(solution)/shard_map/all_gather | solution.py:18
  291.2 2.1 fusion.3
  293.3 2.2 fusion.2
  295.5 0.0 reduce-scatter.3.cloned.1.call-update
  295.5 53.3 %reduce-scatter.5.cloned.1.call-done = f32[48,256]{1,0:T(8,128)} async-done(((f32[1536,256]{1,0:T(8,128)}), f32[48,256]{1,0:T(8,128)}) %reduce-scatter.5.cloned.1.call-update) | async-done | bytes 49168 | tf_op jit(solution)/shard_map/reduce_scatter | solution.py:40
  348.8 162.1 %reduce-scatter.3.cloned.1.call-done = f32[48,256]{1,0:T(8,128)} async-done(((f32[1152,256]{1,0:T(8,128)}), f32[48,256]{1,0:T(8,128)}) %reduce-scatter.3.cloned.1.call-update) | async-done | bytes 49168 | tf_op jit(solution)/shard_map/reduce_scatter | solution.py:31
  510.8 1.5 add_add_fusion
Async XLA Ops:
  6.5 342.3 %reduce-scatter.5.cloned.1.call-start = ((), (), s32[]{:S(2)}) async-start(), calls=%async_computation.3 | async-start | bytes 1622016 | tf_op jit(solution)/shard_map/reduce_scatter | solution.py:40
  203.0 19.7 %copy-start = (s32[3]{0:T(128)S(1)}, s32[3]{0:T(128)}, u32[]{:S(2)}) copy-start(s32[3]{0:T(128)} %constant.48.clone.1) | copy-start | bytes 40
  203.0 307.9 %reduce-scatter.3.cloned.1.call-start = ((), (), s32[]{:S(2)}) async-start(), calls=%async_computation.2 | async-start | bytes 1228800 | tf_op jit(solution)/shard_map/reduce_scatter | solution.py:31
Sparse Core Ops, SparseCore 0:
  203.1 145.6 reduce-scatter.4
  352.2 158.6 reduce-scatter.2
where the time goes:
time: 520 us; the launch traced here: 519 us
  waiting for transfers between devices  215 us (41%)
  blocking collectives  157 us (30%)
  other arithmetic  64.6 us (12%)
  local copies, waits for them, and re-layouts  62.1 us (12%)
  between operations  13.5 us (3%)
  matrix products  6.66 us (1%)
    reduce_scatter x1, waiting for transfers between devices, per_device(): lax.psum_scatter(direct.reshape(ncols, width, pairs).at[my_col].add(own)....  162 us
    all_gather x1, blocking collectives, per_device(): row_group = lax.all_gather(amplitudes, 'col', axis=0, tiled=True)  89.2 us
    all_gather x1, blocking collectives, per_device(): col_group = lax.all_gather(amplitudes, 'row', axis=0, tiled=True)  67.7 us
    scatter-add x1, other arithmetic, per_device(): jnp.zeros((ncols, nrows, width, width), jnp.bfloat16)  59.2 us
    reduce_scatter x1, waiting for transfers between devices, per_device(): lax.psum_scatter(mirror.reshape(nrows, width, pairs).reshape(nrows * widt...  53.3 us
    dot_general x1, local copies, waits for them, and re-layouts, per_device(): direct = jnp.dot(dense, col_group, preferred_element_type=jnp.float32)  17.4 us
    reshape x1, local copies, waits for them, and re-layouts, per_device(): dense = placed.transpose(0, 2, 1, 3).reshape(ncols * width, nrows * width)  17.4 us
  transfers between devices with their start and end apart: 2, of which 2 were waited for; matrix products, arithmetic and copies ran while one was open for 5% of the time, Pallas kernels for 0%

commit v1 on v0

v1 whole, which is shorter than its diff:
```python
import jax
import jax.numpy as jnp
from jax import lax
from jax.experimental import pallas as pl
from jax.experimental.pallas import tpu as pltpu
from jax.sharding import Mesh, PartitionSpec as P

AXES = ("zh", "y", "co", "zl", "x")
SIZES = (2, 8, 2, 6, 4)
ROW_AXES = ("zh", "y", "co")
COL_AXES = ("zl", "x")
TILE = 48
PAIRS = 256
NCOLS = 24
NROWS = 32
PAD = 32
HALF = NROWS * TILE // 2
WIDE = NROWS * TILE
TALL = PAD * TILE
GROUP = 8
LANES = GROUP * TILE


def place_kernel(map_ref, v_ref, x_ref, onehot, dense):
    slots = v_ref.shape[0]
    places = NROWS * PAD

    @pl.when(pl.program_id(0) == 0)
    def _():
        my_zh, my_y, my_co = (lax.axis_index(a) for a in ROW_AXES)
        my_row = my_zh * 16 + my_y * 2 + my_co
        first = map_ref[0:1, :]
        second = map_ref[1:2, :]
        i = first - my_row * NCOLS
        j = (second * 2731) >> 16
        i_place = (i & 3) * 6 + (i >> 2)
        j_place = ((j & 1) ^ my_co) * 16 + ((j >> 1) & 7) * 2 + ((j >> 4) ^ my_zh)
        place = j_place * PAD + i_place
        weight = jnp.where(first == second, 0.5, 1.0)
        for start in range(0, places, 128):
            rows = lax.broadcasted_iota(jnp.int32, (128, slots), 0) + start
            onehot[start : start + 128, :] = jnp.where(rows == place, weight, 0.0).astype(
                jnp.bfloat16
            )

    for start in range(0, places, 256):
        dense[start : start + 256, :] = jnp.dot(
            onehot[start : start + 256, :], v_ref[...], preferred_element_type=jnp.float32
        ).astype(jnp.bfloat16)
    for s in range(GROUP):
        parts = [
            dense[j * PAD : (j + 1) * PAD, s * TILE : (s + 1) * TILE] for j in range(NROWS)
        ]
        x_ref[s * PAD : (s + 1) * PAD, :] = jnp.concatenate(parts, axis=1)


def place(tile_map, v_tiles):
    slots = v_tiles.shape[0]
    return pl.pallas_call(
        place_kernel,
        grid=(TILE // GROUP,),
        in_specs=[
            pl.BlockSpec((2, slots), lambda g: (0, 0)),
            pl.BlockSpec((slots, LANES), lambda g: (0, g)),
        ],
        out_specs=pl.BlockSpec((GROUP * PAD, WIDE), lambda g: (g, 0)),
        out_shape=jax.ShapeDtypeStruct((TALL, WIDE), jnp.bfloat16),
        scratch_shapes=[
            pltpu.VMEM((NROWS * PAD, slots), jnp.bfloat16),
            pltpu.VMEM((NROWS * PAD, LANES), jnp.bfloat16),
        ],
        compiler_params=pltpu.CompilerParams(vmem_limit_bytes=32 * 2**20),
        cost_estimate=pl.CostEstimate(
            flops=2 * 1024 * 512 * 2304, bytes_accessed=8 * 2**20, transcendentals=0
        ),
        name="place",
    )(tile_map, v_tiles)


def mirror_kernel(x_ref, a_ref, own_ref, other_ref, left, right, rows):
    wides = (left, right)
    for h, wide in enumerate(wides):
        lanes = slice(h * 128, h * 128 + 128)
        for i in range(NCOLS):
            wide[pl.ds(i, TILE, stride=PAD), :] = a_ref[i, :, lanes].astype(jnp.float32)
        for i in range(NCOLS, PAD):
            wide[pl.ds(i, TILE, stride=PAD), :] = jnp.zeros((TILE, 128), jnp.float32)
        rows[:, lanes] = wide[...].astype(jnp.bfloat16)
    for out, base in ((other_ref, HALF), (own_ref, 0)):
        for start in range(0, HALF, 256):
            out[start : start + 256, :] = lax.dot_general(
                x_ref[:, base + start : base + start + 256],
                rows[...],
                (((0,), (0,)), ((), ())),
                preferred_element_type=jnp.float32,
            )


def mirror(x, a):
    half = jax.ShapeDtypeStruct((HALF, PAIRS), jnp.float32)
    return pl.pallas_call(
        mirror_kernel,
        out_shape=(half, half),
        scratch_shapes=[
            pltpu.VMEM((TALL, 128), jnp.float32),
            pltpu.VMEM((TALL, 128), jnp.float32),
            pltpu.VMEM((TALL, PAIRS), jnp.bfloat16),
        ],
        compiler_params=pltpu.CompilerParams(vmem_limit_bytes=32 * 2**20),
        cost_estimate=pl.CostEstimate(
            flops=2 * TALL * WIDE * PAIRS, bytes_accessed=8 * 2**20, transcendentals=0
        ),
        name="mirror",
    )(x, a)


def direct_kernel(x_ref, own_ref, other_ref, out_ref, left, right):
    for start in range(0, TALL, 256):
        total = jnp.dot(
            x_ref[start : start + 256, :HALF], own_ref[...], preferred_element_type=jnp.float32
        ) + jnp.dot(
            x_ref[start : start + 256, HALF:], other_ref[...], preferred_element_type=jnp.float32
        )
        left[start : start + 256, :] = total[:, :128]
        right[start : start + 256, :] = total[:, 128:]
    for i in range(NCOLS):
        out_ref[i, :, :128] = left[pl.ds(i, TILE, stride=PAD), :]
        out_ref[i, :, 128:] = right[pl.ds(i, TILE, stride=PAD), :]


def direct(x, own, other):
    return pl.pallas_call(
        direct_kernel,
        out_shape=jax.ShapeDtypeStruct((NCOLS, TILE, PAIRS), jnp.float32),
        scratch_shapes=[
            pltpu.VMEM((TALL, 128), jnp.float32),
            pltpu.VMEM((TALL, 128), jnp.float32),
        ],
        compiler_params=pltpu.CompilerParams(vmem_limit_bytes=32 * 2**20),
        cost_estimate=pl.CostEstimate(
            flops=2 * TALL * WIDE * PAIRS, bytes_accessed=8 * 2**20, transcendentals=0
        ),
        name="direct",
    )(x, own, other)


SWAP = [(0, 1), (1, 0)]


def spread(block, axis, count):
    copies = jnp.broadcast_to(block[None], (count,) + block.shape)
    return lax.all_to_all(copies, axis, split_axis=0, concat_axis=0)


def per_device(amplitudes, residual_in, v_tiles, tile_map):
    far = lax.ppermute(amplitudes, "zh", SWAP)
    line = spread(amplitudes, "zl", 6)
    pair = jnp.stack([amplitudes, far])
    own = spread(pair, "y", 8).reshape(HALF, PAIRS)
    rows = spread(line, "x", 4).reshape(NCOLS, TILE, PAIRS)
    other = lax.ppermute(own, "co", SWAP)
    x = place(tile_map[0, 0].T, v_tiles[0, 0])

    keep, send = mirror(x, rows)
    got = lax.ppermute(send, "co", SWAP)
    ladder_rows = direct(x, own, other)
    col_parts = lax.all_to_all(
        ladder_rows.reshape(4, 6 * TILE, PAIRS), "x", split_axis=0, concat_axis=0
    )
    row_parts = lax.all_to_all(
        (keep + got).reshape(8, 2 * TILE, PAIRS), "y", split_axis=0, concat_axis=0
    )
    col_line = jnp.sum(col_parts, axis=0).reshape(6, TILE, PAIRS)
    col_line = lax.all_to_all(col_line, "zl", split_axis=0, concat_axis=0)
    row_pair = jnp.sum(row_parts, axis=0).reshape(2, TILE, PAIRS)
    row_far = lax.ppermute(row_pair[1], "zh", SWAP)
    return residual_in + row_pair[0] + jnp.sum(col_line, axis=0) + row_far


def solution(mesh):
    fine = Mesh(mesh.devices.reshape(SIZES), AXES)
    return jax.shard_map(
        per_device,
        mesh=fine,
        in_specs=(
            P(AXES, None),
            P(AXES, None),
            P(ROW_AXES, COL_AXES, None, None),
            P(ROW_AXES, COL_AXES, None, None),
        ),
        out_specs=P(AXES, None),
        check_vma=False,
    )
```

time: 520 us -> 141 us (0.27)
  the two profiles are of different devices: /device:TPU:8 before, /device:TPU:132 now
where the time goes in v1:
time: 141 us; the launch traced here: 140 us
  starting transfers between devices  53.6 us (38%)
  waiting for transfers between devices  43.5 us (31%)
  blocking collectives  20.8 us (15%)
  Pallas kernels  11.7 us (8%)
  local copies, waits for them, and re-layouts  6.8 us (5%)
  other arithmetic  3.25 us (2%)
    all_to_all x1, waiting for transfers between devices, per_device(): lax.all_to_all((keep + got).reshape(8, 2 * TILE, PAIRS), 'y', split_axis=...  22.8 us
    all_to_all x1, blocking collectives, spread(): return lax.all_to_all(copies, axis, split_axis=0, concat_axis=0)  20.8 us
    all_to_all x2, starting transfers between devices, spread(): return lax.all_to_all(copies, axis, split_axis=0, concat_axis=0)  12.8 us
    ppermute x1, starting transfers between devices, per_device(): far = lax.ppermute(amplitudes, 'zh', SWAP)  12.7 us
    ppermute x1, waiting for transfers between devices, per_device(): row_far = lax.ppermute(row_pair[1], 'zh', SWAP)  11.2 us
    ppermute x1, starting transfers between devices, per_device(): row_far = lax.ppermute(row_pair[1], 'zh', SWAP)  10 us
    pallas_call x1, Pallas kernels, place(): pl.pallas_call(place_kernel, grid=(TILE // GROUP,), in_specs=[pl.BlockSpe...  5.94 us
    all_to_all x1, starting transfers between devices, per_device(): col_line = lax.all_to_all(col_line, 'zl', split_axis=0, concat_axis=0)  5.79 us
  transfers between devices with their start and end apart: 9, of which 5 were waited for; matrix products, arithmetic and copies ran while one was open for 2% of the time, Pallas kernels for 8%

profile of v1, /device:TPU:132, one launch (start us, length us, event | category | flops | bytes accessed | tf_op | source)
XLA Modules:
  0.0 139.8 jit_solution(6096133567217374103)
XLA Ops:
  0.0 12.7 %collective-permute-start.1 = (bf16[48,256]{1,0:T(8,128)(2,1)}, bf16[48,256]{1,0:T(8,128)(2,1)S(1)}, u32[]{:S(2)}, u32[]{:S(2)}) collective-permute-start(bf16[48,256]{1,0:T(8,128)(2,1)} %param.4), channel_id=1, source_target_pairs={{0,384},{384,0},{1,385},{385,1},{2,386},{386,2},{3,387},{387,3},{4... | collective-permute-start | bytes 73736 | tf_op jit(solution)/shard_map/ppermute | solution.py:156
  12.7 2.0 %collective-permute-done.1 = bf16[48,256]{1,0:T(8,128)(2,1)S(1)} collective-permute-done((bf16[48,256]{1,0:T(8,128)(2,1)}, bf16[48,256]{1,0:T(8,128)(2,1)S(1)}, u32[]{:S(2)}, u32[]{:S(2)}) %collective-permute-start.1) | collective-permute-done | bytes 24608 | tf_op jit(solution)/shard_map/ppermute | solution.py:156
  14.8 0.7 pad_maximum_fusion
  15.5 0.0 copy-start.2
  15.5 0.0 copy-start.3
  15.5 20.8 %all_to_all.30 = bf16[8,2,48,256]{3,2,1,0:T(8,128)(2,1)S(1)} all-to-all(bf16[8,2,48,256]{3,2,1,0:T(8,128)(2,1)S(1)} %broadcast_in_dim.11), channel_id=1, replica_groups=mesh['zh'=2,'y'=8,'co'=2,'zl'=6,'x'=4] {'y'}, dimensions={0} | all-to-all | bytes 786432 | tf_op jit(solution)/shard_map/all_to_all | solution.py:152
  36.4 1.4 %broadcast_in_dim.8 = bf16[6,48,256]{2,1,0:T(8,128)(2,1)} broadcast(bf16[48,256]{1,0:T(8,128)(2,1)} %param.4), dimensions={1,2} | broadcast | bytes 172032 | tf_op jit(solution)/shard_map/broadcast_in_dim | solution.py:151
  37.8 8.0 %all-to-all-start = ((bf16[6,48,256]{2,1,0:T(8,128)(2,1)}), bf16[6,48,256]{2,1,0:T(8,128)(2,1)S(1)}, u32[]{:S(2)}, u32[]{:S(2)}) async-start(bf16[6,48,256]{2,1,0:T(8,128)(2,1)} %broadcast_in_dim.8), calls=%async_computation | async-start | bytes 294912 | tf_op jit(solution)/shard_map/all_to_all | solution.py:152
  45.8 1.9 %collective-permute-start.2 = (bf16[768,256]{1,0:T(8,128)(2,1)S(1)}, bf16[768,256]{1,0:T(8,128)(2,1)S(1)}, u32[]{:S(2)}, u32[]{:S(2)}) collective-permute-start(bf16[768,256]{1,0:T(8,128)(2,1)S(1)} %bitcast.12), channel_id=1, source_target_pairs={{0,24},{24,0},{1,25},{25,1},{2,26},{26,2},{3,27},{27,3},{4,28},{28... | collective-permute-start | bytes 1179656 | tf_op jit(solution)/shard_map/ppermute | solution.py:161
  47.7 5.2 %all-to-all-done = bf16[6,48,256]{2,1,0:T(8,128)(2,1)S(1)} async-done(((bf16[6,48,256]{2,1,0:T(8,128)(2,1)}), bf16[6,48,256]{2,1,0:T(8,128)(2,1)S(1)}, u32[]{:S(2)}, u32[]{:S(2)}) %all-to-all-start) | async-done | bytes 147488 | tf_op jit(solution)/shard_map/all_to_all | solution.py:152
  52.9 0.9 broadcast_in_dim.9
  53.8 4.8 %all-to-all-start.1 = ((bf16[4,6,48,256]{3,2,1,0:T(8,128)(2,1)}), bf16[4,6,48,256]{3,2,1,0:T(8,128)(2,1)S(1)}, u32[]{:S(2)}, u32[]{:S(2)}) async-start(bf16[4,6,48,256]{3,2,1,0:T(8,128)(2,1)} %broadcast_in_dim.9), calls=%async_computation.1 | async-start | bytes 1179648 | tf_op jit(solution)/shard_map/all_to_all | solution.py:152
  58.6 0.0 copy-done.2
  58.6 0.0 copy-done.3
  58.6 5.9 %place.1.x_ref = bf16[1536,1536]{1,0:T(8,128)(2,1)S(1)} custom-call(s32[2,385]{1,0:T(2,128)S(1)} %bitcast.15, bf16[385,2304]{1,0:T(8,128)(2,1)S(1)} %bitcast.14), custom_call_target="tpu_custom_call" | custom-call | flops 2415919104 | bytes 8388608 | tf_op jit(solution)/shard_map/place/pallas_call | solution.py:59
  64.6 0.0 collective-permute-done.2.other_ref
  64.6 3.3 %direct.1 = f32[24,48,256]{2,1,0:T(8,128)} custom-call(bf16[1536,1536]{1,0:T(8,128)(2,1)S(1)} %place.1.x_ref, bf16[768,256]{1,0:T(8,128)(2,1)S(1)} %bitcast.13, bf16[768,256]{1,0:T(8,128)(2,1)S(1)} %collective-permute-done.2.other_ref), custom_call_target="tpu_custom_call" | custom-call | flops 1207959552 | bytes 8388608 | tf_op jit(solution)/shard_map/direct/pallas_call | solution.py:132
  67.8 0.0 copy-start
  67.8 2.1 %copy-done = bf16[1536,1536]{1,0:T(8,128)(2,1)} copy-done((bf16[1536,1536]{1,0:T(8,128)(2,1)}, bf16[1536,1536]{1,0:T(8,128)(2,1)S(1)}, u32[]{:S(2)}) %copy-start) | copy-done | bytes 4718616
  70.0 0.0 all-to-all-done.1
  70.0 4.8 %all-to-all-start.4 = ((f32[4,288,256]{2,1,0:T(8,128)}), f32[4,288,256]{2,1,0:T(8,128)S(1)}, u32[]{:S(2)}, u32[]{:S(2)}) async-start(f32[4,288,256]{2,1,0:T(8,128)} %bitcast.8), calls=%async_computation.4 | async-start | bytes 2359296 | tf_op jit(solution)/shard_map/all_to_all | solution.py:167
  74.8 0.0 copy-start.1
  74.8 2.3 %copy-done.1 = bf16[1536,1536]{1,0:T(8,128)(2,1)S(1)} copy-done((bf16[1536,1536]{1,0:T(8,128)(2,1)S(1)}, bf16[1536,1536]{1,0:T(8,128)(2,1)}, u32[]{:S(2)}) %copy-start.1) | copy-done | bytes 4718616
  77.1 2.5 %mirror.1 = (f32[768,256]{1,0:T(8,128)S(1)}, f32[768,256]{1,0:T(8,128)S(1)}) custom-call(bf16[1536,1536]{1,0:T(8,128)(2,1)S(1)} %copy-done.1, bf16[24,48,256]{2,1,0:T(8,128)(2,1)S(1)} %bitcast.11), custom_call_target="tpu_custom_call" | custom-call | flops 1207959552 | bytes 8388608 | tf_op jit(solution)/shard_map/mirror/pallas_call | solution.py:101
  79.6 1.9 %collective-permute-start = (f32[768,256]{1,0:T(8,128)S(1)}, f32[768,256]{1,0:T(8,128)S(1)}, u32[]{:S(2)}, u32[]{:S(2)}) collective-permute-start(f32[768,256]{1,0:T(8,128)S(1)} %get-tuple-element.8), channel_id=1, source_target_pairs={{0,24},{24,0},{1,25},{25,1},{2,26},{26,2},{3,27},{27,3},{4,28},{28... | collective-permute-start | bytes 2359304 | tf_op jit(solution)/shard_map/ppermute | solution.py:165
  81.6 2.3 %collective-permute-done = f32[768,256]{1,0:T(8,128)S(1)} collective-permute-done((f32[768,256]{1,0:T(8,128)S(1)}, f32[768,256]{1,0:T(8,128)S(1)}, u32[]{:S(2)}, u32[]{:S(2)}) %collective-permute-start) | collective-permute-done | bytes 786464 | tf_op jit(solution)/shard_map/ppermute | solution.py:165
  83.8 1.0 add.12
  84.8 0.0 all-to-all-done.4
  84.8 3.5 %all-to-all-start.2 = ((f32[8,96,256]{2,1,0:T(8,128)}), f32[8,96,256]{2,1,0:T(8,128)S(1)}, u32[]{:S(2)}, u32[]{:S(2)}) async-start(f32[8,96,256]{2,1,0:T(8,128)} %bitcast.4), calls=%async_computation.2 | async-start | bytes 1572864 | tf_op jit(solution)/shard_map/all_to_all | solution.py:170
  88.4 0.0 copy-start.4
  88.4 0.8 reduce_sum.28
  89.2 22.8 %all-to-all-done.2 = f32[8,96,256]{2,1,0:T(8,128)S(1)} async-done(((f32[8,96,256]{2,1,0:T(8,128)}), f32[8,96,256]{2,1,0:T(8,128)S(1)}, u32[]{:S(2)}, u32[]{:S(2)}) %all-to-all-start.2) | async-done | bytes 786464 | tf_op jit(solution)/shard_map/all_to_all | solution.py:170
  112.0 5.8 %all-to-all-start.5 = ((f32[6,48,256]{2,1,0:T(8,128)}), f32[6,48,256]{2,1,0:T(8,128)S(1)}, u32[]{:S(2)}, u32[]{:S(2)}) async-start(f32[6,48,256]{2,1,0:T(8,128)} %bitcast.9), calls=%async_computation.5 | async-start | bytes 589824 | tf_op jit(solution)/shard_map/all_to_all | solution.py:174
  117.8 0.1 reduce_sum.27
  117.9 10.0 %collective-permute-start.3 = (f32[48,256]{1,0:T(8,128)S(1)}, f32[48,256]{1,0:T(8,128)S(1)}, u32[]{:S(2)}, u32[]{:S(2)}) collective-permute-start(f32[48,256]{1,0:T(8,128)S(1)} %slice.11), channel_id=1, source_target_pairs={{0,384},{384,0},{1,385},{385,1},{2,386},{386,2},{3,387},{387,3},{4... | collective-permute-start | bytes 147464 | tf_op jit(solution)/shard_map/ppermute | solution.py:176
  127.9 0.0 all-to-all-done.5
  128.0 11.2 %collective-permute-done.3 = f32[48,256]{1,0:T(8,128)S(1)} collective-permute-done((f32[48,256]{1,0:T(8,128)S(1)}, f32[48,256]{1,0:T(8,128)S(1)}, u32[]{:S(2)}, u32[]{:S(2)}) %collective-permute-start.3) | collective-permute-done | bytes 49184 | tf_op jit(solution)/shard_map/ppermute | solution.py:176
  139.1 0.0 copy-done.4
  139.1 0.6 fusion.1
  (3 shorter events, 0.1 us)
Async XLA Ops:
  0.0 14.8 %collective-permute-start.1 = (bf16[48,256]{1,0:T(8,128)(2,1)}, bf16[48,256]{1,0:T(8,128)(2,1)S(1)}, u32[]{:S(2)}, u32[]{:S(2)}) collective-permute-start(bf16[48,256]{1,0:T(8,128)(2,1)} %param.4), channel_id=1, source_target_pairs={{0,384},{384,0},{1,385},{385,1},{2,386},{386,2},{3,387},{387,3},{4... | collective-permute-start | bytes 73736 | tf_op jit(solution)/shard_map/ppermute | solution.py:156
  15.5 43.1 %copy-start.2 = (bf16[1,1,385,2304]{3,2,1,0:T(8,128)(2,1)S(1)}, bf16[1,1,385,2304]{3,2,1,0:T(8,128)(2,1)}, u32[]{:S(2)}) copy-start(bf16[1,1,385,2304]{3,2,1,0:T(8,128)(2,1)} %param.6) | copy-start | bytes 5322244
  15.5 43.1 %copy-start.3 = (s32[1,1,385,2]{2,3,1,0:T(2,128)S(1)}, s32[1,1,385,2]{2,3,1,0:T(2,128)}, u32[]{:S(2)}) copy-start(s32[1,1,385,2]{2,3,1,0:T(2,128)} %param.7) | copy-start | bytes 9244
  37.8 15.1 %all-to-all-start = ((bf16[6,48,256]{2,1,0:T(8,128)(2,1)}), bf16[6,48,256]{2,1,0:T(8,128)(2,1)S(1)}, u32[]{:S(2)}, u32[]{:S(2)}) async-start(bf16[6,48,256]{2,1,0:T(8,128)(2,1)} %broadcast_in_dim.8), calls=%async_computation | async-start | bytes 294912 | tf_op jit(solution)/shard_map/all_to_all | solution.py:152
  45.8 18.7 %collective-permute-start.2 = (bf16[768,256]{1,0:T(8,128)(2,1)S(1)}, bf16[768,256]{1,0:T(8,128)(2,1)S(1)}, u32[]{:S(2)}, u32[]{:S(2)}) collective-permute-start(bf16[768,256]{1,0:T(8,128)(2,1)S(1)} %bitcast.12), channel_id=1, source_target_pairs={{0,24},{24,0},{1,25},{25,1},{2,26},{26,2},{3,27},{27,3},{4,28},{28... | collective-permute-start | bytes 1179656 | tf_op jit(solution)/shard_map/ppermute | solution.py:161
  53.8 16.2 %all-to-all-start.1 = ((bf16[4,6,48,256]{3,2,1,0:T(8,128)(2,1)}), bf16[4,6,48,256]{3,2,1,0:T(8,128)(2,1)S(1)}, u32[]{:S(2)}, u32[]{:S(2)}) async-start(bf16[4,6,48,256]{3,2,1,0:T(8,128)(2,1)} %broadcast_in_dim.9), calls=%async_computation.1 | async-start | bytes 1179648 | tf_op jit(solution)/shard_map/all_to_all | solution.py:152
  67.8 2.1 %copy-start = (bf16[1536,1536]{1,0:T(8,128)(2,1)}, bf16[1536,1536]{1,0:T(8,128)(2,1)S(1)}, u32[]{:S(2)}) copy-start(bf16[1536,1536]{1,0:T(8,128)(2,1)S(1)} %place.1.x_ref) | copy-start | bytes 14155780
  70.0 14.8 %all-to-all-start.4 = ((f32[4,288,256]{2,1,0:T(8,128)}), f32[4,288,256]{2,1,0:T(8,128)S(1)}, u32[]{:S(2)}, u32[]{:S(2)}) async-start(f32[4,288,256]{2,1,0:T(8,128)} %bitcast.8), calls=%async_computation.4 | async-start | bytes 2359296 | tf_op jit(solution)/shard_map/all_to_all | solution.py:167
  74.8 2.3 %copy-start.1 = (bf16[1536,1536]{1,0:T(8,128)(2,1)S(1)}, bf16[1536,1536]{1,0:T(8,128)(2,1)}, u32[]{:S(2)}) copy-start(bf16[1536,1536]{1,0:T(8,128)(2,1)} %copy-done) | copy-start | bytes 14155780
  79.6 4.2 %collective-permute-start = (f32[768,256]{1,0:T(8,128)S(1)}, f32[768,256]{1,0:T(8,128)S(1)}, u32[]{:S(2)}, u32[]{:S(2)}) collective-permute-start(f32[768,256]{1,0:T(8,128)S(1)} %get-tuple-element.8), channel_id=1, source_target_pairs={{0,24},{24,0},{1,25},{25,1},{2,26},{26,2},{3,27},{27,3},{4,28},{28... | collective-permute-start | bytes 2359304 | tf_op jit(solution)/shard_map/ppermute | solution.py:165
  84.8 27.2 %all-to-all-start.2 = ((f32[8,96,256]{2,1,0:T(8,128)}), f32[8,96,256]{2,1,0:T(8,128)S(1)}, u32[]{:S(2)}, u32[]{:S(2)}) async-start(f32[8,96,256]{2,1,0:T(8,128)} %bitcast.4), calls=%async_computation.2 | async-start | bytes 1572864 | tf_op jit(solution)/shard_map/all_to_all | solution.py:170
  88.4 50.8 %copy-start.4 = (f32[48,256]{1,0:T(8,128)S(1)}, f32[48,256]{1,0:T(8,128)}, u32[]{:S(2)}) copy-start(f32[48,256]{1,0:T(8,128)} %param.5) | copy-start | bytes 147460
  112.0 15.9 %all-to-all-start.5 = ((f32[6,48,256]{2,1,0:T(8,128)}), f32[6,48,256]{2,1,0:T(8,128)S(1)}, u32[]{:S(2)}, u32[]{:S(2)}) async-start(f32[6,48,256]{2,1,0:T(8,128)} %bitcast.9), calls=%async_computation.5 | async-start | bytes 589824 | tf_op jit(solution)/shard_map/all_to_all | solution.py:174
  117.9 21.3 %collective-permute-start.3 = (f32[48,256]{1,0:T(8,128)S(1)}, f32[48,256]{1,0:T(8,128)S(1)}, u32[]{:S(2)}, u32[]{:S(2)}) collective-permute-start(f32[48,256]{1,0:T(8,128)S(1)} %slice.11), channel_id=1, source_target_pairs={{0,384},{384,0},{1,385},{385,1},{2,386},{386,2},{3,387},{387,3},{4... | collective-permute-start | bytes 147464 | tf_op jit(solution)/shard_map/ppermute | solution.py:176

commit v2 on v1

v2 whole, which is shorter than its diff:
```python
import jax
import jax.numpy as jnp
from jax import lax
from jax.experimental import pallas as pl
from jax.experimental.pallas import tpu as pltpu
from jax.sharding import Mesh, PartitionSpec as P

AXES = ("zh", "y", "co", "zl", "x")
SIZES = (2, 8, 2, 6, 4)
ROW_AXES = ("zh", "y", "co")
COL_AXES = ("zl", "x")
TILE = 48
PAIRS = 256
NCOLS = 24
NROWS = 32
PAD = 32
HALF = NROWS * TILE // 2
WIDE = NROWS * TILE
TALL = PAD * TILE
GROUP = 8
LANES = GROUP * TILE


def place_kernel(map_ref, v_ref, x_ref, token_ref, onehot, dense):
    slots = v_ref.shape[0]
    places = NROWS * PAD

    @pl.when(pl.program_id(0) == 0)
    def _():
        token_ref[...] = jnp.zeros_like(token_ref)
        my_zh, my_y, my_co = (lax.axis_index(a) for a in ROW_AXES)
        my_zl, my_x = (lax.axis_index(a) for a in COL_AXES)
        my_row = my_zh * 16 + my_y * 2 + my_co
        first = map_ref[0:1, :]
        second = map_ref[1:2, :]
        i = first - my_row * NCOLS
        j = (second * 2731) >> 16
        run = (i >> 3) - (my_zl >> 1)
        run = jnp.where(run < 0, run + 3, run)
        i_place = ((i & 3) ^ my_x) * 6 + run * 2 + (((i >> 2) & 1) ^ (my_zl & 1))
        j_place = ((j & 1) ^ my_co) * 16 + ((j >> 1) & 7) * 2 + ((j >> 4) ^ my_zh)
        place = j_place * PAD + i_place
        weight = jnp.where(first == second, 0.5, 1.0)
        for start in range(0, places, 128):
            rows = lax.broadcasted_iota(jnp.int32, (128, slots), 0) + start
            onehot[start : start + 128, :] = jnp.where(rows == place, weight, 0.0).astype(
                jnp.bfloat16
            )

    for start in range(0, places, 256):
        dense[start : start + 256, :] = jnp.dot(
            onehot[start : start + 256, :], v_ref[...], preferred_element_type=jnp.float32
        ).astype(jnp.bfloat16)
    for s in range(GROUP):
        parts = [
            dense[j * PAD : (j + 1) * PAD, s * TILE : (s + 1) * TILE] for j in range(NROWS)
        ]
        x_ref[s * PAD : (s + 1) * PAD, :] = jnp.concatenate(parts, axis=1)


def place(tile_map, v_tiles):
    slots = v_tiles.shape[0]
    return pl.pallas_call(
        place_kernel,
        grid=(TILE // GROUP,),
        in_specs=[
            pl.BlockSpec((2, slots), lambda g: (0, 0)),
            pl.BlockSpec((slots, LANES), lambda g: (0, g)),
        ],
        out_specs=(
            pl.BlockSpec((GROUP * PAD, WIDE), lambda g: (g, 0)),
            pl.BlockSpec((8, 128), lambda g: (0, 0)),
        ),
        out_shape=(
            jax.ShapeDtypeStruct((TALL, WIDE), jnp.bfloat16),
            jax.ShapeDtypeStruct((8, 128), jnp.float32),
        ),
        scratch_shapes=[
            pltpu.VMEM((NROWS * PAD, slots), jnp.bfloat16),
            pltpu.VMEM((NROWS * PAD, LANES), jnp.bfloat16),
        ],
        compiler_params=pltpu.CompilerParams(vmem_limit_bytes=8 * 2**20),
        cost_estimate=pl.CostEstimate(
            flops=2 * 1024 * 512 * 2304, bytes_accessed=8 * 2**20, transcendentals=0
        ),
        name="place",
    )(tile_map, v_tiles)


def mirror_kernel(after, x_ref, a0, a1, a2, a3, own_ref, other_ref, left, right, rows):
    wides = (left, right)
    blocks = [a.at[pl.ds(k * TILE, TILE), :] for a in (a0, a1, a2, a3) for k in range(6)]
    for h, wide in enumerate(wides):
        lanes = slice(h * 128, h * 128 + 128)
        for i in range(NCOLS):
            wide[pl.ds(i, TILE, stride=PAD), :] = blocks[i][:, lanes].astype(jnp.float32)
        for i in range(NCOLS, PAD):
            wide[pl.ds(i, TILE, stride=PAD), :] = jnp.zeros((TILE, 128), jnp.float32)
        rows[:, lanes] = wide[...].astype(jnp.bfloat16)
    for out, base in ((other_ref, HALF), (own_ref, 0)):
        for start in range(0, HALF, 256):
            out[start : start + 256, :] = lax.dot_general(
                x_ref[:, base + start : base + start + 256],
                rows[...],
                (((0,), (0,)), ((), ())),
                preferred_element_type=jnp.float32,
            )


def mirror(after, x, *quarters):
    half = jax.ShapeDtypeStruct((HALF, PAIRS), jnp.float32)
    return pl.pallas_call(
        mirror_kernel,
        in_specs=[pl.BlockSpec(memory_space=pl.ANY)]
        + [pl.BlockSpec(memory_space=pltpu.VMEM)] * 5,
        out_shape=(half, half),
        scratch_shapes=[
            pltpu.VMEM((TALL, 128), jnp.float32),
            pltpu.VMEM((TALL, 128), jnp.float32),
            pltpu.VMEM((TALL, PAIRS), jnp.bfloat16),
        ],
        compiler_params=pltpu.CompilerParams(vmem_limit_bytes=16 * 2**20),
        cost_estimate=pl.CostEstimate(
            flops=2 * TALL * WIDE * PAIRS, bytes_accessed=8 * 2**20, transcendentals=0
        ),
        name="mirror",
    )(after, x, *quarters)


def direct_kernel(x_ref, own_ref, other_ref, o0, o1, o2, o3, left, right):
    for start in range(0, TALL, 256):
        total = jnp.dot(
            x_ref[start : start + 256, :HALF], own_ref[...], preferred_element_type=jnp.float32
        ) + jnp.dot(
            x_ref[start : start + 256, HALF:], other_ref[...], preferred_element_type=jnp.float32
        )
        left[start : start + 256, :] = total[:, :128]
        right[start : start + 256, :] = total[:, 128:]
    for i in range(NCOLS):
        out = (o0, o1, o2, o3)[i // 6]
        rows = slice(i % 6 * TILE, i % 6 * TILE + TILE)
        out[rows, :128] = left[pl.ds(i, TILE, stride=PAD), :]
        out[rows, 128:] = right[pl.ds(i, TILE, stride=PAD), :]


def direct(x, own, other):
    return pl.pallas_call(
        direct_kernel,
        out_shape=(jax.ShapeDtypeStruct((6 * TILE, PAIRS), jnp.float32),) * 4,
        scratch_shapes=[
            pltpu.VMEM((TALL, 128), jnp.float32),
            pltpu.VMEM((TALL, 128), jnp.float32),
        ],
        compiler_params=pltpu.CompilerParams(vmem_limit_bytes=16 * 2**20),
        cost_estimate=pl.CostEstimate(
            flops=2 * TALL * WIDE * PAIRS, bytes_accessed=8 * 2**20, transcendentals=0
        ),
        name="direct",
    )(x, own, other)


def stack_kernel(*refs):
    *blocks, out = refs
    start = 0
    for block in blocks:
        out[start : start + block.shape[0], :] = block[...]
        start += block.shape[0]


def stack(*blocks):
    rows = sum(b.shape[0] for b in blocks)
    return pl.pallas_call(
        stack_kernel,
        out_shape=jax.ShapeDtypeStruct((rows, PAIRS), blocks[0].dtype),
        compiler_params=pltpu.CompilerParams(vmem_limit_bytes=4 * 2**20),
        name="stack",
    )(*blocks)


def begin_kernel(after, own, far, beside, pair, both):
    pair[:TILE, :] = own[...]
    pair[TILE:, :] = beside[...]
    for n in range(8):
        both[n, :TILE, :] = own[...]
        both[n, TILE:, :] = far[...]


def begin(after, own, far, beside):
    return pl.pallas_call(
        begin_kernel,
        in_specs=[pl.BlockSpec(memory_space=pl.ANY)]
        + [pl.BlockSpec(memory_space=pltpu.VMEM)] * 3,
        out_shape=(
            jax.ShapeDtypeStruct((2 * TILE, PAIRS), own.dtype),
            jax.ShapeDtypeStruct((8, 2 * TILE, PAIRS), own.dtype),
        ),
        compiler_params=pltpu.CompilerParams(vmem_limit_bytes=4 * 2**20),
        name="begin",
    )(after, own, far, beside)


def total_kernel(count, *refs):
    parts = refs[:count]
    outs = refs[count:]
    rows = outs[0].shape[0]
    for k, out in enumerate(outs):
        terms = []
        for p in parts:
            if len(p.shape) == 3:
                terms += [p[n, k * rows : (k + 1) * rows, :] for n in range(p.shape[0])]
            else:
                terms.append(p[k * rows : (k + 1) * rows, :])
        while len(terms) > 1:
            terms = [sum(terms[n : n + 2]) for n in range(0, len(terms), 2)]
        out[...] = terms[0]


def total(splits, *parts):
    rows = parts[0].shape[-2] // splits
    return pl.pallas_call(
        lambda *refs: total_kernel(len(parts), *refs),
        out_shape=(jax.ShapeDtypeStruct((rows, PAIRS), jnp.float32),) * splits,
        compiler_params=pltpu.CompilerParams(vmem_limit_bytes=8 * 2**20),
        name="total",
    )(*parts)


SWAP = [(0, 1), (1, 0)]


def swap_x(block, k):
    return lax.ppermute(block, "x", [(i, i ^ k) for i in range(4)])


def swap_zl(block):
    return lax.ppermute(block, "zl", [(i, i ^ 1) for i in range(6)])


def turn_zl(block, k):
    return lax.ppermute(block, "zl", [(i, (i + 2 * k) % 6) for i in range(6)])


def per_device(amplitudes, residual_in, v_tiles, tile_map):
    far = lax.ppermute(amplitudes, "zh", SWAP)
    beside = swap_zl(amplitudes)
    x, placed = place(tile_map[0, 0].T, v_tiles[0, 0])

    pair, both = begin(placed, amplitudes, far, beside)
    line = stack(pair, turn_zl(pair, 2), turn_zl(pair, 1))
    quarters = [line] + [swap_x(line, k) for k in (1, 2, 3)]

    own = lax.all_to_all(both, "y", split_axis=0, concat_axis=0).reshape(HALF, PAIRS)
    other = lax.ppermute(own, "co", SWAP)

    keep, send = mirror(own, x, *quarters)
    got = lax.ppermute(send, "co", SWAP)
    row_parts = lax.all_to_all(
        total(1, keep, got)[0].reshape(8, 2 * TILE, PAIRS), "y", split_axis=0, concat_axis=0
    )

    parts = direct(x, own, other)
    run0, run1, run2 = total(3, parts[0], *(swap_x(parts[k], k) for k in (1, 2, 3)))
    col_near, col_send = total(2, run0, turn_zl(run1, 1), turn_zl(run2, 2))
    col_beside = swap_zl(col_send)

    row_near, row_send = total(2, row_parts)
    row_far = lax.ppermute(row_send, "zh", SWAP)
    return residual_in + row_near + col_near + col_beside + row_far


def solution(mesh):
    fine = Mesh(mesh.devices.reshape(SIZES), AXES)
    return jax.shard_map(
        per_device,
        mesh=fine,
        in_specs=(
            P(AXES, None),
            P(AXES, None),
            P(ROW_AXES, COL_AXES, None, None),
            P(ROW_AXES, COL_AXES, None, None),
        ),
        out_specs=P(AXES, None),
        check_vma=False,
    )
```

time: 141 us -> 146 us (1.035)
  the two profiles are of different devices: /device:TPU:132 before, /device:TPU:8 now
where the time goes in v2:
time: 146 us; the launch traced here: 145 us
  starting transfers between devices  80.5 us (55%)
  waiting for transfers between devices  42.2 us (29%)
  Pallas kernels  12.6 us (9%)
  local copies, waits for them, and re-layouts  8.99 us (6%)
    ppermute x6, starting transfers between devices, swap_x(): return lax.ppermute(block, 'x', [(i, i ^ k) for i in range(4)])  19.6 us
    ppermute x4, starting transfers between devices, turn_zl(): return lax.ppermute(block, 'zl', [(i, (i + 2 * k) % 6) for i in range(6)])  17.8 us
    ppermute x6, waiting for transfers between devices, swap_x(): return lax.ppermute(block, 'x', [(i, i ^ k) for i in range(4)])  15.4 us
    ppermute x1, starting transfers between devices, per_device(): far = lax.ppermute(amplitudes, 'zh', SWAP)  15.3 us
    ppermute x4, waiting for transfers between devices, turn_zl(): return lax.ppermute(block, 'zl', [(i, (i + 2 * k) % 6) for i in range(6)])  14 us
    unnamed x14, local copies, waits for them, and re-layouts  8.99 us
    ppermute x1, waiting for transfers between devices, per_device(): row_far = lax.ppermute(row_send, 'zh', SWAP)  8.75 us
    all_to_all x1, starting transfers between devices, per_device(): lax.all_to_all(both, 'y', split_axis=0, concat_axis=0).reshape(HALF, PAIRS)  7.55 us
  transfers between devices with their start and end apart: 18, of which 11 were waited for; matrix products, arithmetic and copies ran while one was open for 0% of the time, Pallas kernels for 6%

profile of v2, /device:TPU:8, one launch (start us, length us, event | category | flops | bytes accessed | tf_op | source)
XLA Modules:
  0.0 145.1 jit_solution(4650896642812593621)
XLA Ops:
  0.0 15.3 %collective-permute-start = (bf16[48,256]{1,0:T(8,128)(2,1)}, bf16[48,256]{1,0:T(8,128)(2,1)S(1)}, u32[]{:S(2)}, u32[]{:S(2)}) collective-permute-start(bf16[48,256]{1,0:T(8,128)(2,1)} %own.1), channel_id=1, source_target_pairs={{0,384},{384,0},{1,385},{385,1},{2,386},{386,2},{3,387},{387,3},{4... | collective-permute-start | bytes 73736 | tf_op jit(solution)/shard_map/ppermute | solution.py:244
  15.3 3.4 %collective-permute-start.1 = (bf16[48,256]{1,0:T(8,128)(2,1)}, bf16[48,256]{1,0:T(8,128)(2,1)S(1)}, u32[]{:S(2)}, u32[]{:S(2)}) collective-permute-start(bf16[48,256]{1,0:T(8,128)(2,1)} %own.1), channel_id=1, source_target_pairs={{0,4},{4,0},{8,12},{12,8},{16,20},{20,16},{1,5},{5,1},{9,13},{13,9... | collective-permute-start | bytes 73736 | tf_op jit(solution)/shard_map/ppermute | solution.py:236
  18.7 1.5 %copy-done.4 = bf16[1,1,385,2304]{3,2,1,0:T(8,128)(2,1)S(1)} copy-done((bf16[1,1,385,2304]{3,2,1,0:T(8,128)(2,1)S(1)}, bf16[1,1,385,2304]{3,2,1,0:T(8,128)(2,1)}, u32[]{:S(2)}) %copy-start.4) | copy-done | bytes 1774104
  20.1 0.7 copy-done.5
  20.8 5.9 %place.1 = (bf16[1536,1536]{1,0:T(8,128)(2,1)S(1)}, f32[8,128]{1,0:T(8,128)S(1)}) custom-call(s32[2,385]{1,0:T(2,128)S(1)} %bitcast.10, bf16[385,2304]{1,0:T(8,128)(2,1)S(1)} %bitcast.9), custom_call_target="tpu_custom_call" | custom-call | flops 2415919104 | bytes 8388608 | tf_op jit(solution)/shard_map/place/pallas_call | solution.py:63
  26.8 2.1 %copy-done = bf16[1536,1536]{1,0:T(8,128)(2,1)} copy-done((bf16[1536,1536]{1,0:T(8,128)(2,1)}, bf16[1536,1536]{1,0:T(8,128)(2,1)S(1)}, u32[]{:S(2)}) %copy-start) | copy-done | bytes 4718616
  28.9 0.0 collective-permute-done.far
  28.9 0.0 collective-permute-done.1.beside
  28.9 0.8 begin.1
  29.7 7.5 %all-to-all-start = ((bf16[8,96,256]{2,1,0:T(8,128)(2,1)}), bf16[8,96,256]{2,1,0:T(8,128)(2,1)S(1)}, u32[]{:S(2)}, u32[]{:S(2)}) async-start(bf16[8,96,256]{2,1,0:T(8,128)(2,1)} %get-tuple-element.23), calls=%async_computation | async-start | bytes 786432 | tf_op jit(solution)/shard_map/all_to_all | solution.py:252
  37.3 6.1 %collective-permute-start.2 = (bf16[96,256]{1,0:T(8,128)(2,1)S(1)}, bf16[96,256]{1,0:T(8,128)(2,1)S(1)}, u32[]{:S(2)}, u32[]{:S(2)}) collective-permute-start(bf16[96,256]{1,0:T(8,128)(2,1)S(1)} %get-tuple-element.25.refs_0_), channel_id=1, source_target_pairs={{0,16},{4,20},{8,0},{12,4},{16,8},{20,12},{1,17},{5,21},{9,1},{13,... | collective-permute-start | bytes 147464 | tf_op jit(solution)/shard_map/ppermute | solution.py:240
  43.4 1.9 %collective-permute-start.3 = (bf16[96,256]{1,0:T(8,128)(2,1)S(1)}, bf16[96,256]{1,0:T(8,128)(2,1)S(1)}, u32[]{:S(2)}, u32[]{:S(2)}) collective-permute-start(bf16[96,256]{1,0:T(8,128)(2,1)S(1)} %get-tuple-element.25.refs_0_), channel_id=1, source_target_pairs={{0,8},{4,12},{8,16},{12,20},{16,0},{20,4},{1,9},{5,13},{9,17},{13,... | collective-permute-start | bytes 147464 | tf_op jit(solution)/shard_map/ppermute | solution.py:240
  45.3 0.0 collective-permute-done.2.refs_1_
  45.3 8.0 %collective-permute-done.3.refs_2_ = bf16[96,256]{1,0:T(8,128)(2,1)S(1)} collective-permute-done((bf16[96,256]{1,0:T(8,128)(2,1)S(1)}, bf16[96,256]{1,0:T(8,128)(2,1)S(1)}, u32[]{:S(2)}, u32[]{:S(2)}) %collective-permute-start.3) | collective-permute-done | bytes 49184 | tf_op jit(solution)/shard_map/ppermute | solution.py:240
  53.3 3.4 %collective-permute-start.4 = (bf16[288,256]{1,0:T(8,128)(2,1)S(1)}, bf16[288,256]{1,0:T(8,128)(2,1)S(1)}, u32[]{:S(2)}, u32[]{:S(2)}) collective-permute-start(bf16[288,256]{1,0:T(8,128)(2,1)S(1)} %stack.1.a0), channel_id=1, source_target_pairs={{0,1},{1,0},{2,3},{3,2},{4,5},{5,4},{6,7},{7,6},{8,9},{9,8},{10,11... | collective-permute-start | bytes 442376 | tf_op jit(solution)/shard_map/ppermute | solution.py:232
  56.7 4.6 %collective-permute-start.5 = (bf16[288,256]{1,0:T(8,128)(2,1)S(1)}, bf16[288,256]{1,0:T(8,128)(2,1)S(1)}, u32[]{:S(2)}, u32[]{:S(2)}) collective-permute-start(bf16[288,256]{1,0:T(8,128)(2,1)S(1)} %stack.1.a0), channel_id=1, source_target_pairs={{0,2},{1,3},{2,0},{3,1},{4,6},{5,7},{6,4},{7,5},{8,10},{9,11},{10,... | collective-permute-start | bytes 442376 | tf_op jit(solution)/shard_map/ppermute | solution.py:232
  61.4 2.4 %collective-permute-start.6 = (bf16[288,256]{1,0:T(8,128)(2,1)S(1)}, bf16[288,256]{1,0:T(8,128)(2,1)S(1)}, u32[]{:S(2)}, u32[]{:S(2)}) collective-permute-start(bf16[288,256]{1,0:T(8,128)(2,1)S(1)} %stack.1.a0), channel_id=1, source_target_pairs={{0,3},{1,2},{2,1},{3,0},{4,7},{5,6},{6,5},{7,4},{8,11},{9,10},{10,... | collective-permute-start | bytes 442376 | tf_op jit(solution)/shard_map/ppermute | solution.py:232
  63.7 0.0 collective-permute-done.4.a1
  63.8 1.6 %collective-permute-done.5.a2 = bf16[288,256]{1,0:T(8,128)(2,1)S(1)} collective-permute-done((bf16[288,256]{1,0:T(8,128)(2,1)S(1)}, bf16[288,256]{1,0:T(8,128)(2,1)S(1)}, u32[]{:S(2)}, u32[]{:S(2)}) %collective-permute-start.5) | collective-permute-done | bytes 147488 | tf_op jit(solution)/shard_map/ppermute | solution.py:232
  65.4 4.2 %collective-permute-done.6.a3 = bf16[288,256]{1,0:T(8,128)(2,1)S(1)} collective-permute-done((bf16[288,256]{1,0:T(8,128)(2,1)S(1)}, bf16[288,256]{1,0:T(8,128)(2,1)S(1)}, u32[]{:S(2)}, u32[]{:S(2)}) %collective-permute-start.6) | collective-permute-done | bytes 147488 | tf_op jit(solution)/shard_map/ppermute | solution.py:232
  69.6 0.0 all-to-all-done
  69.6 2.3 %copy-done.1 = bf16[1536,1536]{1,0:T(8,128)(2,1)S(1)} copy-done((bf16[1536,1536]{1,0:T(8,128)(2,1)S(1)}, bf16[1536,1536]{1,0:T(8,128)(2,1)}, u32[]{:S(2)}) %copy-start.1) | copy-done | bytes 4718616
  71.9 2.5 %mirror.1 = (f32[768,256]{1,0:T(8,128)S(1)}, f32[768,256]{1,0:T(8,128)S(1)}) custom-call(bf16[768,256]{1,0:T(8,128)(2,1)S(1)} %bitcast.6, bf16[1536,1536]{1,0:T(8,128)(2,1)S(1)} %copy-done.1, bf16[288,256]{1,0:T(8,128)(2,1)S(1)} %stack.1.a0, bf16[288,256]{1,0:T(8,128)(2,1)S(1)} %collective-permute-done.4.a1, bf16[288,256]{1,0:T(8,128)(2,1)S(1)} %collective-permute-done.5.a2, ...), custom_call_target="tpu_custom_call" | custom-call | flops 1207959552 | bytes 8388608 | tf_op jit(solution)/shard_map/mirror/pallas_call | solution.py:112
  74.5 1.9 %collective-permute-start.7 = (f32[768,256]{1,0:T(8,128)S(1)}, f32[768,256]{1,0:T(8,128)S(1)}, u32[]{:S(2)}, u32[]{:S(2)}) collective-permute-start(f32[768,256]{1,0:T(8,128)S(1)} %get-tuple-element.27), channel_id=1, source_target_pairs={{0,24},{24,0},{1,25},{25,1},{2,26},{26,2},{3,27},{27,3},{4,28},{28... | collective-permute-start | bytes 2359304 | tf_op jit(solution)/shard_map/ppermute | solution.py:256
  76.4 2.3 %collective-permute-done.7.refs_1_ = f32[768,256]{1,0:T(8,128)S(1)} collective-permute-done((f32[768,256]{1,0:T(8,128)S(1)}, f32[768,256]{1,0:T(8,128)S(1)}, u32[]{:S(2)}, u32[]{:S(2)}) %collective-permute-start.7) | collective-permute-done | bytes 786464 | tf_op jit(solution)/shard_map/ppermute | solution.py:256
  78.6 1.0 total.4
  79.6 7.3 %all-to-all-start.1 = ((f32[8,96,256]{2,1,0:T(8,128)}), f32[8,96,256]{2,1,0:T(8,128)S(1)}, u32[]{:S(2)}, u32[]{:S(2)}) async-start(f32[8,96,256]{2,1,0:T(8,128)} %bitcast.4), calls=%async_computation.1 | async-start | bytes 1572864 | tf_op jit(solution)/shard_map/all_to_all | solution.py:257
  87.0 1.9 %collective-permute-start.8 = (bf16[768,256]{1,0:T(8,128)(2,1)S(1)}, bf16[768,256]{1,0:T(8,128)(2,1)S(1)}, u32[]{:S(2)}, u32[]{:S(2)}) collective-permute-start(bf16[768,256]{1,0:T(8,128)(2,1)S(1)} %bitcast.7), channel_id=1, source_target_pairs={{0,24},{24,0},{1,25},{25,1},{2,26},{26,2},{3,27},{27,3},{4,28},{28... | collective-permute-start | bytes 1179656 | tf_op jit(solution)/shard_map/ppermute | solution.py:253
  88.9 1.7 %collective-permute-done.8.other_ref = bf16[768,256]{1,0:T(8,128)(2,1)S(1)} collective-permute-done((bf16[768,256]{1,0:T(8,128)(2,1)S(1)}, bf16[768,256]{1,0:T(8,128)(2,1)S(1)}, u32[]{:S(2)}, u32[]{:S(2)}) %collective-permute-start.8) | collective-permute-done | bytes 393248 | tf_op jit(solution)/shard_map/ppermute | solution.py:253
  90.6 2.3 %copy-done.2 = bf16[1536,1536]{1,0:T(8,128)(2,1)S(1)} copy-done((bf16[1536,1536]{1,0:T(8,128)(2,1)S(1)}, bf16[1536,1536]{1,0:T(8,128)(2,1)}, u32[]{:S(2)}) %copy-start.2) | copy-done | bytes 4718616
  92.9 2.2 %direct.1 = (f32[288,256]{1,0:T(8,128)S(1)}, f32[288,256]{1,0:T(8,128)S(1)}, f32[288,256]{1,0:T(8,128)S(1)}, f32[288,256]{1,0:T(8,128)S(1)}) custom-call(bf16[1536,1536]{1,0:T(8,128)(2,1)S(1)} %copy-done.2, bf16[768,256]{1,0:T(8,128)(2,1)S(1)} %bitcast.8, bf16[768,256]{1,0:T(8,128)(2,1)S(1)} %collective-permute-done.8.other_ref), custom_call_target="tpu_custom_call" | custom-call | flops 1207959552 | bytes 8388608 | tf_op jit(solution)/shard_map/direct/pallas_call | solution.py:147
  95.1 1.9 %collective-permute-start.10 = (f32[288,256]{1,0:T(8,128)S(1)}, f32[288,256]{1,0:T(8,128)S(1)}, u32[]{:S(2)}, u32[]{:S(2)}) collective-permute-start(f32[288,256]{1,0:T(8,128)S(1)} %get-tuple-element.31), channel_id=1, source_target_pairs={{0,2},{1,3},{2,0},{3,1},{4,6},{5,7},{6,4},{7,5},{8,10},{9,11},{10,... | collective-permute-start | bytes 884744 | tf_op jit(solution)/shard_map/ppermute | solution.py:232
  97.1 3.6 %collective-permute-start.11 = (f32[288,256]{1,0:T(8,128)S(1)}, f32[288,256]{1,0:T(8,128)S(1)}, u32[]{:S(2)}, u32[]{:S(2)}) collective-permute-start(f32[288,256]{1,0:T(8,128)S(1)} %get-tuple-element.32), channel_id=1, source_target_pairs={{0,3},{1,2},{2,1},{3,0},{4,7},{5,6},{6,5},{7,4},{8,11},{9,10},{10,... | collective-permute-start | bytes 884744 | tf_op jit(solution)/shard_map/ppermute | solution.py:232
  100.6 3.7 %collective-permute-start.9 = (f32[288,256]{1,0:T(8,128)S(1)}, f32[288,256]{1,0:T(8,128)S(1)}, u32[]{:S(2)}, u32[]{:S(2)}) collective-permute-start(f32[288,256]{1,0:T(8,128)S(1)} %get-tuple-element.30), channel_id=1, source_target_pairs={{0,1},{1,0},{2,3},{3,2},{4,5},{5,4},{6,7},{7,6},{8,9},{9,8},{10,11... | collective-permute-start | bytes 884744 | tf_op jit(solution)/shard_map/ppermute | solution.py:232
  104.4 4.1 %collective-permute-done.10.refs_2_ = f32[288,256]{1,0:T(8,128)S(1)} collective-permute-done((f32[288,256]{1,0:T(8,128)S(1)}, f32[288,256]{1,0:T(8,128)S(1)}, u32[]{:S(2)}, u32[]{:S(2)}) %collective-permute-start.10) | collective-permute-done | bytes 294944 | tf_op jit(solution)/shard_map/ppermute | solution.py:232
  108.4 5.5 %collective-permute-done.11.refs_3_ = f32[288,256]{1,0:T(8,128)S(1)} collective-permute-done((f32[288,256]{1,0:T(8,128)S(1)}, f32[288,256]{1,0:T(8,128)S(1)}, u32[]{:S(2)}, u32[]{:S(2)}) %collective-permute-start.11) | collective-permute-done | bytes 294944 | tf_op jit(solution)/shard_map/ppermute | solution.py:232
  113.9 0.0 collective-permute-done.9.refs_1_
  113.9 0.1 total.6
  113.9 1.9 %collective-permute-start.12 = (f32[96,256]{1,0:T(8,128)S(1)}, f32[96,256]{1,0:T(8,128)S(1)}, u32[]{:S(2)}, u32[]{:S(2)}) collective-permute-start(f32[96,256]{1,0:T(8,128)S(1)} %get-tuple-element.34), channel_id=1, source_target_pairs={{0,8},{4,12},{8,16},{12,20},{16,0},{20,4},{1,9},{5,13},{9,17},{13,... | collective-permute-start | bytes 294920 | tf_op jit(solution)/shard_map/ppermute | solution.py:240
  115.9 7.8 %collective-permute-start.13 = (f32[96,256]{1,0:T(8,128)S(1)}, f32[96,256]{1,0:T(8,128)S(1)}, u32[]{:S(2)}, u32[]{:S(2)}) collective-permute-start(f32[96,256]{1,0:T(8,128)S(1)} %get-tuple-element.35), channel_id=1, source_target_pairs={{0,16},{4,20},{8,0},{12,4},{16,8},{20,12},{1,17},{5,21},{9,1},{13,... | collective-permute-start | bytes 294920 | tf_op jit(solution)/shard_map/ppermute | solution.py:240
  123.7 5.8 %collective-permute-done.12.refs_1_ = f32[96,256]{1,0:T(8,128)S(1)} collective-permute-done((f32[96,256]{1,0:T(8,128)S(1)}, f32[96,256]{1,0:T(8,128)S(1)}, u32[]{:S(2)}, u32[]{:S(2)}) %collective-permute-start.12) | collective-permute-done | bytes 98336 | tf_op jit(solution)/shard_map/ppermute | solution.py:240
  129.5 0.2 collective-permute-done.13.refs_2_
  129.7 1.9 %collective-permute-start.14 = (f32[48,256]{1,0:T(8,128)S(1)}, f32[48,256]{1,0:T(8,128)S(1)}, u32[]{:S(2)}, u32[]{:S(2)}) collective-permute-start(f32[48,256]{1,0:T(8,128)S(1)} %get-tuple-element.37), channel_id=1, source_target_pairs={{0,4},{4,0},{8,12},{12,8},{16,20},{20,16},{1,5},{5,1},{9,13},{13,9... | collective-permute-start | bytes 147464 | tf_op jit(solution)/shard_map/ppermute | solution.py:236
  131.7 0.0 all-to-all-done.1.refs_0_
  131.7 3.9 %collective-permute-start.15 = (f32[48,256]{1,0:T(8,128)S(1)}, f32[48,256]{1,0:T(8,128)S(1)}, u32[]{:S(2)}, u32[]{:S(2)}) collective-permute-start(f32[48,256]{1,0:T(8,128)S(1)} %get-tuple-element.38), channel_id=1, source_target_pairs={{0,384},{384,0},{1,385},{385,1},{2,386},{386,2},{3,387},{387,3},{4... | collective-permute-start | bytes 147464 | tf_op jit(solution)/shard_map/ppermute | solution.py:267
  135.6 0.1 collective-permute-done.14
  135.7 8.8 %collective-permute-done.15 = f32[48,256]{1,0:T(8,128)S(1)} collective-permute-done((f32[48,256]{1,0:T(8,128)S(1)}, f32[48,256]{1,0:T(8,128)S(1)}, u32[]{:S(2)}, u32[]{:S(2)}) %collective-permute-start.15) | collective-permute-done | bytes 49184 | tf_op jit(solution)/shard_map/ppermute | solution.py:267
  144.5 0.6 add_add_fusion
  (12 shorter events, 0.1 us)
Async XLA Ops:
  0.0 28.9 %copy-start.3 = (bf16[48,256]{1,0:T(8,128)(2,1)S(1)}, bf16[48,256]{1,0:T(8,128)(2,1)}, u32[]{:S(2)}) copy-start(bf16[48,256]{1,0:T(8,128)(2,1)} %own.1) | copy-start | bytes 73732
  0.0 28.9 %collective-permute-start = (bf16[48,256]{1,0:T(8,128)(2,1)}, bf16[48,256]{1,0:T(8,128)(2,1)S(1)}, u32[]{:S(2)}, u32[]{:S(2)}) collective-permute-start(bf16[48,256]{1,0:T(8,128)(2,1)} %own.1), channel_id=1, source_target_pairs={{0,384},{384,0},{1,385},{385,1},{2,386},{386,2},{3,387},{387,3},{4... | collective-permute-start | bytes 73736 | tf_op jit(solution)/shard_map/ppermute | solution.py:244
  15.3 13.7 %collective-permute-start.1 = (bf16[48,256]{1,0:T(8,128)(2,1)}, bf16[48,256]{1,0:T(8,128)(2,1)S(1)}, u32[]{:S(2)}, u32[]{:S(2)}) collective-permute-start(bf16[48,256]{1,0:T(8,128)(2,1)} %own.1), channel_id=1, source_target_pairs={{0,4},{4,0},{8,12},{12,8},{16,20},{20,16},{1,5},{5,1},{9,13},{13,9... | collective-permute-start | bytes 73736 | tf_op jit(solution)/shard_map/ppermute | solution.py:236
  18.7 1.5 %copy-start.4 = (bf16[1,1,385,2304]{3,2,1,0:T(8,128)(2,1)S(1)}, bf16[1,1,385,2304]{3,2,1,0:T(8,128)(2,1)}, u32[]{:S(2)}) copy-start(bf16[1,1,385,2304]{3,2,1,0:T(8,128)(2,1)} %param.6) | copy-start | bytes 5322244
  20.1 0.7 copy-start.5
  26.8 2.1 %copy-start = (bf16[1536,1536]{1,0:T(8,128)(2,1)}, bf16[1536,1536]{1,0:T(8,128)(2,1)S(1)}, u32[]{:S(2)}) copy-start(bf16[1536,1536]{1,0:T(8,128)(2,1)S(1)} %get-tuple-element.24.x_ref) | copy-start | bytes 14155780
  29.7 39.9 %all-to-all-start = ((bf16[8,96,256]{2,1,0:T(8,128)(2,1)}), bf16[8,96,256]{2,1,0:T(8,128)(2,1)S(1)}, u32[]{:S(2)}, u32[]{:S(2)}) async-start(bf16[8,96,256]{2,1,0:T(8,128)(2,1)} %get-tuple-element.23), calls=%async_computation | async-start | bytes 786432 | tf_op jit(solution)/shard_map/all_to_all | solution.py:252
  37.3 8.0 %collective-permute-start.2 = (bf16[96,256]{1,0:T(8,128)(2,1)S(1)}, bf16[96,256]{1,0:T(8,128)(2,1)S(1)}, u32[]{:S(2)}, u32[]{:S(2)}) collective-permute-start(bf16[96,256]{1,0:T(8,128)(2,1)S(1)} %get-tuple-element.25.refs_0_), channel_id=1, source_target_pairs={{0,16},{4,20},{8,0},{12,4},{16,8},{20,12},{1,17},{5,21},{9,1},{13,... | collective-permute-start | bytes 147464 | tf_op jit(solution)/shard_map/ppermute | solution.py:240
  43.4 9.9 %collective-permute-start.3 = (bf16[96,256]{1,0:T(8,128)(2,1)S(1)}, bf16[96,256]{1,0:T(8,128)(2,1)S(1)}, u32[]{:S(2)}, u32[]{:S(2)}) collective-permute-start(bf16[96,256]{1,0:T(8,128)(2,1)S(1)} %get-tuple-element.25.refs_0_), channel_id=1, source_target_pairs={{0,8},{4,12},{8,16},{12,20},{16,0},{20,4},{1,9},{5,13},{9,17},{13,... | collective-permute-start | bytes 147464 | tf_op jit(solution)/shard_map/ppermute | solution.py:240
  53.3 10.4 %collective-permute-start.4 = (bf16[288,256]{1,0:T(8,128)(2,1)S(1)}, bf16[288,256]{1,0:T(8,128)(2,1)S(1)}, u32[]{:S(2)}, u32[]{:S(2)}) collective-permute-start(bf16[288,256]{1,0:T(8,128)(2,1)S(1)} %stack.1.a0), channel_id=1, source_target_pairs={{0,1},{1,0},{2,3},{3,2},{4,5},{5,4},{6,7},{7,6},{8,9},{9,8},{10,11... | collective-permute-start | bytes 442376 | tf_op jit(solution)/shard_map/ppermute | solution.py:232
  56.7 8.6 %collective-permute-start.5 = (bf16[288,256]{1,0:T(8,128)(2,1)S(1)}, bf16[288,256]{1,0:T(8,128)(2,1)S(1)}, u32[]{:S(2)}, u32[]{:S(2)}) collective-permute-start(bf16[288,256]{1,0:T(8,128)(2,1)S(1)} %stack.1.a0), channel_id=1, source_target_pairs={{0,2},{1,3},{2,0},{3,1},{4,6},{5,7},{6,4},{7,5},{8,10},{9,11},{10,... | collective-permute-start | bytes 442376 | tf_op jit(solution)/shard_map/ppermute | solution.py:232
  61.4 8.2 %collective-permute-start.6 = (bf16[288,256]{1,0:T(8,128)(2,1)S(1)}, bf16[288,256]{1,0:T(8,128)(2,1)S(1)}, u32[]{:S(2)}, u32[]{:S(2)}) collective-permute-start(bf16[288,256]{1,0:T(8,128)(2,1)S(1)} %stack.1.a0), channel_id=1, source_target_pairs={{0,3},{1,2},{2,1},{3,0},{4,7},{5,6},{6,5},{7,4},{8,11},{9,10},{10,... | collective-permute-start | bytes 442376 | tf_op jit(solution)/shard_map/ppermute | solution.py:232
  69.6 2.3 %copy-start.1 = (bf16[1536,1536]{1,0:T(8,128)(2,1)S(1)}, bf16[1536,1536]{1,0:T(8,128)(2,1)}, u32[]{:S(2)}) copy-start(bf16[1536,1536]{1,0:T(8,128)(2,1)} %copy-done) | copy-start | bytes 14155780
  74.5 4.2 %collective-permute-start.7 = (f32[768,256]{1,0:T(8,128)S(1)}, f32[768,256]{1,0:T(8,128)S(1)}, u32[]{:S(2)}, u32[]{:S(2)}) collective-permute-start(f32[768,256]{1,0:T(8,128)S(1)} %get-tuple-element.27), channel_id=1, source_target_pairs={{0,24},{24,0},{1,25},{25,1},{2,26},{26,2},{3,27},{27,3},{4,28},{28... | collective-permute-start | bytes 2359304 | tf_op jit(solution)/shard_map/ppermute | solution.py:256
  79.6 64.9 %copy-start.6 = (f32[48,256]{1,0:T(8,128)S(1)}, f32[48,256]{1,0:T(8,128)}, u32[]{:S(2)}) copy-start(f32[48,256]{1,0:T(8,128)} %param.5) | copy-start | bytes 147460
  79.6 52.0 %all-to-all-start.1 = ((f32[8,96,256]{2,1,0:T(8,128)}), f32[8,96,256]{2,1,0:T(8,128)S(1)}, u32[]{:S(2)}, u32[]{:S(2)}) async-start(f32[8,96,256]{2,1,0:T(8,128)} %bitcast.4), calls=%async_computation.1 | async-start | bytes 1572864 | tf_op jit(solution)/shard_map/all_to_all | solution.py:257
  87.0 3.6 %collective-permute-start.8 = (bf16[768,256]{1,0:T(8,128)(2,1)S(1)}, bf16[768,256]{1,0:T(8,128)(2,1)S(1)}, u32[]{:S(2)}, u32[]{:S(2)}) collective-permute-start(bf16[768,256]{1,0:T(8,128)(2,1)S(1)} %bitcast.7), channel_id=1, source_target_pairs={{0,24},{24,0},{1,25},{25,1},{2,26},{26,2},{3,27},{27,3},{4,28},{28... | collective-permute-start | bytes 1179656 | tf_op jit(solution)/shard_map/ppermute | solution.py:253
  90.6 2.3 %copy-start.2 = (bf16[1536,1536]{1,0:T(8,128)(2,1)S(1)}, bf16[1536,1536]{1,0:T(8,128)(2,1)}, u32[]{:S(2)}) copy-start(bf16[1536,1536]{1,0:T(8,128)(2,1)} %copy-done) | copy-start | bytes 14155780
  95.1 13.3 %collective-permute-start.10 = (f32[288,256]{1,0:T(8,128)S(1)}, f32[288,256]{1,0:T(8,128)S(1)}, u32[]{:S(2)}, u32[]{:S(2)}) collective-permute-start(f32[288,256]{1,0:T(8,128)S(1)} %get-tuple-element.31), channel_id=1, source_target_pairs={{0,2},{1,3},{2,0},{3,1},{4,6},{5,7},{6,4},{7,5},{8,10},{9,11},{10,... | collective-permute-start | bytes 884744 | tf_op jit(solution)/shard_map/ppermute | solution.py:232
  97.1 16.8 %collective-permute-start.11 = (f32[288,256]{1,0:T(8,128)S(1)}, f32[288,256]{1,0:T(8,128)S(1)}, u32[]{:S(2)}, u32[]{:S(2)}) collective-permute-start(f32[288,256]{1,0:T(8,128)S(1)} %get-tuple-element.32), channel_id=1, source_target_pairs={{0,3},{1,2},{2,1},{3,0},{4,7},{5,6},{6,5},{7,4},{8,11},{9,10},{10,... | collective-permute-start | bytes 884744 | tf_op jit(solution)/shard_map/ppermute | solution.py:232
  100.6 13.2 %collective-permute-start.9 = (f32[288,256]{1,0:T(8,128)S(1)}, f32[288,256]{1,0:T(8,128)S(1)}, u32[]{:S(2)}, u32[]{:S(2)}) collective-permute-start(f32[288,256]{1,0:T(8,128)S(1)} %get-tuple-element.30), channel_id=1, source_target_pairs={{0,1},{1,0},{2,3},{3,2},{4,5},{5,4},{6,7},{7,6},{8,9},{9,8},{10,11... | collective-permute-start | bytes 884744 | tf_op jit(solution)/shard_map/ppermute | solution.py:232
  113.9 15.5 %collective-permute-start.12 = (f32[96,256]{1,0:T(8,128)S(1)}, f32[96,256]{1,0:T(8,128)S(1)}, u32[]{:S(2)}, u32[]{:S(2)}) collective-permute-start(f32[96,256]{1,0:T(8,128)S(1)} %get-tuple-element.34), channel_id=1, source_target_pairs={{0,8},{4,12},{8,16},{12,20},{16,0},{20,4},{1,9},{5,13},{9,17},{13,... | collective-permute-start | bytes 294920 | tf_op jit(solution)/shard_map/ppermute | solution.py:240
  115.9 13.8 %collective-permute-start.13 = (f32[96,256]{1,0:T(8,128)S(1)}, f32[96,256]{1,0:T(8,128)S(1)}, u32[]{:S(2)}, u32[]{:S(2)}) collective-permute-start(f32[96,256]{1,0:T(8,128)S(1)} %get-tuple-element.35), channel_id=1, source_target_pairs={{0,16},{4,20},{8,0},{12,4},{16,8},{20,12},{1,17},{5,21},{9,1},{13,... | collective-permute-start | bytes 294920 | tf_op jit(solution)/shard_map/ppermute | solution.py:240
  129.7 6.0 %collective-permute-start.14 = (f32[48,256]{1,0:T(8,128)S(1)}, f32[48,256]{1,0:T(8,128)S(1)}, u32[]{:S(2)}, u32[]{:S(2)}) collective-permute-start(f32[48,256]{1,0:T(8,128)S(1)} %get-tuple-element.37), channel_id=1, source_target_pairs={{0,4},{4,0},{8,12},{12,8},{16,20},{20,16},{1,5},{5,1},{9,13},{13,9... | collective-permute-start | bytes 147464 | tf_op jit(solution)/shard_map/ppermute | solution.py:236
  131.7 12.7 %collective-permute-start.15 = (f32[48,256]{1,0:T(8,128)S(1)}, f32[48,256]{1,0:T(8,128)S(1)}, u32[]{:S(2)}, u32[]{:S(2)}) collective-permute-start(f32[48,256]{1,0:T(8,128)S(1)} %get-tuple-element.38), channel_id=1, source_target_pairs={{0,384},{384,0},{1,385},{385,1},{2,386},{386,2},{3,387},{387,3},{4... | collective-permute-start | bytes 147464 | tf_op jit(solution)/shard_map/ppermute | solution.py:267

commit v3 on v1

v3 whole, which is shorter than its diff:
```python
import jax
import jax.numpy as jnp
from jax import lax
from jax.experimental import pallas as pl
from jax.experimental.pallas import tpu as pltpu
from jax.sharding import Mesh, PartitionSpec as P

AXES = ("zh", "y", "co", "zl", "x")
SIZES = (2, 8, 2, 6, 4)
ROW_AXES = ("zh", "y", "co")
COL_AXES = ("zl", "x")
TILE = 48
PAIRS = 256
NCOLS = 24
NROWS = 32
PAD = 32
HALF = NROWS * TILE // 2
WIDE = NROWS * TILE
TALL = PAD * TILE
GROUP = 8
GROUPS = TILE // GROUP
LANES = GROUP * TILE
CHUNK = 256
CHUNKS = WIDE // CHUNK
LINE = 6 * TILE
EXTRA = 16
HBM = pl.BlockSpec(memory_space=pltpu.HBM)
VMEM = pl.BlockSpec(memory_space=pltpu.VMEM)


def params(mib):
    return pltpu.CompilerParams(vmem_limit_bytes=mib * 2**20)


def place_kernel(map_ref, v_hbm, x_hbm, token_ref, v, x, onehot, dense, v_sem, x_sem):
    slots = v_hbm.shape[0]
    places = NROWS * PAD

    def v_copy(g):
        lanes = pl.ds(pl.multiple_of(g * LANES, LANES), LANES)
        return pltpu.make_async_copy(v_hbm.at[:, lanes], v.at[g], v_sem.at[g])

    def x_copy(g):
        rows = pl.ds(pl.multiple_of(g * CHUNK, CHUNK), CHUNK)
        return pltpu.make_async_copy(x.at[rows, :], x_hbm.at[rows, :], x_sem.at[g])

    for g in range(GROUPS):
        v_copy(g).start()
    token_ref[...] = jnp.zeros_like(token_ref)
    my_zh, my_y, my_co = (lax.axis_index(a) for a in ROW_AXES)
    my_x = lax.axis_index("x")
    my_row = my_zh * 16 + my_y * 2 + my_co
    first = map_ref[0:1, :]
    second = map_ref[1:2, :]
    i = first - my_row * NCOLS
    j = (second * 2731) >> 16
    i_place = ((i & 3) ^ my_x) * 6 + (i >> 2)
    j_place = ((j & 1) ^ my_co) * 16 + ((j >> 1) & 7) * 2 + ((j >> 4) ^ my_zh)
    place = j_place * PAD + i_place
    weight = jnp.where(first == second, 0.5, 1.0)
    for start in range(0, places, 128):
        rows = lax.broadcasted_iota(jnp.int32, (128, slots), 0) + start
        onehot[start : start + 128, :] = jnp.where(rows == place, weight, 0.0).astype(
            jnp.bfloat16
        )

    @pl.loop(0, GROUPS)
    def _(g):
        v_copy(g).wait()
        for start in range(0, places, 256):
            dense[start : start + 256, :] = jnp.dot(
                onehot[start : start + 256, :], v[g], preferred_element_type=jnp.float32
            ).astype(jnp.bfloat16)
        for s in range(GROUP):
            parts = [
                dense[j * PAD : (j + 1) * PAD, s * TILE : (s + 1) * TILE] for j in range(NROWS)
            ]
            rows = pl.ds(pl.multiple_of(g * CHUNK + s * PAD, PAD), PAD)
            x[rows, :] = jnp.concatenate(parts, axis=1)
        x_copy(g).start()

    for g in range(GROUPS):
        x_copy(g).wait()


def place(tile_map, v_tiles):
    slots = v_tiles.shape[0]
    return pl.pallas_call(
        place_kernel,
        in_specs=[VMEM, HBM],
        out_specs=(HBM, VMEM),
        out_shape=(
            jax.ShapeDtypeStruct((TALL, WIDE), jnp.bfloat16),
            jax.ShapeDtypeStruct((8, 128), jnp.float32),
        ),
        scratch_shapes=[
            pltpu.VMEM((GROUPS, slots, LANES), jnp.bfloat16),
            pltpu.VMEM((TALL, WIDE), jnp.bfloat16),
            pltpu.VMEM((NROWS * PAD, slots), jnp.bfloat16),
            pltpu.VMEM((NROWS * PAD, LANES), jnp.bfloat16),
            pltpu.SemaphoreType.DMA((GROUPS,)),
            pltpu.SemaphoreType.DMA((GROUPS,)),
        ],
        compiler_params=params(60),
        cost_estimate=pl.CostEstimate(
            flops=2 * 1024 * 512 * 2304, bytes_accessed=8 * 2**20, transcendentals=0
        ),
        name="place",
    )(tile_map, v_tiles)


def begin_kernel(after, own, far, both):
    for n in range(8):
        both[n, :TILE, :] = own[...]
        both[n, TILE:, :] = far[...]


def begin(after, own, far):
    return pl.pallas_call(
        begin_kernel,
        in_specs=[pl.BlockSpec(memory_space=pl.ANY), VMEM, VMEM],
        out_shape=jax.ShapeDtypeStruct((8, 2 * TILE, PAIRS), own.dtype),
        compiler_params=params(4),
        name="begin",
    )(after, own, far)


def mirror_kernel(after, x_hbm, a0, a1, a2, a3, own_ref, other_ref, x, left, right, rows, sem):
    def copy(c):
        return pltpu.make_async_copy(
            x_hbm.at[:, c * CHUNK : (c + 1) * CHUNK], x.at[c], sem.at[c]
        )

    order = (3, 4, 5, 0, 1, 2)
    for c in order:
        copy(c).start()
    blocks = [a.at[k] for a in (a0, a1, a2, a3) for k in range(6)]
    for h, wide in enumerate((left, right)):
        lanes = slice(h * 128, h * 128 + 128)
        for i in range(NCOLS):
            wide[pl.ds(i, TILE, stride=PAD), :] = blocks[i][:, lanes].astype(jnp.float32)
        for i in range(NCOLS, PAD):
            wide[pl.ds(i, TILE, stride=PAD), :] = jnp.zeros((TILE, 128), jnp.float32)
        rows[:, lanes] = wide[...].astype(jnp.bfloat16)
    for c in order:
        copy(c).wait()
        out = own_ref if c < 3 else other_ref
        start = c % 3 * CHUNK
        out[start : start + CHUNK, :] = lax.dot_general(
            x[c], rows[...], (((0,), (0,)), ((), ())), preferred_element_type=jnp.float32
        )


def mirror(after, x, *quarters):
    half = jax.ShapeDtypeStruct((HALF, PAIRS), jnp.float32)
    return pl.pallas_call(
        mirror_kernel,
        in_specs=[pl.BlockSpec(memory_space=pl.ANY), HBM] + [VMEM] * 4,
        out_shape=(half, half),
        scratch_shapes=[
            pltpu.VMEM((CHUNKS, TALL, CHUNK), jnp.bfloat16),
            pltpu.VMEM((TALL, 128), jnp.float32),
            pltpu.VMEM((TALL, 128), jnp.float32),
            pltpu.VMEM((TALL, PAIRS), jnp.bfloat16),
            pltpu.SemaphoreType.DMA((CHUNKS,)),
        ],
        compiler_params=params(60),
        cost_estimate=pl.CostEstimate(
            flops=2 * TALL * WIDE * PAIRS, bytes_accessed=8 * 2**20, transcendentals=0
        ),
        name="mirror",
    )(after, x, *quarters)


def code(groups, out):
    row = lax.broadcasted_iota(jnp.int32, (EXTRA, PAIRS), 0)
    extra = jnp.zeros((EXTRA, PAIRS), jnp.int32)
    for n, block in enumerate(groups):
        top = jnp.max(jnp.abs(block), axis=0, keepdims=True)
        power = jnp.ceil(jnp.log2(jnp.maximum(top, 2.0**-100)))
        scaled = jnp.floor(block * jnp.exp2(15.0 - power) + 0.5)
        whole = jnp.clip(scaled, -32767.0, 32767.0).astype(jnp.int32)
        out[n * TILE : (n + 1) * TILE, :] = whole.astype(jnp.int16)
        extra = jnp.where(row == n, power.astype(jnp.int32), extra)
    out[len(groups) * TILE :, :] = extra.astype(jnp.int16)


def decode(coded, count):
    extra = coded[count * TILE :, :].astype(jnp.int32).astype(jnp.float32)
    step = jnp.exp2(extra - 15.0)
    return [
        coded[n * TILE : (n + 1) * TILE, :].astype(jnp.int32).astype(jnp.float32)
        * step[n : n + 1, :]
        for n in range(count)
    ]


def direct_kernel(x_hbm, own_ref, other_ref, o0, o1, o2, o3, x, left, right, sem):
    def copy(c):
        rows = slice(c * CHUNK, (c + 1) * CHUNK)
        return pltpu.make_async_copy(x_hbm.at[rows, :], x.at[rows, :], sem.at[c])

    for c in range(CHUNKS):
        copy(c).start()
    for c in range(CHUNKS):
        rows = slice(c * CHUNK, (c + 1) * CHUNK)
        copy(c).wait()
        both = jnp.dot(
            x[rows, :HALF], own_ref[...], preferred_element_type=jnp.float32
        ) + jnp.dot(x[rows, HALF:], other_ref[...], preferred_element_type=jnp.float32)
        left[rows, :] = both[:, :128]
        right[rows, :] = both[:, 128:]

    def block(i):
        rows = pl.ds(i, TILE, stride=PAD)
        return jnp.concatenate([left[rows, :], right[rows, :]], axis=1)

    for q, out in ((1, o1), (2, o2), (3, o3)):
        code([block(q * 6 + n) for n in range(6)], out)
    for n in range(6):
        o0[n * TILE : (n + 1) * TILE, :] = block(n)


def direct(x, own, other):
    coded = jax.ShapeDtypeStruct((LINE + EXTRA, PAIRS), jnp.int16)
    return pl.pallas_call(
        direct_kernel,
        in_specs=[HBM, VMEM, VMEM],
        out_shape=(jax.ShapeDtypeStruct((LINE, PAIRS), jnp.float32),) + (coded,) * 3,
        scratch_shapes=[
            pltpu.VMEM((TALL, WIDE), jnp.bfloat16),
            pltpu.VMEM((TALL, 128), jnp.float32),
            pltpu.VMEM((TALL, 128), jnp.float32),
            pltpu.SemaphoreType.DMA((CHUNKS,)),
        ],
        compiler_params=params(60),
        cost_estimate=pl.CostEstimate(
            flops=2 * TALL * WIDE * PAIRS, bytes_accessed=8 * 2**20, transcendentals=0
        ),
        name="direct",
    )(x, own, other)


def code_y_kernel(keep, got, out):
    @pl.loop(0, 8)
    def _(n):
        rows = pl.multiple_of(n * 2 * TILE, 2 * TILE)
        groups = [
            keep[pl.ds(rows + k * TILE, TILE), :] + got[pl.ds(rows + k * TILE, TILE), :]
            for k in range(2)
        ]
        code(groups, out.at[n])


def code_y(keep, got):
    return pl.pallas_call(
        code_y_kernel,
        out_shape=jax.ShapeDtypeStruct((8, 2 * TILE + EXTRA, PAIRS), jnp.int16),
        compiler_params=params(6),
        name="code_y",
    )(keep, got)


def sum_y_kernel(coded, near, send):
    totals = decode(coded.at[0], 2)
    for n in range(1, 8):
        totals = [a + b for a, b in zip(totals, decode(coded.at[n], 2))]
    near[...], send[...] = totals


def sum_y(coded):
    return pl.pallas_call(
        sum_y_kernel,
        out_shape=(jax.ShapeDtypeStruct((TILE, PAIRS), jnp.float32),) * 2,
        compiler_params=params(4),
        name="sum_y",
    )(coded)


def sum_x_kernel(keep, c1, c2, c3, out):
    parts = [decode(c, 6) for c in (c1, c2, c3)]
    for n in range(6):
        out[n] = (keep[n * TILE : (n + 1) * TILE, :] + parts[0][n]) + (parts[1][n] + parts[2][n])


def sum_x(keep, *coded):
    return pl.pallas_call(
        sum_x_kernel,
        out_shape=jax.ShapeDtypeStruct((6, TILE, PAIRS), jnp.float32),
        compiler_params=params(4),
        name="sum_x",
    )(keep, *coded)


def end_kernel(residual, near, far, line, out):
    a = (line[0] + line[1]) + (line[2] + line[3])
    out[...] = (residual[...] + (near[...] + far[...])) + (a + (line[4] + line[5]))


def end(residual, near, far, line):
    return pl.pallas_call(
        end_kernel,
        out_shape=jax.ShapeDtypeStruct((TILE, PAIRS), jnp.float32),
        compiler_params=params(4),
        name="end",
    )(residual, near, far, line)


SWAP = [(0, 1), (1, 0)]


def swap_x(block, k):
    return lax.ppermute(block, "x", [(i, i ^ k) for i in range(4)])


def trade(block, axis):
    return lax.all_to_all(block, axis, split_axis=0, concat_axis=0)


def per_device(amplitudes, residual_in, v_tiles, tile_map):
    far = lax.ppermute(amplitudes, "zh", SWAP)
    line = trade(jnp.broadcast_to(amplitudes[None], (6, TILE, PAIRS)), "zl")
    x, placed = place(tile_map[0, 0].T, v_tiles[0, 0])
    own = trade(begin(placed, amplitudes, far), "y").reshape(HALF, PAIRS)
    other = lax.ppermute(own, "co", SWAP)

    keep, send = mirror(own, x, line, *(swap_x(line, k) for k in (1, 2, 3)))
    got = lax.ppermute(send, "co", SWAP)
    row_parts = trade(code_y(keep, got), "y")

    parts = direct(x, own, other)
    col_line = sum_x(parts[0], *(swap_x(parts[k], k) for k in (1, 2, 3)))
    col_line = trade(col_line, "zl")

    row_near, row_send = sum_y(row_parts)
    row_far = lax.ppermute(row_send, "zh", SWAP)
    return end(residual_in, row_near, row_far, col_line)


def solution(mesh):
    fine = Mesh(mesh.devices.reshape(SIZES), AXES)
    return jax.shard_map(
        per_device,
        mesh=fine,
        in_specs=(
            P(AXES, None),
            P(AXES, None),
            P(ROW_AXES, COL_AXES, None, None),
            P(ROW_AXES, COL_AXES, None, None),
        ),
        out_specs=P(AXES, None),
        check_vma=False,
    )
```

time: 141 us -> 135 us (0.957)
  the two profiles are of different devices: /device:TPU:132 before, /device:TPU:10 now
where the time goes in v3:
time: 135 us; the launch traced here: 134 us
  starting transfers between devices  71.1 us (53%)
  waiting for transfers between devices  30.2 us (22%)
  Pallas kernels  26.9 us (20%)
  local copies, waits for them, and re-layouts  5.81 us (4%)
    all_to_all x4, starting transfers between devices, trade(): return lax.all_to_all(block, axis, split_axis=0, concat_axis=0)  34.5 us
    ppermute x6, starting transfers between devices, swap_x(): return lax.ppermute(block, 'x', [(i, i ^ k) for i in range(4)])  18.9 us
    all_to_all x4, waiting for transfers between devices, trade(): return lax.all_to_all(block, axis, split_axis=0, concat_axis=0)  13.4 us
    ppermute x6, waiting for transfers between devices, swap_x(): return lax.ppermute(block, 'x', [(i, i ^ k) for i in range(4)])  12.4 us
    ppermute x1, starting transfers between devices, per_device(): far = lax.ppermute(amplitudes, 'zh', SWAP)  10 us
    pallas_call x1, Pallas kernels, place(): pl.pallas_call(place_kernel, in_specs=[VMEM, HBM], out_specs=(HBM, VMEM),...  8.98 us
    pallas_call x1, Pallas kernels, mirror(): pl.pallas_call(mirror_kernel, in_specs=[pl.BlockSpec(memory_space=pl.ANY)...  7.19 us
    pallas_call x1, Pallas kernels, direct(): pl.pallas_call(direct_kernel, in_specs=[HBM, VMEM, VMEM], out_shape=(jax....  7.12 us
  transfers between devices with their start and end apart: 14, of which 7 were waited for; matrix products, arithmetic and copies ran while one was open for 0% of the time, Pallas kernels for 13%

profile of v3, /device:TPU:10, one launch (start us, length us, event | category | flops | bytes accessed | tf_op | source)
XLA Modules:
  0.0 134.2 jit_solution(381265940259355358)
XLA Ops:
  0.0 1.5 %broadcast_in_dim.2 = bf16[6,48,256]{2,1,0:T(8,128)(2,1)} broadcast(bf16[48,256]{1,0:T(8,128)(2,1)} %own.1), dimensions={1,2} | broadcast | bytes 172032 | tf_op jit(solution)/shard_map/broadcast_in_dim | solution.py:322
  1.5 12.1 %all-to-all-start.1 = ((bf16[6,48,256]{2,1,0:T(8,128)(2,1)}), bf16[6,48,256]{2,1,0:T(8,128)(2,1)S(1)}, u32[]{:S(2)}, u32[]{:S(2)}) async-start(bf16[6,48,256]{2,1,0:T(8,128)(2,1)} %broadcast_in_dim.2), calls=%async_computation.1 | async-start | bytes 294912 | tf_op jit(solution)/shard_map/all_to_all | solution.py:317
  13.6 10.0 %collective-permute-start = (bf16[48,256]{1,0:T(8,128)(2,1)}, bf16[48,256]{1,0:T(8,128)(2,1)S(1)}, u32[]{:S(2)}, u32[]{:S(2)}) collective-permute-start(bf16[48,256]{1,0:T(8,128)(2,1)} %own.1), channel_id=1, source_target_pairs={{0,384},{384,0},{1,385},{385,1},{2,386},{386,2},{3,387},{387,3},{4... | collective-permute-start | bytes 73736 | tf_op jit(solution)/shard_map/ppermute | solution.py:321
  23.6 9.0 %place.1 = (bf16[1536,1536]{1,0:T(8,128)(2,1)}, f32[8,128]{1,0:T(8,128)}) custom-call(s32[2,385]{1,0:T(2,128)} %bitcast.9, bf16[385,2304]{1,0:T(8,128)(2,1)} %bitcast.8), custom_call_target="tpu_custom_call" | custom-call | flops 2415919104 | bytes 8388608 | tf_op jit(solution)/shard_map/place/pallas_call | solution.py:88
  32.6 0.0 collective-permute-done.far
  32.6 0.0 copy-done.2
  32.6 0.0 copy-start.4
  32.6 0.7 copy-done.4
  33.3 0.8 begin.1
  34.1 0.0 all-to-all-done.1.a0
  34.1 7.5 %all-to-all-start = ((bf16[8,96,256]{2,1,0:T(8,128)(2,1)}), bf16[8,96,256]{2,1,0:T(8,128)(2,1)S(1)}, u32[]{:S(2)}, u32[]{:S(2)}) async-start(bf16[8,96,256]{2,1,0:T(8,128)(2,1)} %begin.1), calls=%async_computation | async-start | bytes 786432 | tf_op jit(solution)/shard_map/all_to_all | solution.py:317
  41.6 2.4 %collective-permute-start.1 = (bf16[6,48,256]{2,1,0:T(8,128)(2,1)S(1)}, bf16[6,48,256]{2,1,0:T(8,128)(2,1)S(1)}, u32[]{:S(2)}, u32[]{:S(2)}) collective-permute-start(bf16[6,48,256]{2,1,0:T(8,128)(2,1)S(1)} %all-to-all-done.1.a0), channel_id=1, source_target_pairs={{0,1},{1,0},{2,3},{3,2},{4,5},{5,4},{6,7},{7,6},{8,9},{9,8},{10,11... | collective-permute-start | bytes 442376 | tf_op jit(solution)/shard_map/ppermute | solution.py:313
  44.1 4.3 %collective-permute-start.2 = (bf16[6,48,256]{2,1,0:T(8,128)(2,1)S(1)}, bf16[6,48,256]{2,1,0:T(8,128)(2,1)S(1)}, u32[]{:S(2)}, u32[]{:S(2)}) collective-permute-start(bf16[6,48,256]{2,1,0:T(8,128)(2,1)S(1)} %all-to-all-done.1.a0), channel_id=1, source_target_pairs={{0,2},{1,3},{2,0},{3,1},{4,6},{5,7},{6,4},{7,5},{8,10},{9,11},{10,... | collective-permute-start | bytes 442376 | tf_op jit(solution)/shard_map/ppermute | solution.py:313
  48.4 2.4 %collective-permute-start.3 = (bf16[6,48,256]{2,1,0:T(8,128)(2,1)S(1)}, bf16[6,48,256]{2,1,0:T(8,128)(2,1)S(1)}, u32[]{:S(2)}, u32[]{:S(2)}) collective-permute-start(bf16[6,48,256]{2,1,0:T(8,128)(2,1)S(1)} %all-to-all-done.1.a0), channel_id=1, source_target_pairs={{0,3},{1,2},{2,1},{3,0},{4,7},{5,6},{6,5},{7,4},{8,11},{9,10},{10,... | collective-permute-start | bytes 442376 | tf_op jit(solution)/shard_map/ppermute | solution.py:313
  50.9 0.0 collective-permute-done.1.a1
  50.9 0.0 copy-start.8
  50.9 2.0 %collective-permute-done.2.a2 = bf16[6,48,256]{2,1,0:T(8,128)(2,1)S(1)} collective-permute-done((bf16[6,48,256]{2,1,0:T(8,128)(2,1)S(1)}, bf16[6,48,256]{2,1,0:T(8,128)(2,1)S(1)}, u32[]{:S(2)}, u32[]{:S(2)}) %collective-permute-start.2) | collective-permute-done | bytes 147488 | tf_op jit(solution)/shard_map/ppermute | solution.py:313
  52.9 3.1 %collective-permute-done.3.a3 = bf16[6,48,256]{2,1,0:T(8,128)(2,1)S(1)} collective-permute-done((bf16[6,48,256]{2,1,0:T(8,128)(2,1)S(1)}, bf16[6,48,256]{2,1,0:T(8,128)(2,1)S(1)}, u32[]{:S(2)}, u32[]{:S(2)}) %collective-permute-start.3) | collective-permute-done | bytes 147488 | tf_op jit(solution)/shard_map/ppermute | solution.py:313
  55.9 0.0 all-to-all-done
  55.9 0.0 copy-done.6
  55.9 0.0 copy-done.8
  56.0 0.6 copy-done.10
  56.6 0.2 copy-done.5
  56.7 7.2 %mirror.1 = (f32[768,256]{1,0:T(8,128)}, f32[768,256]{1,0:T(8,128)}) custom-call(bf16[768,256]{1,0:T(8,128)(2,1)} %bitcast.5, bf16[1536,1536]{1,0:T(8,128)(2,1)} %get-tuple-element.16.x_hbm, bf16[6,48,256]{2,1,0:T(8,128)(2,1)} %copy-done.6, bf16[6,48,256]{2,1,0:T(8,128)(2,1)} %copy-done.8, bf16[6,48,256]{2,1,0:T(8,128)(2,1)} %copy-done.9, ...), custom_call_target="tpu_custom_call" | custom-call | flops 1207959552 | bytes 8388608 | tf_op jit(solution)/shard_map/mirror/pallas_call | solution.py:156
  63.9 1.9 %collective-permute-start.4 = (f32[768,256]{1,0:T(8,128)}, f32[768,256]{1,0:T(8,128)S(1)}, u32[]{:S(2)}, u32[]{:S(2)}) collective-permute-start(f32[768,256]{1,0:T(8,128)} %get-tuple-element.18), channel_id=1, source_target_pairs={{0,24},{24,0},{1,25},{25,1},{2,26},{26,2},{3,27},{27,3},{4,28},{28... | collective-permute-start | bytes 2359304 | tf_op jit(solution)/shard_map/ppermute | solution.py:328
  65.9 2.5 %collective-permute-done.4.got = f32[768,256]{1,0:T(8,128)S(1)} collective-permute-done((f32[768,256]{1,0:T(8,128)}, f32[768,256]{1,0:T(8,128)S(1)}, u32[]{:S(2)}, u32[]{:S(2)}) %collective-permute-start.4) | collective-permute-done | bytes 786464 | tf_op jit(solution)/shard_map/ppermute | solution.py:328
  68.3 1.1 copy-done
  69.5 1.2 code_y.1
  70.7 7.3 %all-to-all-start.2 = ((s16[8,112,256]{2,1,0:T(8,128)(2,1)}), s16[8,112,256]{2,1,0:T(8,128)(2,1)S(1)}, u32[]{:S(2)}, u32[]{:S(2)}) async-start(s16[8,112,256]{2,1,0:T(8,128)(2,1)} %code_y.1), calls=%async_computation.2 | async-start | bytes 917504 | tf_op jit(solution)/shard_map/all_to_all | solution.py:317
  78.0 1.9 %collective-permute-start.6 = (bf16[768,256]{1,0:T(8,128)(2,1)}, bf16[768,256]{1,0:T(8,128)(2,1)S(1)}, u32[]{:S(2)}, u32[]{:S(2)}) collective-permute-start(bf16[768,256]{1,0:T(8,128)(2,1)} %bitcast.6), channel_id=1, source_target_pairs={{0,24},{24,0},{1,25},{25,1},{2,26},{26,2},{3,27},{27,3},{4,28},{28... | collective-permute-start | bytes 1179656 | tf_op jit(solution)/shard_map/ppermute | solution.py:325
  79.9 1.9 %collective-permute-done.6.other_ref = bf16[768,256]{1,0:T(8,128)(2,1)S(1)} collective-permute-done((bf16[768,256]{1,0:T(8,128)(2,1)}, bf16[768,256]{1,0:T(8,128)(2,1)S(1)}, u32[]{:S(2)}, u32[]{:S(2)}) %collective-permute-start.6) | collective-permute-done | bytes 393248 | tf_op jit(solution)/shard_map/ppermute | solution.py:325
  81.8 0.8 copy-done.7
  82.6 7.1 %direct.1 = (f32[288,256]{1,0:T(8,128)}, s16[304,256]{1,0:T(8,128)(2,1)}, s16[304,256]{1,0:T(8,128)(2,1)}, s16[304,256]{1,0:T(8,128)(2,1)}) custom-call(bf16[1536,1536]{1,0:T(8,128)(2,1)} %get-tuple-element.16.x_hbm, bf16[768,256]{1,0:T(8,128)(2,1)} %bitcast.7, bf16[768,256]{1,0:T(8,128)(2,1)} %copy-done.7), custom_call_target="tpu_custom_call" | custom-call | flops 1207959552 | bytes 8388608 | tf_op jit(solution)/shard_map/direct/pallas_call | solution.py:226
  89.7 4.5 %collective-permute-start.7 = (s16[304,256]{1,0:T(8,128)(2,1)}, s16[304,256]{1,0:T(8,128)(2,1)S(1)}, u32[]{:S(2)}, u32[]{:S(2)}) collective-permute-start(s16[304,256]{1,0:T(8,128)(2,1)} %get-tuple-element.22), channel_id=1, source_target_pairs={{0,1},{1,0},{2,3},{3,2},{4,5},{5,4},{6,7},{7,6},{8,9},{9,8},{10,11... | collective-permute-start | bytes 466952 | tf_op jit(solution)/shard_map/ppermute | solution.py:313
  94.2 1.9 %collective-permute-start.8 = (s16[304,256]{1,0:T(8,128)(2,1)}, s16[304,256]{1,0:T(8,128)(2,1)S(1)}, u32[]{:S(2)}, u32[]{:S(2)}) collective-permute-start(s16[304,256]{1,0:T(8,128)(2,1)} %get-tuple-element.23), channel_id=1, source_target_pairs={{0,2},{1,3},{2,0},{3,1},{4,6},{5,7},{6,4},{7,5},{8,10},{9,11},{10,... | collective-permute-start | bytes 466952 | tf_op jit(solution)/shard_map/ppermute | solution.py:313
  96.1 3.4 %collective-permute-start.9 = (s16[304,256]{1,0:T(8,128)(2,1)}, s16[304,256]{1,0:T(8,128)(2,1)S(1)}, u32[]{:S(2)}, u32[]{:S(2)}) collective-permute-start(s16[304,256]{1,0:T(8,128)(2,1)} %get-tuple-element.24), channel_id=1, source_target_pairs={{0,3},{1,2},{2,1},{3,0},{4,7},{5,6},{6,5},{7,4},{8,11},{9,10},{10,... | collective-permute-start | bytes 466952 | tf_op jit(solution)/shard_map/ppermute | solution.py:313
  99.5 0.0 collective-permute-done.7.c1
  99.5 4.2 %collective-permute-done.8.c2 = s16[304,256]{1,0:T(8,128)(2,1)S(1)} collective-permute-done((s16[304,256]{1,0:T(8,128)(2,1)}, s16[304,256]{1,0:T(8,128)(2,1)S(1)}, u32[]{:S(2)}, u32[]{:S(2)}) %collective-permute-start.8) | collective-permute-done | bytes 155680 | tf_op jit(solution)/shard_map/ppermute | solution.py:313
  103.7 3.2 %collective-permute-done.9.c3 = s16[304,256]{1,0:T(8,128)(2,1)S(1)} collective-permute-done((s16[304,256]{1,0:T(8,128)(2,1)}, s16[304,256]{1,0:T(8,128)(2,1)S(1)}, u32[]{:S(2)}, u32[]{:S(2)}) %collective-permute-start.9) | collective-permute-done | bytes 155680 | tf_op jit(solution)/shard_map/ppermute | solution.py:313
  106.9 1.0 copy-done.1
  107.9 0.8 sum_x.1
  108.7 0.0 all-to-all-done.2.coded
  108.7 7.5 %all-to-all-start.3 = ((f32[6,48,256]{2,1,0:T(8,128)}), f32[6,48,256]{2,1,0:T(8,128)S(1)}, u32[]{:S(2)}, u32[]{:S(2)}) async-start(f32[6,48,256]{2,1,0:T(8,128)} %sum_x.1), calls=%async_computation.3 | async-start | bytes 589824 | tf_op jit(solution)/shard_map/all_to_all | solution.py:317
  116.2 0.1 sum_y.1
  116.3 3.8 %collective-permute-start.5 = (f32[48,256]{1,0:T(8,128)S(1)}, f32[48,256]{1,0:T(8,128)S(1)}, u32[]{:S(2)}, u32[]{:S(2)}) collective-permute-start(f32[48,256]{1,0:T(8,128)S(1)} %get-tuple-element.20), channel_id=1, source_target_pairs={{0,384},{384,0},{1,385},{385,1},{2,386},{386,2},{3,387},{387,3},{4... | collective-permute-start | bytes 147464 | tf_op jit(solution)/shard_map/ppermute | solution.py:336
  120.2 13.4 %all-to-all-done.3.line = f32[6,48,256]{2,1,0:T(8,128)S(1)} async-done(((f32[6,48,256]{2,1,0:T(8,128)}), f32[6,48,256]{2,1,0:T(8,128)S(1)}, u32[]{:S(2)}, u32[]{:S(2)}) %all-to-all-start.3) | async-done | bytes 294944 | tf_op jit(solution)/shard_map/all_to_all | solution.py:317
  133.6 0.0 collective-permute-done.5.far
  133.6 0.6 end.1
  (11 shorter events, 0.0 us)
Async XLA Ops:
  0.0 32.6 %copy-start.2 = (bf16[48,256]{1,0:T(8,128)(2,1)S(1)}, bf16[48,256]{1,0:T(8,128)(2,1)}, u32[]{:S(2)}) copy-start(bf16[48,256]{1,0:T(8,128)(2,1)} %own.1) | copy-start | bytes 73732
  1.5 32.6 %all-to-all-start.1 = ((bf16[6,48,256]{2,1,0:T(8,128)(2,1)}), bf16[6,48,256]{2,1,0:T(8,128)(2,1)S(1)}, u32[]{:S(2)}, u32[]{:S(2)}) async-start(bf16[6,48,256]{2,1,0:T(8,128)(2,1)} %broadcast_in_dim.2), calls=%async_computation.1 | async-start | bytes 294912 | tf_op jit(solution)/shard_map/all_to_all | solution.py:317
  13.6 19.0 %collective-permute-start = (bf16[48,256]{1,0:T(8,128)(2,1)}, bf16[48,256]{1,0:T(8,128)(2,1)S(1)}, u32[]{:S(2)}, u32[]{:S(2)}) collective-permute-start(bf16[48,256]{1,0:T(8,128)(2,1)} %own.1), channel_id=1, source_target_pairs={{0,384},{384,0},{1,385},{385,1},{2,386},{386,2},{3,387},{387,3},{4... | collective-permute-start | bytes 73736 | tf_op jit(solution)/shard_map/ppermute | solution.py:321
  32.6 0.7 copy-start.4
  34.1 21.8 %copy-start.6 = (bf16[6,48,256]{2,1,0:T(8,128)(2,1)}, bf16[6,48,256]{2,1,0:T(8,128)(2,1)S(1)}, u32[]{:S(2)}) copy-start(bf16[6,48,256]{2,1,0:T(8,128)(2,1)S(1)} %all-to-all-done.1.a0) | copy-start | bytes 442372
  34.1 21.8 %all-to-all-start = ((bf16[8,96,256]{2,1,0:T(8,128)(2,1)}), bf16[8,96,256]{2,1,0:T(8,128)(2,1)S(1)}, u32[]{:S(2)}, u32[]{:S(2)}) async-start(bf16[8,96,256]{2,1,0:T(8,128)(2,1)} %begin.1), calls=%async_computation | async-start | bytes 786432 | tf_op jit(solution)/shard_map/all_to_all | solution.py:317
  41.6 9.2 %collective-permute-start.1 = (bf16[6,48,256]{2,1,0:T(8,128)(2,1)S(1)}, bf16[6,48,256]{2,1,0:T(8,128)(2,1)S(1)}, u32[]{:S(2)}, u32[]{:S(2)}) collective-permute-start(bf16[6,48,256]{2,1,0:T(8,128)(2,1)S(1)} %all-to-all-done.1.a0), channel_id=1, source_target_pairs={{0,1},{1,0},{2,3},{3,2},{4,5},{5,4},{6,7},{7,6},{8,9},{9,8},{10,11... | collective-permute-start | bytes 442376 | tf_op jit(solution)/shard_map/ppermute | solution.py:313
  44.1 8.8 %collective-permute-start.2 = (bf16[6,48,256]{2,1,0:T(8,128)(2,1)S(1)}, bf16[6,48,256]{2,1,0:T(8,128)(2,1)S(1)}, u32[]{:S(2)}, u32[]{:S(2)}) collective-permute-start(bf16[6,48,256]{2,1,0:T(8,128)(2,1)S(1)} %all-to-all-done.1.a0), channel_id=1, source_target_pairs={{0,2},{1,3},{2,0},{3,1},{4,6},{5,7},{6,4},{7,5},{8,10},{9,11},{10,... | collective-permute-start | bytes 442376 | tf_op jit(solution)/shard_map/ppermute | solution.py:313
  48.4 7.5 %collective-permute-start.3 = (bf16[6,48,256]{2,1,0:T(8,128)(2,1)S(1)}, bf16[6,48,256]{2,1,0:T(8,128)(2,1)S(1)}, u32[]{:S(2)}, u32[]{:S(2)}) collective-permute-start(bf16[6,48,256]{2,1,0:T(8,128)(2,1)S(1)} %all-to-all-done.1.a0), channel_id=1, source_target_pairs={{0,3},{1,2},{2,1},{3,0},{4,7},{5,6},{6,5},{7,4},{8,11},{9,10},{10,... | collective-permute-start | bytes 442376 | tf_op jit(solution)/shard_map/ppermute | solution.py:313
  50.9 5.1 %copy-start.8 = (bf16[6,48,256]{2,1,0:T(8,128)(2,1)}, bf16[6,48,256]{2,1,0:T(8,128)(2,1)S(1)}, u32[]{:S(2)}) copy-start(bf16[6,48,256]{2,1,0:T(8,128)(2,1)S(1)} %collective-permute-done.1.a1) | copy-start | bytes 442372
  52.9 3.1 %copy-start.9 = (bf16[6,48,256]{2,1,0:T(8,128)(2,1)}, bf16[6,48,256]{2,1,0:T(8,128)(2,1)S(1)}, u32[]{:S(2)}) copy-start(bf16[6,48,256]{2,1,0:T(8,128)(2,1)S(1)} %collective-permute-done.2.a2) | copy-start | bytes 442372
  55.9 0.7 copy-start.10
  55.9 0.8 copy-start.5
  63.9 4.4 %collective-permute-start.4 = (f32[768,256]{1,0:T(8,128)}, f32[768,256]{1,0:T(8,128)S(1)}, u32[]{:S(2)}, u32[]{:S(2)}) collective-permute-start(f32[768,256]{1,0:T(8,128)} %get-tuple-element.18), channel_id=1, source_target_pairs={{0,24},{24,0},{1,25},{25,1},{2,26},{26,2},{3,27},{27,3},{4,28},{28... | collective-permute-start | bytes 2359304 | tf_op jit(solution)/shard_map/ppermute | solution.py:328
  68.3 1.1 copy-start
  70.7 62.9 %copy-start.3 = (f32[48,256]{1,0:T(8,128)S(1)}, f32[48,256]{1,0:T(8,128)}, u32[]{:S(2)}) copy-start(f32[48,256]{1,0:T(8,128)} %residual.1) | copy-start | bytes 147460
  70.7 38.0 %all-to-all-start.2 = ((s16[8,112,256]{2,1,0:T(8,128)(2,1)}), s16[8,112,256]{2,1,0:T(8,128)(2,1)S(1)}, u32[]{:S(2)}, u32[]{:S(2)}) async-start(s16[8,112,256]{2,1,0:T(8,128)(2,1)} %code_y.1), calls=%async_computation.2 | async-start | bytes 917504 | tf_op jit(solution)/shard_map/all_to_all | solution.py:317
  78.0 3.8 %collective-permute-start.6 = (bf16[768,256]{1,0:T(8,128)(2,1)}, bf16[768,256]{1,0:T(8,128)(2,1)S(1)}, u32[]{:S(2)}, u32[]{:S(2)}) collective-permute-start(bf16[768,256]{1,0:T(8,128)(2,1)} %bitcast.6), channel_id=1, source_target_pairs={{0,24},{24,0},{1,25},{25,1},{2,26},{26,2},{3,27},{27,3},{4,28},{28... | collective-permute-start | bytes 1179656 | tf_op jit(solution)/shard_map/ppermute | solution.py:325
  81.8 0.8 copy-start.7
  89.7 9.8 %collective-permute-start.7 = (s16[304,256]{1,0:T(8,128)(2,1)}, s16[304,256]{1,0:T(8,128)(2,1)S(1)}, u32[]{:S(2)}, u32[]{:S(2)}) collective-permute-start(s16[304,256]{1,0:T(8,128)(2,1)} %get-tuple-element.22), channel_id=1, source_target_pairs={{0,1},{1,0},{2,3},{3,2},{4,5},{5,4},{6,7},{7,6},{8,9},{9,8},{10,11... | collective-permute-start | bytes 466952 | tf_op jit(solution)/shard_map/ppermute | solution.py:313
  94.2 9.5 %collective-permute-start.8 = (s16[304,256]{1,0:T(8,128)(2,1)}, s16[304,256]{1,0:T(8,128)(2,1)S(1)}, u32[]{:S(2)}, u32[]{:S(2)}) collective-permute-start(s16[304,256]{1,0:T(8,128)(2,1)} %get-tuple-element.23), channel_id=1, source_target_pairs={{0,2},{1,3},{2,0},{3,1},{4,6},{5,7},{6,4},{7,5},{8,10},{9,11},{10,... | collective-permute-start | bytes 466952 | tf_op jit(solution)/shard_map/ppermute | solution.py:313
  96.1 10.8 %collective-permute-start.9 = (s16[304,256]{1,0:T(8,128)(2,1)}, s16[304,256]{1,0:T(8,128)(2,1)S(1)}, u32[]{:S(2)}, u32[]{:S(2)}) collective-permute-start(s16[304,256]{1,0:T(8,128)(2,1)} %get-tuple-element.24), channel_id=1, source_target_pairs={{0,3},{1,2},{2,1},{3,0},{4,7},{5,6},{6,5},{7,4},{8,11},{9,10},{10,... | collective-permute-start | bytes 466952 | tf_op jit(solution)/shard_map/ppermute | solution.py:313
  106.9 1.0 copy-start.1
  108.7 24.9 %all-to-all-start.3 = ((f32[6,48,256]{2,1,0:T(8,128)}), f32[6,48,256]{2,1,0:T(8,128)S(1)}, u32[]{:S(2)}, u32[]{:S(2)}) async-start(f32[6,48,256]{2,1,0:T(8,128)} %sum_x.1), calls=%async_computation.3 | async-start | bytes 589824 | tf_op jit(solution)/shard_map/all_to_all | solution.py:317
  116.3 17.3 %collective-permute-start.5 = (f32[48,256]{1,0:T(8,128)S(1)}, f32[48,256]{1,0:T(8,128)S(1)}, u32[]{:S(2)}, u32[]{:S(2)}) collective-permute-start(f32[48,256]{1,0:T(8,128)S(1)} %get-tuple-element.20), channel_id=1, source_target_pairs={{0,384},{384,0},{1,385},{385,1},{2,386},{386,2},{3,387},{387,3},{4... | collective-permute-start | bytes 147464 | tf_op jit(solution)/shard_map/ppermute | solution.py:336

commit v4 on v3

--- a/solution.py
+++ b/solution.py
@@ -1,3 +1,5 @@
+import functools
+
 import jax
 import jax.numpy as jnp
 from jax import lax
@@ -109,67 +111,62 @@
     )(tile_map, v_tiles)
 
 
-def begin_kernel(after, own, far, both):
-    for n in range(8):
-        both[n, :TILE, :] = own[...]
-        both[n, TILE:, :] = far[...]
-
-
-def begin(after, own, far):
-    return pl.pallas_call(
-        begin_kernel,
-        in_specs=[pl.BlockSpec(memory_space=pl.ANY), VMEM, VMEM],
-        out_shape=jax.ShapeDtypeStruct((8, 2 * TILE, PAIRS), own.dtype),
+def copies_kernel(skip, *refs):
+    *blocks, out = refs[skip:]
+    for n in range(out.shape[0]):
+        start = 0
+        for block in blocks:
+            out[n, start : start + block.shape[0], :] = block[...]
+            start += block.shape[0]
+
+
+def copies(count, after, *blocks):
+    rows = sum(b.shape[0] for b in blocks)
+    return pl.pallas_call(
+        functools.partial(copies_kernel, len(after)),
+        in_specs=[pl.BlockSpec(memory_space=pl.ANY)] * len(after) + [VMEM] * len(blocks),
+        out_shape=jax.ShapeDtypeStruct((count, rows, PAIRS), blocks[0].dtype),
         compiler_params=params(4),
-        name="begin",
-    )(after, own, far)
-
-
-def mirror_kernel(after, x_hbm, a0, a1, a2, a3, own_ref, other_ref, x, left, right, rows, sem):
-    def copy(c):
-        return pltpu.make_async_copy(
-            x_hbm.at[:, c * CHUNK : (c + 1) * CHUNK], x.at[c], sem.at[c]
-        )
-
-    order = (3, 4, 5, 0, 1, 2)
-    for c in order:
-        copy(c).start()
-    blocks = [a.at[k] for a in (a0, a1, a2, a3) for k in range(6)]
+        name="copies",
+    )(*after, *blocks)
+
+
+def mirror_kernel(x, a0, a1, a2, a3, own_ref, other_ref, left, right, rows):
+    quarters = (a0, a1, a2, a3)
     for h, wide in enumerate((left, right)):
         lanes = slice(h * 128, h * 128 + 128)
         for i in range(NCOLS):
-            wide[pl.ds(i, TILE, stride=PAD), :] = blocks[i][:, lanes].astype(jnp.float32)
+            block = quarters[i // 6][i % 6, :, lanes]
+            wide[pl.ds(i, TILE, stride=PAD), :] = block.astype(jnp.float32)
         for i in range(NCOLS, PAD):
             wide[pl.ds(i, TILE, stride=PAD), :] = jnp.zeros((TILE, 128), jnp.float32)
         rows[:, lanes] = wide[...].astype(jnp.bfloat16)
-    for c in order:
-        copy(c).wait()
-        out = own_ref if c < 3 else other_ref
-        start = c % 3 * CHUNK
-        out[start : start + CHUNK, :] = lax.dot_general(
-            x[c], rows[...], (((0,), (0,)), ((), ())), preferred_element_type=jnp.float32
-        )
-
-
-def mirror(after, x, *quarters):
+    for out, base in ((other_ref, HALF), (own_ref, 0)):
+        for start in range(0, HALF, CHUNK):
+            out[start : start + CHUNK, :] = lax.dot_general(
+                x[:, base + start : base + start + CHUNK],
+                rows[...],
+                (((0,), (0,)), ((), ())),
+                preferred_element_type=jnp.float32,
+            )
+
+
+def mirror(x, *quarters):
     half = jax.ShapeDtypeStruct((HALF, PAIRS), jnp.float32)
     return pl.pallas_call(
         mirror_kernel,
-        in_specs=[pl.BlockSpec(memory_space=pl.ANY), HBM] + [VMEM] * 4,
         out_shape=(half, half),
         scratch_shapes=[
-            pltpu.VMEM((CHUNKS, TALL, CHUNK), jnp.bfloat16),
             pltpu.VMEM((TALL, 128), jnp.float32),
             pltpu.VMEM((TALL, 128), jnp.float32),
             pltpu.VMEM((TALL, PAIRS), jnp.bfloat16),
-            pltpu.SemaphoreType.DMA((CHUNKS,)),
         ],
-        compiler_params=params(60),
+        compiler_params=params(16),
         cost_estimate=pl.CostEstimate(
             flops=2 * TALL * WIDE * PAIRS, bytes_accessed=8 * 2**20, transcendentals=0
         ),
         name="mirror",
-    )(after, x, *quarters)
+    )(x, *quarters)
 
 
 def code(groups, out):
@@ -195,16 +192,9 @@
     ]
 
 
-def direct_kernel(x_hbm, own_ref, other_ref, o0, o1, o2, o3, x, left, right, sem):
-    def copy(c):
-        rows = slice(c * CHUNK, (c + 1) * CHUNK)
-        return pltpu.make_async_copy(x_hbm.at[rows, :], x.at[rows, :], sem.at[c])
-
-    for c in range(CHUNKS):
-        copy(c).start()
-    for c in range(CHUNKS):
-        rows = slice(c * CHUNK, (c + 1) * CHUNK)
-        copy(c).wait()
+def direct_kernel(x, own_ref, other_ref, o0, o1, o2, o3, left, right):
+    for start in range(0, TALL, CHUNK):
+        rows = slice(start, start + CHUNK)
         both = jnp.dot(
             x[rows, :HALF], own_ref[...], preferred_element_type=jnp.float32
         ) + jnp.dot(x[rows, HALF:], other_ref[...], preferred_element_type=jnp.float32)
@@ -225,15 +215,12 @@
     coded = jax.ShapeDtypeStruct((LINE + EXTRA, PAIRS), jnp.int16)
     return pl.pallas_call(
         direct_kernel,
-        in_specs=[HBM, VMEM, VMEM],
         out_shape=(jax.ShapeDtypeStruct((LINE, PAIRS), jnp.float32),) + (coded,) * 3,
         scratch_shapes=[
-            pltpu.VMEM((TALL, WIDE), jnp.bfloat16),
             pltpu.VMEM((TALL, 128), jnp.float32),
             pltpu.VMEM((TALL, 128), jnp.float32),
-            pltpu.SemaphoreType.DMA((CHUNKS,)),
         ],
-        compiler_params=params(60),
+        compiler_params=params(16),
         cost_estimate=pl.CostEstimate(
             flops=2 * TALL * WIDE * PAIRS, bytes_accessed=8 * 2**20, transcendentals=0
         ),
@@ -280,19 +267,21 @@
 def sum_x_kernel(keep, c1, c2, c3, out):
     parts = [decode(c, 6) for c in (c1, c2, c3)]
     for n in range(6):
-        out[n] = (keep[n * TILE : (n + 1) * TILE, :] + parts[0][n]) + (parts[1][n] + parts[2][n])
+        near = keep[n * TILE : (n + 1) * TILE, :]
+        code([(near + parts[0][n]) + (parts[1][n] + parts[2][n])], out.at[n])
 
 
 def sum_x(keep, *coded):
     return pl.pallas_call(
         sum_x_kernel,
-        out_shape=jax.ShapeDtypeStruct((6, TILE, PAIRS), jnp.float32),
+        out_shape=jax.ShapeDtypeStruct((6, TILE + EXTRA, PAIRS), jnp.int16),
         compiler_params=params(4),
         name="sum_x",
     )(keep, *coded)
 
 
-def end_kernel(residual, near, far, line, out):
+def end_kernel(residual, near, far, coded, out):
+    line = [decode(coded.at[n], 1)[0] for n in range(6)]
     a = (line[0] + line[1]) + (line[2] + line[3])
     out[...] = (residual[...] + (near[...] + far[...])) + (a + (line[4] + line[5]))
 
@@ -321,14 +310,20 @@
     far = lax.ppermute(amplitudes, "zh", SWAP)
     line = trade(jnp.broadcast_to(amplitudes[None], (6, TILE, PAIRS)), "zl")
     x, placed = place(tile_map[0, 0].T, v_tiles[0, 0])
-    own = trade(begin(placed, amplitudes, far), "y").reshape(HALF, PAIRS)
+    both = copies(8, (placed,), amplitudes, far)
+    own = trade(both, "y").reshape(HALF, PAIRS)
+    quarters = [line] + [swap_x(line, k) for k in (1, 2, 3)]
+    own, *quarters = lax.optimization_barrier((own, *quarters))
+
     other = lax.ppermute(own, "co", SWAP)
-
-    keep, send = mirror(own, x, line, *(swap_x(line, k) for k in (1, 2, 3)))
+    keep, send = mirror(x, *quarters)
     got = lax.ppermute(send, "co", SWAP)
-    row_parts = trade(code_y(keep, got), "y")
-
     parts = direct(x, own, other)
+    got, *parts = lax.optimization_barrier((got, *parts))
+    coded_y = code_y(keep, got)
+    coded_y, *parts = lax.optimization_barrier((coded_y, *parts))
+    row_parts = trade(coded_y, "y")
+
     col_line = sum_x(parts[0], *(swap_x(parts[k], k) for k in (1, 2, 3)))
     col_line = trade(col_line, "zl")
 

time: 135 us -> 117 us (0.87)
  the two profiles are of different devices: /device:TPU:10 before, /device:TPU:4 now
where the time goes in v4:
time: 117 us; the launch traced here: 116 us
  starting transfers between devices  71.2 us (61%)
  waiting for transfers between devices  22.9 us (20%)
  Pallas kernels  17.2 us (15%)
  local copies, waits for them, and re-layouts  4.52 us (4%)
    all_to_all x4, starting transfers between devices, trade(): return lax.all_to_all(block, axis, split_axis=0, concat_axis=0)  33.9 us
    ppermute x6, starting transfers between devices, swap_x(): return lax.ppermute(block, 'x', [(i, i ^ k) for i in range(4)])  19 us
    all_to_all x4, waiting for transfers between devices, trade(): return lax.all_to_all(block, axis, split_axis=0, concat_axis=0)  11 us
    ppermute x6, waiting for transfers between devices, swap_x(): return lax.ppermute(block, 'x', [(i, i ^ k) for i in range(4)])  10.6 us
    ppermute x1, starting transfers between devices, per_device(): far = lax.ppermute(amplitudes, 'zh', SWAP)  10 us
    pallas_call x1, Pallas kernels, place(): pl.pallas_call(place_kernel, in_specs=[VMEM, HBM], out_specs=(HBM, VMEM),...  8.97 us
    ppermute x1, starting transfers between devices, per_device(): row_far = lax.ppermute(row_send, 'zh', SWAP)  3.79 us
    unnamed x8, local copies, waits for them, and re-layouts  3.03 us
  transfers between devices with their start and end apart: 14, of which 7 were waited for; matrix products, arithmetic and copies ran while one was open for 0% of the time, Pallas kernels for 11%

profile of v4, /device:TPU:4, one launch (start us, length us, event | category | flops | bytes accessed | tf_op | source)
XLA Modules:
  0.0 116.1 jit_solution(9201658299697075956)
XLA Ops:
  0.0 0.0 copy-start.1
  0.0 1.5 %broadcast_in_dim.2 = bf16[6,48,256]{2,1,0:T(8,128)(2,1)} broadcast(bf16[48,256]{1,0:T(8,128)(2,1)} %refs_1_.1), dimensions={1,2} | broadcast | bytes 172032 | tf_op jit(solution)/shard_map/broadcast_in_dim | solution.py:311
  1.5 12.1 %all-to-all-start.1 = ((bf16[6,48,256]{2,1,0:T(8,128)(2,1)}), bf16[6,48,256]{2,1,0:T(8,128)(2,1)S(1)}, u32[]{:S(2)}, u32[]{:S(2)}) async-start(bf16[6,48,256]{2,1,0:T(8,128)(2,1)} %broadcast_in_dim.2), calls=%async_computation.1 | async-start | bytes 294912 | tf_op jit(solution)/shard_map/all_to_all | solution.py:306
  13.6 10.0 %collective-permute-start = (bf16[48,256]{1,0:T(8,128)(2,1)}, bf16[48,256]{1,0:T(8,128)(2,1)S(1)}, u32[]{:S(2)}, u32[]{:S(2)}) collective-permute-start(bf16[48,256]{1,0:T(8,128)(2,1)} %refs_1_.1), channel_id=1, source_target_pairs={{0,384},{384,0},{1,385},{385,1},{2,386},{386,2},{3,387},{387,3},{4... | collective-permute-start | bytes 73736 | tf_op jit(solution)/shard_map/ppermute | solution.py:310
  23.6 9.0 %place.1 = (bf16[1536,1536]{1,0:T(8,128)(2,1)}, f32[8,128]{1,0:T(8,128)}) custom-call(s32[2,385]{1,0:T(2,128)} %bitcast.8, bf16[385,2304]{1,0:T(8,128)(2,1)} %bitcast.7), custom_call_target="tpu_custom_call" | custom-call | flops 2415919104 | bytes 8388608 | tf_op jit(solution)/shard_map/place/pallas_call | solution.py:90
  32.6 0.0 collective-permute-done.refs_2_
  32.6 0.0 copy-done.1
  32.6 0.0 copy-start.3
  32.6 0.7 copy-done.3
  33.3 0.8 copies.1
  34.1 0.0 all-to-all-done.1.a0
  34.1 7.1 %all-to-all-start = ((bf16[8,96,256]{2,1,0:T(8,128)(2,1)}), bf16[8,96,256]{2,1,0:T(8,128)(2,1)S(1)}, u32[]{:S(2)}, u32[]{:S(2)}) async-start(bf16[8,96,256]{2,1,0:T(8,128)(2,1)} %copies.1), calls=%async_computation | async-start | bytes 786432 | tf_op jit(solution)/shard_map/all_to_all | solution.py:306
  41.2 2.4 %collective-permute-start.3 = (bf16[6,48,256]{2,1,0:T(8,128)(2,1)S(1)}, bf16[6,48,256]{2,1,0:T(8,128)(2,1)S(1)}, u32[]{:S(2)}, u32[]{:S(2)}) collective-permute-start(bf16[6,48,256]{2,1,0:T(8,128)(2,1)S(1)} %all-to-all-done.1.a0), channel_id=1, source_target_pairs={{0,3},{1,2},{2,1},{3,0},{4,7},{5,6},{6,5},{7,4},{8,11},{9,10},{10,... | collective-permute-start | bytes 442376 | tf_op jit(solution)/shard_map/ppermute | solution.py:302
  43.6 4.6 %collective-permute-start.2 = (bf16[6,48,256]{2,1,0:T(8,128)(2,1)S(1)}, bf16[6,48,256]{2,1,0:T(8,128)(2,1)S(1)}, u32[]{:S(2)}, u32[]{:S(2)}) collective-permute-start(bf16[6,48,256]{2,1,0:T(8,128)(2,1)S(1)} %all-to-all-done.1.a0), channel_id=1, source_target_pairs={{0,2},{1,3},{2,0},{3,1},{4,6},{5,7},{6,4},{7,5},{8,10},{9,11},{10,... | collective-permute-start | bytes 442376 | tf_op jit(solution)/shard_map/ppermute | solution.py:302
  48.3 2.7 %collective-permute-start.1 = (bf16[6,48,256]{2,1,0:T(8,128)(2,1)S(1)}, bf16[6,48,256]{2,1,0:T(8,128)(2,1)S(1)}, u32[]{:S(2)}, u32[]{:S(2)}) collective-permute-start(bf16[6,48,256]{2,1,0:T(8,128)(2,1)S(1)} %all-to-all-done.1.a0), channel_id=1, source_target_pairs={{0,1},{1,0},{2,3},{3,2},{4,5},{5,4},{6,7},{7,6},{8,9},{9,8},{10,11... | collective-permute-start | bytes 442376 | tf_op jit(solution)/shard_map/ppermute | solution.py:302
  51.0 0.0 collective-permute-done.3.a3
  51.0 2.6 %collective-permute-done.2.a2 = bf16[6,48,256]{2,1,0:T(8,128)(2,1)S(1)} collective-permute-done((bf16[6,48,256]{2,1,0:T(8,128)(2,1)S(1)}, bf16[6,48,256]{2,1,0:T(8,128)(2,1)S(1)}, u32[]{:S(2)}, u32[]{:S(2)}) %collective-permute-start.2) | collective-permute-done | bytes 147488 | tf_op jit(solution)/shard_map/ppermute | solution.py:302
  53.7 1.7 %collective-permute-done.1.a1 = bf16[6,48,256]{2,1,0:T(8,128)(2,1)S(1)} collective-permute-done((bf16[6,48,256]{2,1,0:T(8,128)(2,1)S(1)}, bf16[6,48,256]{2,1,0:T(8,128)(2,1)S(1)}, u32[]{:S(2)}, u32[]{:S(2)}) %collective-permute-start.1) | collective-permute-done | bytes 147488 | tf_op jit(solution)/shard_map/ppermute | solution.py:302
  55.4 0.0 all-to-all-done
  55.4 0.0 copy-start
  55.4 2.3 %copy-done = bf16[1536,1536]{1,0:T(8,128)(2,1)S(1)} copy-done((bf16[1536,1536]{1,0:T(8,128)(2,1)S(1)}, bf16[1536,1536]{1,0:T(8,128)(2,1)}, u32[]{:S(2)}) %copy-start) | copy-done | bytes 4718616
  57.7 2.5 %mirror.1 = (f32[768,256]{1,0:T(8,128)S(1)}, f32[768,256]{1,0:T(8,128)S(1)}) custom-call(bf16[1536,1536]{1,0:T(8,128)(2,1)S(1)} %copy-done, bf16[6,48,256]{2,1,0:T(8,128)(2,1)S(1)} %all-to-all-done.1.a0, bf16[6,48,256]{2,1,0:T(8,128)(2,1)S(1)} %collective-permute-done.1.a1, bf16[6,48,256]{2,1,0:T(8,128)(2,1)S(1)} %collective-permute-done.2.a2, ...), custom_call_target="tpu_custom_call" | custom-call | flops 1207959552 | bytes 8388608 | tf_op jit(solution)/shard_map/mirror/pallas_call | solution.py:156
  60.2 0.0 copy-start.2
  60.2 2.1 %collective-permute-start.4 = (f32[768,256]{1,0:T(8,128)S(1)}, f32[768,256]{1,0:T(8,128)S(1)}, u32[]{:S(2)}, u32[]{:S(2)}) collective-permute-start(f32[768,256]{1,0:T(8,128)S(1)} %get-tuple-element.37), channel_id=1, source_target_pairs={{0,24},{24,0},{1,25},{25,1},{2,26},{26,2},{3,27},{27,3},{4,28},{28... | collective-permute-start | bytes 2359304 | tf_op jit(solution)/shard_map/ppermute | solution.py:320
  62.3 2.4 %collective-permute-start.5 = (bf16[768,256]{1,0:T(8,128)(2,1)S(1)}, bf16[768,256]{1,0:T(8,128)(2,1)S(1)}, u32[]{:S(2)}, u32[]{:S(2)}) collective-permute-start(bf16[768,256]{1,0:T(8,128)(2,1)S(1)} %bitcast.5), channel_id=1, source_target_pairs={{0,24},{24,0},{1,25},{25,1},{2,26},{26,2},{3,27},{27,3},{4,28},{28... | collective-permute-start | bytes 1179656 | tf_op jit(solution)/shard_map/ppermute | solution.py:318
  64.7 1.3 %collective-permute-done.5.other_ref = bf16[768,256]{1,0:T(8,128)(2,1)S(1)} collective-permute-done((bf16[768,256]{1,0:T(8,128)(2,1)S(1)}, bf16[768,256]{1,0:T(8,128)(2,1)S(1)}, u32[]{:S(2)}, u32[]{:S(2)}) %collective-permute-start.5) | collective-permute-done | bytes 393248 | tf_op jit(solution)/shard_map/ppermute | solution.py:318
  66.0 2.1 %direct.1 = (f32[288,256]{1,0:T(8,128)S(1)}, s16[304,256]{1,0:T(8,128)(2,1)S(1)}, s16[304,256]{1,0:T(8,128)(2,1)S(1)}, s16[304,256]{1,0:T(8,128)(2,1)S(1)}) custom-call(bf16[1536,1536]{1,0:T(8,128)(2,1)S(1)} %copy-done, bf16[768,256]{1,0:T(8,128)(2,1)S(1)} %bitcast.6, bf16[768,256]{1,0:T(8,128)(2,1)S(1)} %collective-permute-done.5.other_ref), custom_call_target="tpu_custom_call" | custom-call | flops 1207959552 | bytes 8388608 | tf_op jit(solution)/shard_map/direct/pallas_call | solution.py:216
  68.1 0.0 collective-permute-done.4.got
  68.1 1.2 %code_y.1 = s16[8,112,256]{2,1,0:T(8,128)(2,1)} custom-call(f32[768,256]{1,0:T(8,128)S(1)} %get-tuple-element.36.keep, f32[768,256]{1,0:T(8,128)S(1)} %collective-permute-done.4.got), custom_call_target="tpu_custom_call" | custom-call | tf_op jit(solution)/shard_map/code_y/pallas_call | solution.py:243
  69.3 7.2 %all-to-all-start.2 = ((s16[8,112,256]{2,1,0:T(8,128)(2,1)}), s16[8,112,256]{2,1,0:T(8,128)(2,1)S(1)}, u32[]{:S(2)}, u32[]{:S(2)}) async-start(s16[8,112,256]{2,1,0:T(8,128)(2,1)} %code_y.1), calls=%async_computation.2 | async-start | bytes 917504 | tf_op jit(solution)/shard_map/all_to_all | solution.py:306
  76.6 3.0 %collective-permute-start.7 = (s16[304,256]{1,0:T(8,128)(2,1)S(1)}, s16[304,256]{1,0:T(8,128)(2,1)S(1)}, u32[]{:S(2)}, u32[]{:S(2)}) collective-permute-start(s16[304,256]{1,0:T(8,128)(2,1)S(1)} %get-tuple-element.52), channel_id=1, source_target_pairs={{0,1},{1,0},{2,3},{3,2},{4,5},{5,4},{6,7},{7,6},{8,9},{9,8},{10,11... | collective-permute-start | bytes 466952 | tf_op jit(solution)/shard_map/ppermute | solution.py:302
  79.6 2.4 %collective-permute-start.8 = (s16[304,256]{1,0:T(8,128)(2,1)S(1)}, s16[304,256]{1,0:T(8,128)(2,1)S(1)}, u32[]{:S(2)}, u32[]{:S(2)}) collective-permute-start(s16[304,256]{1,0:T(8,128)(2,1)S(1)} %get-tuple-element.53), channel_id=1, source_target_pairs={{0,2},{1,3},{2,0},{3,1},{4,6},{5,7},{6,4},{7,5},{8,10},{9,11},{10,... | collective-permute-start | bytes 466952 | tf_op jit(solution)/shard_map/ppermute | solution.py:302
  82.0 3.8 %collective-permute-start.9 = (s16[304,256]{1,0:T(8,128)(2,1)S(1)}, s16[304,256]{1,0:T(8,128)(2,1)S(1)}, u32[]{:S(2)}, u32[]{:S(2)}) collective-permute-start(s16[304,256]{1,0:T(8,128)(2,1)S(1)} %get-tuple-element.54), channel_id=1, source_target_pairs={{0,3},{1,2},{2,1},{3,0},{4,7},{5,6},{6,5},{7,4},{8,11},{9,10},{10,... | collective-permute-start | bytes 466952 | tf_op jit(solution)/shard_map/ppermute | solution.py:302
  85.8 0.0 collective-permute-done.7.c1
  85.8 3.0 %collective-permute-done.8.c2 = s16[304,256]{1,0:T(8,128)(2,1)S(1)} collective-permute-done((s16[304,256]{1,0:T(8,128)(2,1)S(1)}, s16[304,256]{1,0:T(8,128)(2,1)S(1)}, u32[]{:S(2)}, u32[]{:S(2)}) %collective-permute-start.8) | collective-permute-done | bytes 155680 | tf_op jit(solution)/shard_map/ppermute | solution.py:302
  88.8 3.2 %collective-permute-done.9.c3 = s16[304,256]{1,0:T(8,128)(2,1)S(1)} collective-permute-done((s16[304,256]{1,0:T(8,128)(2,1)S(1)}, s16[304,256]{1,0:T(8,128)(2,1)S(1)}, u32[]{:S(2)}, u32[]{:S(2)}) %collective-permute-start.9) | collective-permute-done | bytes 155680 | tf_op jit(solution)/shard_map/ppermute | solution.py:302
  92.1 0.9 sum_x.1
  93.0 0.2 all-to-all-done.2.coded
  93.2 7.5 %all-to-all-start.3 = ((s16[6,64,256]{2,1,0:T(8,128)(2,1)}), s16[6,64,256]{2,1,0:T(8,128)(2,1)S(1)}, u32[]{:S(2)}, u32[]{:S(2)}) async-start(s16[6,64,256]{2,1,0:T(8,128)(2,1)} %sum_x.1), calls=%async_computation.3 | async-start | bytes 393216 | tf_op jit(solution)/shard_map/all_to_all | solution.py:306
  100.7 0.1 sum_y.1
  100.8 3.8 %collective-permute-start.6 = (f32[48,256]{1,0:T(8,128)S(1)}, f32[48,256]{1,0:T(8,128)S(1)}, u32[]{:S(2)}, u32[]{:S(2)}) collective-permute-start(f32[48,256]{1,0:T(8,128)S(1)} %get-tuple-element.50), channel_id=1, source_target_pairs={{0,384},{384,0},{1,385},{385,1},{2,386},{386,2},{3,387},{387,3},{4... | collective-permute-start | bytes 147464 | tf_op jit(solution)/shard_map/ppermute | solution.py:331
  104.6 10.8 %all-to-all-done.3.coded = s16[6,64,256]{2,1,0:T(8,128)(2,1)S(1)} async-done(((s16[6,64,256]{2,1,0:T(8,128)(2,1)}), s16[6,64,256]{2,1,0:T(8,128)(2,1)S(1)}, u32[]{:S(2)}, u32[]{:S(2)}) %all-to-all-start.3) | async-done | bytes 196640 | tf_op jit(solution)/shard_map/all_to_all | solution.py:306
  115.4 0.0 collective-permute-done.6.far
  115.4 0.0 copy-done.2
  115.4 0.7 end.1
Async XLA Ops:
  0.0 32.6 %copy-start.1 = (bf16[48,256]{1,0:T(8,128)(2,1)S(1)}, bf16[48,256]{1,0:T(8,128)(2,1)}, u32[]{:S(2)}) copy-start(bf16[48,256]{1,0:T(8,128)(2,1)} %refs_1_.1) | copy-start | bytes 73732
  1.5 32.6 %all-to-all-start.1 = ((bf16[6,48,256]{2,1,0:T(8,128)(2,1)}), bf16[6,48,256]{2,1,0:T(8,128)(2,1)S(1)}, u32[]{:S(2)}, u32[]{:S(2)}) async-start(bf16[6,48,256]{2,1,0:T(8,128)(2,1)} %broadcast_in_dim.2), calls=%async_computation.1 | async-start | bytes 294912 | tf_op jit(solution)/shard_map/all_to_all | solution.py:306
  13.6 19.0 %collective-permute-start = (bf16[48,256]{1,0:T(8,128)(2,1)}, bf16[48,256]{1,0:T(8,128)(2,1)S(1)}, u32[]{:S(2)}, u32[]{:S(2)}) collective-permute-start(bf16[48,256]{1,0:T(8,128)(2,1)} %refs_1_.1), channel_id=1, source_target_pairs={{0,384},{384,0},{1,385},{385,1},{2,386},{386,2},{3,387},{387,3},{4... | collective-permute-start | bytes 73736 | tf_op jit(solution)/shard_map/ppermute | solution.py:310
  32.6 0.7 copy-start.3
  34.1 21.3 %all-to-all-start = ((bf16[8,96,256]{2,1,0:T(8,128)(2,1)}), bf16[8,96,256]{2,1,0:T(8,128)(2,1)S(1)}, u32[]{:S(2)}, u32[]{:S(2)}) async-start(bf16[8,96,256]{2,1,0:T(8,128)(2,1)} %copies.1), calls=%async_computation | async-start | bytes 786432 | tf_op jit(solution)/shard_map/all_to_all | solution.py:306
  41.2 9.8 %collective-permute-start.3 = (bf16[6,48,256]{2,1,0:T(8,128)(2,1)S(1)}, bf16[6,48,256]{2,1,0:T(8,128)(2,1)S(1)}, u32[]{:S(2)}, u32[]{:S(2)}) collective-permute-start(bf16[6,48,256]{2,1,0:T(8,128)(2,1)S(1)} %all-to-all-done.1.a0), channel_id=1, source_target_pairs={{0,3},{1,2},{2,1},{3,0},{4,7},{5,6},{6,5},{7,4},{8,11},{9,10},{10,... | collective-permute-start | bytes 442376 | tf_op jit(solution)/shard_map/ppermute | solution.py:302
  43.6 10.0 %collective-permute-start.2 = (bf16[6,48,256]{2,1,0:T(8,128)(2,1)S(1)}, bf16[6,48,256]{2,1,0:T(8,128)(2,1)S(1)}, u32[]{:S(2)}, u32[]{:S(2)}) collective-permute-start(bf16[6,48,256]{2,1,0:T(8,128)(2,1)S(1)} %all-to-all-done.1.a0), channel_id=1, source_target_pairs={{0,2},{1,3},{2,0},{3,1},{4,6},{5,7},{6,4},{7,5},{8,10},{9,11},{10,... | collective-permute-start | bytes 442376 | tf_op jit(solution)/shard_map/ppermute | solution.py:302
  48.3 7.1 %collective-permute-start.1 = (bf16[6,48,256]{2,1,0:T(8,128)(2,1)S(1)}, bf16[6,48,256]{2,1,0:T(8,128)(2,1)S(1)}, u32[]{:S(2)}, u32[]{:S(2)}) collective-permute-start(bf16[6,48,256]{2,1,0:T(8,128)(2,1)S(1)} %all-to-all-done.1.a0), channel_id=1, source_target_pairs={{0,1},{1,0},{2,3},{3,2},{4,5},{5,4},{6,7},{7,6},{8,9},{9,8},{10,11... | collective-permute-start | bytes 442376 | tf_op jit(solution)/shard_map/ppermute | solution.py:302
  55.4 2.3 %copy-start = (bf16[1536,1536]{1,0:T(8,128)(2,1)S(1)}, bf16[1536,1536]{1,0:T(8,128)(2,1)}, u32[]{:S(2)}) copy-start(bf16[1536,1536]{1,0:T(8,128)(2,1)} %get-tuple-element.30.x) | copy-start | bytes 14155780
  60.2 55.1 %copy-start.2 = (f32[48,256]{1,0:T(8,128)S(1)}, f32[48,256]{1,0:T(8,128)}, u32[]{:S(2)}) copy-start(f32[48,256]{1,0:T(8,128)} %residual.1) | copy-start | bytes 147460
  60.2 7.9 %collective-permute-start.4 = (f32[768,256]{1,0:T(8,128)S(1)}, f32[768,256]{1,0:T(8,128)S(1)}, u32[]{:S(2)}, u32[]{:S(2)}) collective-permute-start(f32[768,256]{1,0:T(8,128)S(1)} %get-tuple-element.37), channel_id=1, source_target_pairs={{0,24},{24,0},{1,25},{25,1},{2,26},{26,2},{3,27},{27,3},{4,28},{28... | collective-permute-start | bytes 2359304 | tf_op jit(solution)/shard_map/ppermute | solution.py:320
  62.3 3.7 %collective-permute-start.5 = (bf16[768,256]{1,0:T(8,128)(2,1)S(1)}, bf16[768,256]{1,0:T(8,128)(2,1)S(1)}, u32[]{:S(2)}, u32[]{:S(2)}) collective-permute-start(bf16[768,256]{1,0:T(8,128)(2,1)S(1)} %bitcast.5), channel_id=1, source_target_pairs={{0,24},{24,0},{1,25},{25,1},{2,26},{26,2},{3,27},{27,3},{4,28},{28... | collective-permute-start | bytes 1179656 | tf_op jit(solution)/shard_map/ppermute | solution.py:318
  69.3 23.8 %all-to-all-start.2 = ((s16[8,112,256]{2,1,0:T(8,128)(2,1)}), s16[8,112,256]{2,1,0:T(8,128)(2,1)S(1)}, u32[]{:S(2)}, u32[]{:S(2)}) async-start(s16[8,112,256]{2,1,0:T(8,128)(2,1)} %code_y.1), calls=%async_computation.2 | async-start | bytes 917504 | tf_op jit(solution)/shard_map/all_to_all | solution.py:306
  76.6 9.2 %collective-permute-start.7 = (s16[304,256]{1,0:T(8,128)(2,1)S(1)}, s16[304,256]{1,0:T(8,128)(2,1)S(1)}, u32[]{:S(2)}, u32[]{:S(2)}) collective-permute-start(s16[304,256]{1,0:T(8,128)(2,1)S(1)} %get-tuple-element.52), channel_id=1, source_target_pairs={{0,1},{1,0},{2,3},{3,2},{4,5},{5,4},{6,7},{7,6},{8,9},{9,8},{10,11... | collective-permute-start | bytes 466952 | tf_op jit(solution)/shard_map/ppermute | solution.py:302
  79.6 9.2 %collective-permute-start.8 = (s16[304,256]{1,0:T(8,128)(2,1)S(1)}, s16[304,256]{1,0:T(8,128)(2,1)S(1)}, u32[]{:S(2)}, u32[]{:S(2)}) collective-permute-start(s16[304,256]{1,0:T(8,128)(2,1)S(1)} %get-tuple-element.53), channel_id=1, source_target_pairs={{0,2},{1,3},{2,0},{3,1},{4,6},{5,7},{6,4},{7,5},{8,10},{9,11},{10,... | collective-permute-start | bytes 466952 | tf_op jit(solution)/shard_map/ppermute | solution.py:302
  82.0 10.0 %collective-permute-start.9 = (s16[304,256]{1,0:T(8,128)(2,1)S(1)}, s16[304,256]{1,0:T(8,128)(2,1)S(1)}, u32[]{:S(2)}, u32[]{:S(2)}) collective-permute-start(s16[304,256]{1,0:T(8,128)(2,1)S(1)} %get-tuple-element.54), channel_id=1, source_target_pairs={{0,3},{1,2},{2,1},{3,0},{4,7},{5,6},{6,5},{7,4},{8,11},{9,10},{10,... | collective-permute-start | bytes 466952 | tf_op jit(solution)/shard_map/ppermute | solution.py:302
  93.2 22.2 %all-to-all-start.3 = ((s16[6,64,256]{2,1,0:T(8,128)(2,1)}), s16[6,64,256]{2,1,0:T(8,128)(2,1)S(1)}, u32[]{:S(2)}, u32[]{:S(2)}) async-start(s16[6,64,256]{2,1,0:T(8,128)(2,1)} %sum_x.1), calls=%async_computation.3 | async-start | bytes 393216 | tf_op jit(solution)/shard_map/all_to_all | solution.py:306
  100.8 14.6 %collective-permute-start.6 = (f32[48,256]{1,0:T(8,128)S(1)}, f32[48,256]{1,0:T(8,128)S(1)}, u32[]{:S(2)}, u32[]{:S(2)}) collective-permute-start(f32[48,256]{1,0:T(8,128)S(1)} %get-tuple-element.50), channel_id=1, source_target_pairs={{0,384},{384,0},{1,385},{385,1},{2,386},{386,2},{3,387},{387,3},{4... | collective-permute-start | bytes 147464 | tf_op jit(solution)/shard_map/ppermute | solution.py:331

commit v5 on v4

--- a/solution.py
+++ b/solution.py
@@ -19,11 +19,11 @@
 HALF = NROWS * TILE // 2
 WIDE = NROWS * TILE
 TALL = PAD * TILE
-GROUP = 8
+GROUP = 16
 GROUPS = TILE // GROUP
 LANES = GROUP * TILE
 CHUNK = 256
-CHUNKS = WIDE // CHUNK
+DEPTH = GROUP * PAD
 LINE = 6 * TILE
 EXTRA = 16
 HBM = pl.BlockSpec(memory_space=pltpu.HBM)
@@ -34,7 +34,7 @@
     return pltpu.CompilerParams(vmem_limit_bytes=mib * 2**20)
 
 
-def place_kernel(map_ref, v_hbm, x_hbm, token_ref, v, x, onehot, dense, v_sem, x_sem):
+def place_kernel(map_ref, v_hbm, x_hbm, v, x, onehot, dense, v_sem, x_sem):
     slots = v_hbm.shape[0]
     places = NROWS * PAD
 
@@ -43,12 +43,11 @@
         return pltpu.make_async_copy(v_hbm.at[:, lanes], v.at[g], v_sem.at[g])
 
     def x_copy(g):
-        rows = pl.ds(pl.multiple_of(g * CHUNK, CHUNK), CHUNK)
+        rows = pl.ds(pl.multiple_of(g * DEPTH, DEPTH), DEPTH)
         return pltpu.make_async_copy(x.at[rows, :], x_hbm.at[rows, :], x_sem.at[g])
 
     for g in range(GROUPS):
         v_copy(g).start()
-    token_ref[...] = jnp.zeros_like(token_ref)
     my_zh, my_y, my_co = (lax.axis_index(a) for a in ROW_AXES)
     my_x = lax.axis_index("x")
     my_row = my_zh * 16 + my_y * 2 + my_co
@@ -77,7 +76,7 @@
             parts = [
                 dense[j * PAD : (j + 1) * PAD, s * TILE : (s + 1) * TILE] for j in range(NROWS)
             ]
-            rows = pl.ds(pl.multiple_of(g * CHUNK + s * PAD, PAD), PAD)
+            rows = pl.ds(pl.multiple_of(g * DEPTH + s * PAD, PAD), PAD)
             x[rows, :] = jnp.concatenate(parts, axis=1)
         x_copy(g).start()
 
@@ -90,11 +89,8 @@
     return pl.pallas_call(
         place_kernel,
         in_specs=[VMEM, HBM],
-        out_specs=(HBM, VMEM),
-        out_shape=(
-            jax.ShapeDtypeStruct((TALL, WIDE), jnp.bfloat16),
-            jax.ShapeDtypeStruct((8, 128), jnp.float32),
-        ),
+        out_specs=HBM,
+        out_shape=jax.ShapeDtypeStruct((TALL, WIDE), jnp.bfloat16),
         scratch_shapes=[
             pltpu.VMEM((GROUPS, slots, LANES), jnp.bfloat16),
             pltpu.VMEM((TALL, WIDE), jnp.bfloat16),
@@ -129,6 +125,20 @@
         compiler_params=params(4),
         name="copies",
     )(*after, *blocks)
+
+
+def meet_kernel(after, x, block, out):
+    out[...] = block[...]
+
+
+def meet(after, x, block):
+    return pl.pallas_call(
+        meet_kernel,
+        in_specs=[pl.BlockSpec(memory_space=pl.ANY), VMEM, VMEM],
+        out_shape=jax.ShapeDtypeStruct(block.shape, block.dtype),
+        compiler_params=params(16),
+        name="meet",
+    )(after, x, block)
 
 
 def mirror_kernel(x, a0, a1, a2, a3, own_ref, other_ref, left, right, rows):
@@ -308,12 +318,13 @@
 
 def per_device(amplitudes, residual_in, v_tiles, tile_map):
     far = lax.ppermute(amplitudes, "zh", SWAP)
-    line = trade(jnp.broadcast_to(amplitudes[None], (6, TILE, PAIRS)), "zl")
-    x, placed = place(tile_map[0, 0].T, v_tiles[0, 0])
-    both = copies(8, (placed,), amplitudes, far)
-    own = trade(both, "y").reshape(HALF, PAIRS)
-    quarters = [line] + [swap_x(line, k) for k in (1, 2, 3)]
-    own, *quarters = lax.optimization_barrier((own, *quarters))
+    line = trade(copies(6, (), amplitudes), "zl")
+    x = place(tile_map[0, 0].T, v_tiles[0, 0])
+    x, far = lax.optimization_barrier((x, far))
+    own = trade(copies(8, (), amplitudes, far), "y").reshape(HALF, PAIRS)
+    quarters = [swap_x(line, k) for k in (1, 2, 3)]
+    near = meet(own, x, line)
+    quarters = [near] + quarters
 
     other = lax.ppermute(own, "co", SWAP)
     keep, send = mirror(x, *quarters)

time: 117 us -> 112 us (0.957)
  waiting for transfers between devices: 22.9 us -> 21.2 us
  local copies, waits for them, and re-layouts: 4.52 us -> 3.08 us
    ppermute x6, waiting for transfers between devices: 10.6 us -> 6.26 us  [swap_x(): return lax.ppermute(block, 'x', [(i, i ^ k) for i in range(4)])]
    all_to_all x4, waiting for transfers between devices: 11 us -> 13.6 us  [trade(): return lax.all_to_all(block, axis, split_axis=0, concat_axis=0)]
    all_to_all x4, starting transfers between devices: 33.9 us -> 31.6 us  [trade(): return lax.all_to_all(block, axis, split_axis=0, concat_axis=0)]
    broadcast_in_dim x1 -> x0, local copies, waits for them, and re-layouts: 1.49 us -> none  [per_device(): line = trade(jnp.broadcast_to(amplitudes[None], (6, TILE, PAIRS)), 'zl')]
    ppermute x1, starting transfers between devices: 3.79 us -> 5.07 us  [per_device(): row_far = lax.ppermute(row_send, 'zh', SWAP)]
    pallas_call x1 -> x2, Pallas kernels: 8.97 us -> 7.71 us  [the longest x1 7.7 us: place(): pl.pallas_call(place_kernel, in_specs=[VMEM, HBM], out_specs=HBM, out_sha...]
  transfers between devices with their start and end apart: 14 -> 14, of which waited for: 7 -> 6; matrix products, arithmetic and copies ran while one was open for 0% -> 0% of each run, Pallas kernels for 11% -> 10%
where the time goes in v5:
time: 112 us; the launch traced here: 111 us
  starting transfers between devices  70.1 us (63%)
  waiting for transfers between devices  21.2 us (19%)
  Pallas kernels  16.7 us (15%)
  local copies, waits for them, and re-layouts  3.08 us (3%)
    all_to_all x4, starting transfers between devices, trade(): return lax.all_to_all(block, axis, split_axis=0, concat_axis=0)  31.6 us
    ppermute x6, starting transfers between devices, swap_x(): return lax.ppermute(block, 'x', [(i, i ^ k) for i in range(4)])  19 us
    all_to_all x4, waiting for transfers between devices, trade(): return lax.all_to_all(block, axis, split_axis=0, concat_axis=0)  13.6 us
    ppermute x1, starting transfers between devices, per_device(): far = lax.ppermute(amplitudes, 'zh', SWAP)  10 us
    pallas_call x1, Pallas kernels, place(): pl.pallas_call(place_kernel, in_specs=[VMEM, HBM], out_specs=HBM, out_sha...  7.7 us
    ppermute x6, waiting for transfers between devices, swap_x(): return lax.ppermute(block, 'x', [(i, i ^ k) for i in range(4)])  6.26 us
    ppermute x1, starting transfers between devices, per_device(): row_far = lax.ppermute(row_send, 'zh', SWAP)  5.07 us
    unnamed x8, local copies, waits for them, and re-layouts  3.08 us
  transfers between devices with their start and end apart: 14, of which 6 were waited for; matrix products, arithmetic and copies ran while one was open for 0% of the time, Pallas kernels for 10%

profile of v5, /device:TPU:4, one launch (start us, length us, event | category | flops | bytes accessed | tf_op | source)
XLA Modules:
  0.0 111.2 jit_solution(17953196120675063065)
XLA Ops:
  0.0 0.0 copy-start.1
  0.0 0.7 copy-done.1
  0.7 0.0 copy-start.2
  0.7 0.7 copies.3
  1.4 12.1 %all-to-all-start.1 = ((bf16[6,48,256]{2,1,0:T(8,128)(2,1)}), bf16[6,48,256]{2,1,0:T(8,128)(2,1)S(1)}, u32[]{:S(2)}, u32[]{:S(2)}) async-start(bf16[6,48,256]{2,1,0:T(8,128)(2,1)} %copies.3), calls=%async_computation.1 | async-start | bytes 294912 | tf_op jit(solution)/shard_map/all_to_all | solution.py:316
  13.5 10.0 %collective-permute-start = (bf16[48,256]{1,0:T(8,128)(2,1)}, bf16[48,256]{1,0:T(8,128)(2,1)S(1)}, u32[]{:S(2)}, u32[]{:S(2)}) collective-permute-start(bf16[48,256]{1,0:T(8,128)(2,1)} %refs_0_.3), channel_id=1, source_target_pairs={{0,384},{384,0},{1,385},{385,1},{2,386},{386,2},{3,387},{387,3},{4... | collective-permute-start | bytes 73736 | tf_op jit(solution)/shard_map/ppermute | solution.py:320
  23.6 7.7 %place.1.x = bf16[1536,1536]{1,0:T(8,128)(2,1)} custom-call(s32[2,385]{1,0:T(2,128)} %bitcast.9, bf16[385,2304]{1,0:T(8,128)(2,1)} %bitcast.8), custom_call_target="tpu_custom_call" | custom-call | flops 2415919104 | bytes 8388608 | tf_op jit(solution)/shard_map/place/pallas_call | solution.py:89
  31.3 0.0 collective-permute-done.refs_1_
  31.3 0.0 copy-done.2
  31.3 0.8 copies.2
  32.1 0.0 all-to-all-done.1.block
  32.1 7.1 %all-to-all-start = ((bf16[8,96,256]{2,1,0:T(8,128)(2,1)}), bf16[8,96,256]{2,1,0:T(8,128)(2,1)S(1)}, u32[]{:S(2)}, u32[]{:S(2)}) async-start(bf16[8,96,256]{2,1,0:T(8,128)(2,1)} %copies.2), calls=%async_computation | async-start | bytes 786432 | tf_op jit(solution)/shard_map/all_to_all | solution.py:316
  39.2 2.4 %collective-permute-start.3 = (bf16[6,48,256]{2,1,0:T(8,128)(2,1)S(1)}, bf16[6,48,256]{2,1,0:T(8,128)(2,1)S(1)}, u32[]{:S(2)}, u32[]{:S(2)}) collective-permute-start(bf16[6,48,256]{2,1,0:T(8,128)(2,1)S(1)} %all-to-all-done.1.block), channel_id=1, source_target_pairs={{0,3},{1,2},{2,1},{3,0},{4,7},{5,6},{6,5},{7,4},{8,11},{9,10},{10,... | collective-permute-start | bytes 442376 | tf_op jit(solution)/shard_map/ppermute | solution.py:312
  41.6 4.6 %collective-permute-start.2 = (bf16[6,48,256]{2,1,0:T(8,128)(2,1)S(1)}, bf16[6,48,256]{2,1,0:T(8,128)(2,1)S(1)}, u32[]{:S(2)}, u32[]{:S(2)}) collective-permute-start(bf16[6,48,256]{2,1,0:T(8,128)(2,1)S(1)} %all-to-all-done.1.block), channel_id=1, source_target_pairs={{0,2},{1,3},{2,0},{3,1},{4,6},{5,7},{6,4},{7,5},{8,10},{9,11},{10,... | collective-permute-start | bytes 442376 | tf_op jit(solution)/shard_map/ppermute | solution.py:312
  46.3 2.7 %collective-permute-start.1 = (bf16[6,48,256]{2,1,0:T(8,128)(2,1)S(1)}, bf16[6,48,256]{2,1,0:T(8,128)(2,1)S(1)}, u32[]{:S(2)}, u32[]{:S(2)}) collective-permute-start(bf16[6,48,256]{2,1,0:T(8,128)(2,1)S(1)} %all-to-all-done.1.block), channel_id=1, source_target_pairs={{0,1},{1,0},{2,3},{3,2},{4,5},{5,4},{6,7},{7,6},{8,9},{9,8},{10,11... | collective-permute-start | bytes 442376 | tf_op jit(solution)/shard_map/ppermute | solution.py:312
  49.0 4.3 %all-to-all-done = bf16[8,96,256]{2,1,0:T(8,128)(2,1)S(1)} async-done(((bf16[8,96,256]{2,1,0:T(8,128)(2,1)}), bf16[8,96,256]{2,1,0:T(8,128)(2,1)S(1)}, u32[]{:S(2)}, u32[]{:S(2)}) %all-to-all-start) | async-done | bytes 393248 | tf_op jit(solution)/shard_map/all_to_all | solution.py:316
  53.3 0.0 copy-start
  53.3 2.3 %copy-done = bf16[1536,1536]{1,0:T(8,128)(2,1)S(1)} copy-done((bf16[1536,1536]{1,0:T(8,128)(2,1)S(1)}, bf16[1536,1536]{1,0:T(8,128)(2,1)}, u32[]{:S(2)}) %copy-start) | copy-done | bytes 4718616
  55.7 0.0 collective-permute-done.3.a3
  55.7 0.0 collective-permute-done.2.a2
  55.7 0.0 collective-permute-done.1.a1
  55.7 2.5 %mirror.1 = (f32[768,256]{1,0:T(8,128)S(1)}, f32[768,256]{1,0:T(8,128)S(1)}) custom-call(bf16[1536,1536]{1,0:T(8,128)(2,1)S(1)} %copy-done, bf16[6,48,256]{2,1,0:T(8,128)(2,1)S(1)} %meet.1.a0, bf16[6,48,256]{2,1,0:T(8,128)(2,1)S(1)} %collective-permute-done.1.a1, bf16[6,48,256]{2,1,0:T(8,128)(2,1)S(1)} %collective-permute-done.2.a2, ...), custom_call_target="tpu_custom_call" | custom-call | flops 1207959552 | bytes 8388608 | tf_op jit(solution)/shard_map/mirror/pallas_call | solution.py:166
  58.2 0.0 copy-start.3
  58.2 2.1 %collective-permute-start.4 = (f32[768,256]{1,0:T(8,128)S(1)}, f32[768,256]{1,0:T(8,128)S(1)}, u32[]{:S(2)}, u32[]{:S(2)}) collective-permute-start(f32[768,256]{1,0:T(8,128)S(1)} %get-tuple-element.28), channel_id=1, source_target_pairs={{0,24},{24,0},{1,25},{25,1},{2,26},{26,2},{3,27},{27,3},{4,28},{28... | collective-permute-start | bytes 2359304 | tf_op jit(solution)/shard_map/ppermute | solution.py:331
  60.3 2.4 %collective-permute-start.5 = (bf16[768,256]{1,0:T(8,128)(2,1)S(1)}, bf16[768,256]{1,0:T(8,128)(2,1)S(1)}, u32[]{:S(2)}, u32[]{:S(2)}) collective-permute-start(bf16[768,256]{1,0:T(8,128)(2,1)S(1)} %bitcast.6), channel_id=1, source_target_pairs={{0,24},{24,0},{1,25},{25,1},{2,26},{26,2},{3,27},{27,3},{4,28},{28... | collective-permute-start | bytes 1179656 | tf_op jit(solution)/shard_map/ppermute | solution.py:329
  62.7 1.3 %collective-permute-done.5.other_ref = bf16[768,256]{1,0:T(8,128)(2,1)S(1)} collective-permute-done((bf16[768,256]{1,0:T(8,128)(2,1)S(1)}, bf16[768,256]{1,0:T(8,128)(2,1)S(1)}, u32[]{:S(2)}, u32[]{:S(2)}) %collective-permute-start.5) | collective-permute-done | bytes 393248 | tf_op jit(solution)/shard_map/ppermute | solution.py:329
  64.0 2.1 %direct.1 = (f32[288,256]{1,0:T(8,128)S(1)}, s16[304,256]{1,0:T(8,128)(2,1)S(1)}, s16[304,256]{1,0:T(8,128)(2,1)S(1)}, s16[304,256]{1,0:T(8,128)(2,1)S(1)}) custom-call(bf16[1536,1536]{1,0:T(8,128)(2,1)S(1)} %copy-done, bf16[768,256]{1,0:T(8,128)(2,1)S(1)} %bitcast.7, bf16[768,256]{1,0:T(8,128)(2,1)S(1)} %collective-permute-done.5.other_ref), custom_call_target="tpu_custom_call" | custom-call | flops 1207959552 | bytes 8388608 | tf_op jit(solution)/shard_map/direct/pallas_call | solution.py:226
  66.1 0.0 collective-permute-done.4.got
  66.1 1.2 %code_y.1 = s16[8,112,256]{2,1,0:T(8,128)(2,1)} custom-call(f32[768,256]{1,0:T(8,128)S(1)} %get-tuple-element.27.keep, f32[768,256]{1,0:T(8,128)S(1)} %collective-permute-done.4.got), custom_call_target="tpu_custom_call" | custom-call | tf_op jit(solution)/shard_map/code_y/pallas_call | solution.py:253
  67.3 4.9 %all-to-all-start.2 = ((s16[8,112,256]{2,1,0:T(8,128)(2,1)}), s16[8,112,256]{2,1,0:T(8,128)(2,1)S(1)}, u32[]{:S(2)}, u32[]{:S(2)}) async-start(s16[8,112,256]{2,1,0:T(8,128)(2,1)} %code_y.1), calls=%async_computation.2 | async-start | bytes 917504 | tf_op jit(solution)/shard_map/all_to_all | solution.py:316
  72.2 3.0 %collective-permute-start.7 = (s16[304,256]{1,0:T(8,128)(2,1)S(1)}, s16[304,256]{1,0:T(8,128)(2,1)S(1)}, u32[]{:S(2)}, u32[]{:S(2)}) collective-permute-start(s16[304,256]{1,0:T(8,128)(2,1)S(1)} %get-tuple-element.42), channel_id=1, source_target_pairs={{0,1},{1,0},{2,3},{3,2},{4,5},{5,4},{6,7},{7,6},{8,9},{9,8},{10,11... | collective-permute-start | bytes 466952 | tf_op jit(solution)/shard_map/ppermute | solution.py:312
  75.2 2.4 %collective-permute-start.8 = (s16[304,256]{1,0:T(8,128)(2,1)S(1)}, s16[304,256]{1,0:T(8,128)(2,1)S(1)}, u32[]{:S(2)}, u32[]{:S(2)}) collective-permute-start(s16[304,256]{1,0:T(8,128)(2,1)S(1)} %get-tuple-element.43), channel_id=1, source_target_pairs={{0,2},{1,3},{2,0},{3,1},{4,6},{5,7},{6,4},{7,5},{8,10},{9,11},{10,... | collective-permute-start | bytes 466952 | tf_op jit(solution)/shard_map/ppermute | solution.py:312
  77.7 3.8 %collective-permute-start.9 = (s16[304,256]{1,0:T(8,128)(2,1)S(1)}, s16[304,256]{1,0:T(8,128)(2,1)S(1)}, u32[]{:S(2)}, u32[]{:S(2)}) collective-permute-start(s16[304,256]{1,0:T(8,128)(2,1)S(1)} %get-tuple-element.44), channel_id=1, source_target_pairs={{0,3},{1,2},{2,1},{3,0},{4,7},{5,6},{6,5},{7,4},{8,11},{9,10},{10,... | collective-permute-start | bytes 466952 | tf_op jit(solution)/shard_map/ppermute | solution.py:312
  81.4 0.0 collective-permute-done.7.c1
  81.4 3.0 %collective-permute-done.8.c2 = s16[304,256]{1,0:T(8,128)(2,1)S(1)} collective-permute-done((s16[304,256]{1,0:T(8,128)(2,1)S(1)}, s16[304,256]{1,0:T(8,128)(2,1)S(1)}, u32[]{:S(2)}, u32[]{:S(2)}) %collective-permute-start.8) | collective-permute-done | bytes 155680 | tf_op jit(solution)/shard_map/ppermute | solution.py:312
  84.5 3.2 %collective-permute-done.9.c3 = s16[304,256]{1,0:T(8,128)(2,1)S(1)} collective-permute-done((s16[304,256]{1,0:T(8,128)(2,1)S(1)}, s16[304,256]{1,0:T(8,128)(2,1)S(1)}, u32[]{:S(2)}, u32[]{:S(2)}) %collective-permute-start.9) | collective-permute-done | bytes 155680 | tf_op jit(solution)/shard_map/ppermute | solution.py:312
  87.7 0.9 sum_x.1
  88.6 0.2 all-to-all-done.2.coded
  88.8 7.5 %all-to-all-start.3 = ((s16[6,64,256]{2,1,0:T(8,128)(2,1)}), s16[6,64,256]{2,1,0:T(8,128)(2,1)S(1)}, u32[]{:S(2)}, u32[]{:S(2)}) async-start(s16[6,64,256]{2,1,0:T(8,128)(2,1)} %sum_x.1), calls=%async_computation.3 | async-start | bytes 393216 | tf_op jit(solution)/shard_map/all_to_all | solution.py:316
  96.3 0.1 sum_y.1
  96.4 5.1 %collective-permute-start.6 = (f32[48,256]{1,0:T(8,128)S(1)}, f32[48,256]{1,0:T(8,128)S(1)}, u32[]{:S(2)}, u32[]{:S(2)}) collective-permute-start(f32[48,256]{1,0:T(8,128)S(1)} %get-tuple-element.40), channel_id=1, source_target_pairs={{0,384},{384,0},{1,385},{385,1},{2,386},{386,2},{3,387},{387,3},{4... | collective-permute-start | bytes 147464 | tf_op jit(solution)/shard_map/ppermute | solution.py:342
  101.5 9.1 %all-to-all-done.3.coded = s16[6,64,256]{2,1,0:T(8,128)(2,1)S(1)} async-done(((s16[6,64,256]{2,1,0:T(8,128)(2,1)}), s16[6,64,256]{2,1,0:T(8,128)(2,1)S(1)}, u32[]{:S(2)}, u32[]{:S(2)}) %all-to-all-start.3) | async-done | bytes 196640 | tf_op jit(solution)/shard_map/all_to_all | solution.py:316
  110.6 0.0 collective-permute-done.6.far
  110.6 0.0 copy-done.3
  110.6 0.7 end.1
  (1 shorter events, 0.0 us)
Async XLA Ops:
  0.0 0.7 copy-start.1
  0.7 30.5 %copy-start.2 = (bf16[48,256]{1,0:T(8,128)(2,1)S(1)}, bf16[48,256]{1,0:T(8,128)(2,1)}, u32[]{:S(2)}) copy-start(bf16[48,256]{1,0:T(8,128)(2,1)} %refs_0_.3) | copy-start | bytes 73732
  1.4 30.6 %all-to-all-start.1 = ((bf16[6,48,256]{2,1,0:T(8,128)(2,1)}), bf16[6,48,256]{2,1,0:T(8,128)(2,1)S(1)}, u32[]{:S(2)}, u32[]{:S(2)}) async-start(bf16[6,48,256]{2,1,0:T(8,128)(2,1)} %copies.3), calls=%async_computation.1 | async-start | bytes 294912 | tf_op jit(solution)/shard_map/all_to_all | solution.py:316
  13.5 17.7 %collective-permute-start = (bf16[48,256]{1,0:T(8,128)(2,1)}, bf16[48,256]{1,0:T(8,128)(2,1)S(1)}, u32[]{:S(2)}, u32[]{:S(2)}) collective-permute-start(bf16[48,256]{1,0:T(8,128)(2,1)} %refs_0_.3), channel_id=1, source_target_pairs={{0,384},{384,0},{1,385},{385,1},{2,386},{386,2},{3,387},{387,3},{4... | collective-permute-start | bytes 73736 | tf_op jit(solution)/shard_map/ppermute | solution.py:320
  32.1 21.2 %all-to-all-start = ((bf16[8,96,256]{2,1,0:T(8,128)(2,1)}), bf16[8,96,256]{2,1,0:T(8,128)(2,1)S(1)}, u32[]{:S(2)}, u32[]{:S(2)}) async-start(bf16[8,96,256]{2,1,0:T(8,128)(2,1)} %copies.2), calls=%async_computation | async-start | bytes 786432 | tf_op jit(solution)/shard_map/all_to_all | solution.py:316
  39.2 16.5 %collective-permute-start.3 = (bf16[6,48,256]{2,1,0:T(8,128)(2,1)S(1)}, bf16[6,48,256]{2,1,0:T(8,128)(2,1)S(1)}, u32[]{:S(2)}, u32[]{:S(2)}) collective-permute-start(bf16[6,48,256]{2,1,0:T(8,128)(2,1)S(1)} %all-to-all-done.1.block), channel_id=1, source_target_pairs={{0,3},{1,2},{2,1},{3,0},{4,7},{5,6},{6,5},{7,4},{8,11},{9,10},{10,... | collective-permute-start | bytes 442376 | tf_op jit(solution)/shard_map/ppermute | solution.py:312
  41.6 14.1 %collective-permute-start.2 = (bf16[6,48,256]{2,1,0:T(8,128)(2,1)S(1)}, bf16[6,48,256]{2,1,0:T(8,128)(2,1)S(1)}, u32[]{:S(2)}, u32[]{:S(2)}) collective-permute-start(bf16[6,48,256]{2,1,0:T(8,128)(2,1)S(1)} %all-to-all-done.1.block), channel_id=1, source_target_pairs={{0,2},{1,3},{2,0},{3,1},{4,6},{5,7},{6,4},{7,5},{8,10},{9,11},{10,... | collective-permute-start | bytes 442376 | tf_op jit(solution)/shard_map/ppermute | solution.py:312
  46.3 9.4 %collective-permute-start.1 = (bf16[6,48,256]{2,1,0:T(8,128)(2,1)S(1)}, bf16[6,48,256]{2,1,0:T(8,128)(2,1)S(1)}, u32[]{:S(2)}, u32[]{:S(2)}) collective-permute-start(bf16[6,48,256]{2,1,0:T(8,128)(2,1)S(1)} %all-to-all-done.1.block), channel_id=1, source_target_pairs={{0,1},{1,0},{2,3},{3,2},{4,5},{5,4},{6,7},{7,6},{8,9},{9,8},{10,11... | collective-permute-start | bytes 442376 | tf_op jit(solution)/shard_map/ppermute | solution.py:312
  53.3 2.3 %copy-start = (bf16[1536,1536]{1,0:T(8,128)(2,1)S(1)}, bf16[1536,1536]{1,0:T(8,128)(2,1)}, u32[]{:S(2)}) copy-start(bf16[1536,1536]{1,0:T(8,128)(2,1)} %place.1.x) | copy-start | bytes 14155780
  58.2 52.4 %copy-start.3 = (f32[48,256]{1,0:T(8,128)S(1)}, f32[48,256]{1,0:T(8,128)}, u32[]{:S(2)}) copy-start(f32[48,256]{1,0:T(8,128)} %residual.1) | copy-start | bytes 147460
  58.2 7.9 %collective-permute-start.4 = (f32[768,256]{1,0:T(8,128)S(1)}, f32[768,256]{1,0:T(8,128)S(1)}, u32[]{:S(2)}, u32[]{:S(2)}) collective-permute-start(f32[768,256]{1,0:T(8,128)S(1)} %get-tuple-element.28), channel_id=1, source_target_pairs={{0,24},{24,0},{1,25},{25,1},{2,26},{26,2},{3,27},{27,3},{4,28},{28... | collective-permute-start | bytes 2359304 | tf_op jit(solution)/shard_map/ppermute | solution.py:331
  60.3 3.7 %collective-permute-start.5 = (bf16[768,256]{1,0:T(8,128)(2,1)S(1)}, bf16[768,256]{1,0:T(8,128)(2,1)S(1)}, u32[]{:S(2)}, u32[]{:S(2)}) collective-permute-start(bf16[768,256]{1,0:T(8,128)(2,1)S(1)} %bitcast.6), channel_id=1, source_target_pairs={{0,24},{24,0},{1,25},{25,1},{2,26},{26,2},{3,27},{27,3},{4,28},{28... | collective-permute-start | bytes 1179656 | tf_op jit(solution)/shard_map/ppermute | solution.py:329
  67.3 21.5 %all-to-all-start.2 = ((s16[8,112,256]{2,1,0:T(8,128)(2,1)}), s16[8,112,256]{2,1,0:T(8,128)(2,1)S(1)}, u32[]{:S(2)}, u32[]{:S(2)}) async-start(s16[8,112,256]{2,1,0:T(8,128)(2,1)} %code_y.1), calls=%async_computation.2 | async-start | bytes 917504 | tf_op jit(solution)/shard_map/all_to_all | solution.py:316
  72.2 9.2 %collective-permute-start.7 = (s16[304,256]{1,0:T(8,128)(2,1)S(1)}, s16[304,256]{1,0:T(8,128)(2,1)S(1)}, u32[]{:S(2)}, u32[]{:S(2)}) collective-permute-start(s16[304,256]{1,0:T(8,128)(2,1)S(1)} %get-tuple-element.42), channel_id=1, source_target_pairs={{0,1},{1,0},{2,3},{3,2},{4,5},{5,4},{6,7},{7,6},{8,9},{9,8},{10,11... | collective-permute-start | bytes 466952 | tf_op jit(solution)/shard_map/ppermute | solution.py:312
  75.2 9.2 %collective-permute-start.8 = (s16[304,256]{1,0:T(8,128)(2,1)S(1)}, s16[304,256]{1,0:T(8,128)(2,1)S(1)}, u32[]{:S(2)}, u32[]{:S(2)}) collective-permute-start(s16[304,256]{1,0:T(8,128)(2,1)S(1)} %get-tuple-element.43), channel_id=1, source_target_pairs={{0,2},{1,3},{2,0},{3,1},{4,6},{5,7},{6,4},{7,5},{8,10},{9,11},{10,... | collective-permute-start | bytes 466952 | tf_op jit(solution)/shard_map/ppermute | solution.py:312
  77.7 10.0 %collective-permute-start.9 = (s16[304,256]{1,0:T(8,128)(2,1)S(1)}, s16[304,256]{1,0:T(8,128)(2,1)S(1)}, u32[]{:S(2)}, u32[]{:S(2)}) collective-permute-start(s16[304,256]{1,0:T(8,128)(2,1)S(1)} %get-tuple-element.44), channel_id=1, source_target_pairs={{0,3},{1,2},{2,1},{3,0},{4,7},{5,6},{6,5},{7,4},{8,11},{9,10},{10,... | collective-permute-start | bytes 466952 | tf_op jit(solution)/shard_map/ppermute | solution.py:312
  88.8 21.7 %all-to-all-start.3 = ((s16[6,64,256]{2,1,0:T(8,128)(2,1)}), s16[6,64,256]{2,1,0:T(8,128)(2,1)S(1)}, u32[]{:S(2)}, u32[]{:S(2)}) async-start(s16[6,64,256]{2,1,0:T(8,128)(2,1)} %sum_x.1), calls=%async_computation.3 | async-start | bytes 393216 | tf_op jit(solution)/shard_map/all_to_all | solution.py:316
  96.4 14.1 %collective-permute-start.6 = (f32[48,256]{1,0:T(8,128)S(1)}, f32[48,256]{1,0:T(8,128)S(1)}, u32[]{:S(2)}, u32[]{:S(2)}) collective-permute-start(f32[48,256]{1,0:T(8,128)S(1)} %get-tuple-element.40), channel_id=1, source_target_pairs={{0,384},{384,0},{1,385},{385,1},{2,386},{386,2},{3,387},{387,3},{4... | collective-permute-start | bytes 147464 | tf_op jit(solution)/shard_map/ppermute | solution.py:342

commit v6 on v5

--- a/solution.py
+++ b/solution.py
@@ -202,7 +202,7 @@
     ]
 
 
-def direct_kernel(x, own_ref, other_ref, o0, o1, o2, o3, left, right):
+def direct_kernel(x, own_ref, other_ref, o0, o3, coded, left, right):
     for start in range(0, TALL, CHUNK):
         rows = slice(start, start + CHUNK)
         both = jnp.dot(
@@ -215,17 +215,19 @@
         rows = pl.ds(i, TILE, stride=PAD)
         return jnp.concatenate([left[rows, :], right[rows, :]], axis=1)
 
-    for q, out in ((1, o1), (2, o2), (3, o3)):
-        code([block(q * 6 + n) for n in range(6)], out)
-    for n in range(6):
-        o0[n * TILE : (n + 1) * TILE, :] = block(n)
+    for q in (1, 2):
+        code([block(q * 6 + n) for n in range(6)], coded.at[q - 1])
+    for q, out in ((0, o0), (3, o3)):
+        for n in range(6):
+            out[n * TILE : (n + 1) * TILE, :] = block(q * 6 + n)
 
 
 def direct(x, own, other):
-    coded = jax.ShapeDtypeStruct((LINE + EXTRA, PAIRS), jnp.int16)
+    line = jax.ShapeDtypeStruct((LINE, PAIRS), jnp.float32)
+    coded = jax.ShapeDtypeStruct((2, LINE + EXTRA, PAIRS), jnp.int16)
     return pl.pallas_call(
         direct_kernel,
-        out_shape=(jax.ShapeDtypeStruct((LINE, PAIRS), jnp.float32),) + (coded,) * 3,
+        out_shape=(line, line, coded),
         scratch_shapes=[
             pltpu.VMEM((TALL, 128), jnp.float32),
             pltpu.VMEM((TALL, 128), jnp.float32),
@@ -274,20 +276,39 @@
     )(coded)
 
 
-def sum_x_kernel(keep, c1, c2, c3, out):
-    parts = [decode(c, 6) for c in (c1, c2, c3)]
+def half_x_kernel(o0, o3, got, near, send):
+    first, second = decode(got.at[0], 6), decode(got.at[1], 6)
     for n in range(6):
-        near = keep[n * TILE : (n + 1) * TILE, :]
-        code([(near + parts[0][n]) + (parts[1][n] + parts[2][n])], out.at[n])
-
-
-def sum_x(keep, *coded):
+        rows = slice(n * TILE, (n + 1) * TILE)
+        near[rows, :] = o0[rows, :] + first[n]
+    code([o3[n * TILE : (n + 1) * TILE, :] + second[n] for n in range(6)], send)
+
+
+def half_x(o0, o3, got):
+    return pl.pallas_call(
+        half_x_kernel,
+        out_shape=(
+            jax.ShapeDtypeStruct((LINE, PAIRS), jnp.float32),
+            jax.ShapeDtypeStruct((LINE + EXTRA, PAIRS), jnp.int16),
+        ),
+        compiler_params=params(6),
+        name="half_x",
+    )(o0, o3, got)
+
+
+def sum_x_kernel(near, got, out):
+    parts = decode(got, 6)
+    for n in range(6):
+        code([near[n * TILE : (n + 1) * TILE, :] + parts[n]], out.at[n])
+
+
+def sum_x(near, got):
     return pl.pallas_call(
         sum_x_kernel,
         out_shape=jax.ShapeDtypeStruct((6, TILE + EXTRA, PAIRS), jnp.int16),
         compiler_params=params(4),
         name="sum_x",
-    )(keep, *coded)
+    )(near, got)
 
 
 def end_kernel(residual, near, far, coded, out):
@@ -322,20 +343,21 @@
     x = place(tile_map[0, 0].T, v_tiles[0, 0])
     x, far = lax.optimization_barrier((x, far))
     own = trade(copies(8, (), amplitudes, far), "y").reshape(HALF, PAIRS)
-    quarters = [swap_x(line, k) for k in (1, 2, 3)]
-    near = meet(own, x, line)
-    quarters = [near] + quarters
+    quarters = [meet(own, x, line)] + [swap_x(line, k) for k in (1, 2, 3)]
+    own, *quarters = lax.optimization_barrier((own, *quarters))
 
     other = lax.ppermute(own, "co", SWAP)
+    o0, o3, pair = direct(x, own, other)
+    o0, *quarters = lax.optimization_barrier((o0, *quarters))
+    beside = swap_x(pair, 1)
+
     keep, send = mirror(x, *quarters)
+    send, beside = lax.optimization_barrier((send, beside))
     got = lax.ppermute(send, "co", SWAP)
-    parts = direct(x, own, other)
-    got, *parts = lax.optimization_barrier((got, *parts))
-    coded_y = code_y(keep, got)
-    coded_y, *parts = lax.optimization_barrier((coded_y, *parts))
-    row_parts = trade(coded_y, "y")
-
-    col_line = sum_x(parts[0], *(swap_x(parts[k], k) for k in (1, 2, 3)))
+    near, last = half_x(o0, o3, beside)
+    got, near, last = lax.optimization_barrier((got, near, last))
+    row_parts = trade(code_y(keep, got), "y")
+    col_line = sum_x(near, swap_x(last, 3))
     col_line = trade(col_line, "zl")
 
     row_near, row_send = sum_y(row_parts)

time: 112 us -> 123 us (1.098)
  waiting for transfers between devices: 21.2 us -> 36.2 us
  starting transfers between devices: 70.1 us -> 65.4 us
    all_to_all x4, waiting for transfers between devices: 13.6 us -> 21.2 us  [trade(): return lax.all_to_all(block, axis, split_axis=0, concat_axis=0)]
    ppermute x6 -> x5, waiting for transfers between devices: 6.26 us -> 11.3 us  [swap_x(): return lax.ppermute(block, 'x', [(i, i ^ k) for i in range(4)])]
    ppermute x6 -> x5, starting transfers between devices: 19 us -> 15 us  [swap_x(): return lax.ppermute(block, 'x', [(i, i ^ k) for i in range(4)])]
    ppermute x1, waiting for transfers between devices: 0.01 us -> 2.05 us  [per_device(): got = lax.ppermute(send, 'co', SWAP)]
  transfers between devices with their start and end apart: 14 -> 13, of which waited for: 6 -> 7; matrix products, arithmetic and copies ran while one was open for 0% -> 0% of each run, Pallas kernels for 10% -> 10%
where the time goes in v6:
time: 123 us; the launch traced here: 122 us
  starting transfers between devices  65.4 us (53%)
  waiting for transfers between devices  36.2 us (29%)
  Pallas kernels  16.9 us (14%)
  local copies, waits for them, and re-layouts  3.08 us (3%)
    all_to_all x4, starting transfers between devices, trade(): return lax.all_to_all(block, axis, split_axis=0, concat_axis=0)  31.5 us
    all_to_all x4, waiting for transfers between devices, trade(): return lax.all_to_all(block, axis, split_axis=0, concat_axis=0)  21.2 us
    ppermute x5, starting transfers between devices, swap_x(): return lax.ppermute(block, 'x', [(i, i ^ k) for i in range(4)])  15 us
    ppermute x5, waiting for transfers between devices, swap_x(): return lax.ppermute(block, 'x', [(i, i ^ k) for i in range(4)])  11.3 us
    ppermute x1, starting transfers between devices, per_device(): far = lax.ppermute(amplitudes, 'zh', SWAP)  10 us
    pallas_call x1, Pallas kernels, place(): pl.pallas_call(place_kernel, in_specs=[VMEM, HBM], out_specs=HBM, out_sha...  7.7 us
    ppermute x1, starting transfers between devices, per_device(): row_far = lax.ppermute(row_send, 'zh', SWAP)  5.07 us
    unnamed x8, local copies, waits for them, and re-layouts  3.08 us
  transfers between devices with their start and end apart: 13, of which 7 were waited for; matrix products, arithmetic and copies ran while one was open for 0% of the time, Pallas kernels for 10%

profile of v6, /device:TPU:4, one launch (start us, length us, event | category | flops | bytes accessed | tf_op | source)
XLA Modules:
  0.0 121.8 jit_solution(11805986634924162068)
XLA Ops:
  0.0 0.0 copy-start.1
  0.0 0.7 copy-done.1
  0.7 0.0 copy-start.2
  0.7 0.7 copies.3
  1.4 12.1 %all-to-all-start.1 = ((bf16[6,48,256]{2,1,0:T(8,128)(2,1)}), bf16[6,48,256]{2,1,0:T(8,128)(2,1)S(1)}, u32[]{:S(2)}, u32[]{:S(2)}) async-start(bf16[6,48,256]{2,1,0:T(8,128)(2,1)} %copies.3), calls=%async_computation.1 | async-start | bytes 294912 | tf_op jit(solution)/shard_map/all_to_all | solution.py:337
  13.5 10.0 %collective-permute-start = (bf16[48,256]{1,0:T(8,128)(2,1)}, bf16[48,256]{1,0:T(8,128)(2,1)S(1)}, u32[]{:S(2)}, u32[]{:S(2)}) collective-permute-start(bf16[48,256]{1,0:T(8,128)(2,1)} %refs_0_.3), channel_id=1, source_target_pairs={{0,384},{384,0},{1,385},{385,1},{2,386},{386,2},{3,387},{387,3},{4... | collective-permute-start | bytes 73736 | tf_op jit(solution)/shard_map/ppermute | solution.py:341
  23.6 7.7 %place.1.x = bf16[1536,1536]{1,0:T(8,128)(2,1)} custom-call(s32[2,385]{1,0:T(2,128)} %bitcast.9, bf16[385,2304]{1,0:T(8,128)(2,1)} %bitcast.8), custom_call_target="tpu_custom_call" | custom-call | flops 2415919104 | bytes 8388608 | tf_op jit(solution)/shard_map/place/pallas_call | solution.py:89
  31.3 0.0 collective-permute-done.refs_1_
  31.3 0.0 copy-done.2
  31.3 0.8 copies.2
  32.1 0.0 all-to-all-done.1.block
  32.1 7.1 %all-to-all-start = ((bf16[8,96,256]{2,1,0:T(8,128)(2,1)}), bf16[8,96,256]{2,1,0:T(8,128)(2,1)S(1)}, u32[]{:S(2)}, u32[]{:S(2)}) async-start(bf16[8,96,256]{2,1,0:T(8,128)(2,1)} %copies.2), calls=%async_computation | async-start | bytes 786432 | tf_op jit(solution)/shard_map/all_to_all | solution.py:337
  39.2 2.4 %collective-permute-start.3 = (bf16[6,48,256]{2,1,0:T(8,128)(2,1)S(1)}, bf16[6,48,256]{2,1,0:T(8,128)(2,1)S(1)}, u32[]{:S(2)}, u32[]{:S(2)}) collective-permute-start(bf16[6,48,256]{2,1,0:T(8,128)(2,1)S(1)} %all-to-all-done.1.block), channel_id=1, source_target_pairs={{0,3},{1,2},{2,1},{3,0},{4,7},{5,6},{6,5},{7,4},{8,11},{9,10},{10,... | collective-permute-start | bytes 442376 | tf_op jit(solution)/shard_map/ppermute | solution.py:333
  41.6 4.6 %collective-permute-start.2 = (bf16[6,48,256]{2,1,0:T(8,128)(2,1)S(1)}, bf16[6,48,256]{2,1,0:T(8,128)(2,1)S(1)}, u32[]{:S(2)}, u32[]{:S(2)}) collective-permute-start(bf16[6,48,256]{2,1,0:T(8,128)(2,1)S(1)} %all-to-all-done.1.block), channel_id=1, source_target_pairs={{0,2},{1,3},{2,0},{3,1},{4,6},{5,7},{6,4},{7,5},{8,10},{9,11},{10,... | collective-permute-start | bytes 442376 | tf_op jit(solution)/shard_map/ppermute | solution.py:333
  46.3 2.7 %collective-permute-start.1 = (bf16[6,48,256]{2,1,0:T(8,128)(2,1)S(1)}, bf16[6,48,256]{2,1,0:T(8,128)(2,1)S(1)}, u32[]{:S(2)}, u32[]{:S(2)}) collective-permute-start(bf16[6,48,256]{2,1,0:T(8,128)(2,1)S(1)} %all-to-all-done.1.block), channel_id=1, source_target_pairs={{0,1},{1,0},{2,3},{3,2},{4,5},{5,4},{6,7},{7,6},{8,9},{9,8},{10,11... | collective-permute-start | bytes 442376 | tf_op jit(solution)/shard_map/ppermute | solution.py:333
  49.0 4.3 %all-to-all-done = bf16[8,96,256]{2,1,0:T(8,128)(2,1)S(1)} async-done(((bf16[8,96,256]{2,1,0:T(8,128)(2,1)}), bf16[8,96,256]{2,1,0:T(8,128)(2,1)S(1)}, u32[]{:S(2)}, u32[]{:S(2)}) %all-to-all-start) | async-done | bytes 393248 | tf_op jit(solution)/shard_map/all_to_all | solution.py:337
  53.3 0.0 copy-start
  53.3 2.3 %copy-done = bf16[1536,1536]{1,0:T(8,128)(2,1)S(1)} copy-done((bf16[1536,1536]{1,0:T(8,128)(2,1)S(1)}, bf16[1536,1536]{1,0:T(8,128)(2,1)}, u32[]{:S(2)}) %copy-start) | copy-done | bytes 4718616
  55.7 0.0 collective-permute-done.3.a3
  55.7 0.0 collective-permute-done.2.a2
  55.7 0.0 collective-permute-done.1.a1
  55.7 1.9 %collective-permute-start.4 = (bf16[768,256]{1,0:T(8,128)(2,1)S(1)}, bf16[768,256]{1,0:T(8,128)(2,1)S(1)}, u32[]{:S(2)}, u32[]{:S(2)}) collective-permute-start(bf16[768,256]{1,0:T(8,128)(2,1)S(1)} %bitcast.6), channel_id=1, source_target_pairs={{0,24},{24,0},{1,25},{25,1},{2,26},{26,2},{3,27},{27,3},{4,28},{28... | collective-permute-start | bytes 1179656 | tf_op jit(solution)/shard_map/ppermute | solution.py:349
  57.6 1.7 %collective-permute-done.4.other_ref = bf16[768,256]{1,0:T(8,128)(2,1)S(1)} collective-permute-done((bf16[768,256]{1,0:T(8,128)(2,1)S(1)}, bf16[768,256]{1,0:T(8,128)(2,1)S(1)}, u32[]{:S(2)}, u32[]{:S(2)}) %collective-permute-start.4) | collective-permute-done | bytes 393248 | tf_op jit(solution)/shard_map/ppermute | solution.py:349
  59.3 2.2 %direct.1 = (f32[288,256]{1,0:T(8,128)S(1)}, f32[288,256]{1,0:T(8,128)S(1)}, s16[2,304,256]{2,1,0:T(8,128)(2,1)S(1)}) custom-call(bf16[1536,1536]{1,0:T(8,128)(2,1)S(1)} %copy-done, bf16[768,256]{1,0:T(8,128)(2,1)S(1)} %bitcast.7, bf16[768,256]{1,0:T(8,128)(2,1)S(1)} %collective-permute-done.4.other_ref), custom_call_target="tpu_custom_call" | custom-call | flops 1207959552 | bytes 8388608 | tf_op jit(solution)/shard_map/direct/pallas_call | solution.py:228
  61.5 3.1 %collective-permute-start.5 = (s16[2,304,256]{2,1,0:T(8,128)(2,1)S(1)}, s16[2,304,256]{2,1,0:T(8,128)(2,1)S(1)}, u32[]{:S(2)}, u32[]{:S(2)}) collective-permute-start(s16[2,304,256]{2,1,0:T(8,128)(2,1)S(1)} %get-tuple-element.45), channel_id=1, source_target_pairs={{0,1},{1,0},{2,3},{3,2},{4,5},{5,4},{6,7},{7,6},{8,9},{9,8},{10,11... | collective-permute-start | bytes 933896 | tf_op jit(solution)/shard_map/ppermute | solution.py:333
  64.6 0.0 copy-start.3
  64.6 2.5 %mirror.1 = (f32[768,256]{1,0:T(8,128)S(1)}, f32[768,256]{1,0:T(8,128)S(1)}) custom-call(bf16[1536,1536]{1,0:T(8,128)(2,1)S(1)} %copy-done, bf16[6,48,256]{2,1,0:T(8,128)(2,1)S(1)} %meet.1.a0, bf16[6,48,256]{2,1,0:T(8,128)(2,1)S(1)} %collective-permute-done.1.a1, bf16[6,48,256]{2,1,0:T(8,128)(2,1)S(1)} %collective-permute-done.2.a2, ...), custom_call_target="tpu_custom_call" | custom-call | flops 1207959552 | bytes 8388608 | tf_op jit(solution)/shard_map/mirror/pallas_call | solution.py:166
  67.1 5.7 %collective-permute-done.5.got = s16[2,304,256]{2,1,0:T(8,128)(2,1)S(1)} collective-permute-done((s16[2,304,256]{2,1,0:T(8,128)(2,1)S(1)}, s16[2,304,256]{2,1,0:T(8,128)(2,1)S(1)}, u32[]{:S(2)}, u32[]{:S(2)}) %collective-permute-start.5) | collective-permute-done | bytes 311328 | tf_op jit(solution)/shard_map/ppermute | solution.py:333
  72.8 1.9 %collective-permute-start.6 = (f32[768,256]{1,0:T(8,128)S(1)}, f32[768,256]{1,0:T(8,128)S(1)}, u32[]{:S(2)}, u32[]{:S(2)}) collective-permute-start(f32[768,256]{1,0:T(8,128)S(1)} %get-tuple-element.46), channel_id=1, source_target_pairs={{0,24},{24,0},{1,25},{25,1},{2,26},{26,2},{3,27},{27,3},{4,28},{28... | collective-permute-start | bytes 2359304 | tf_op jit(solution)/shard_map/ppermute | solution.py:356
  74.7 0.2 half_x.1
  74.9 2.0 %collective-permute-done.6.got = f32[768,256]{1,0:T(8,128)S(1)} collective-permute-done((f32[768,256]{1,0:T(8,128)S(1)}, f32[768,256]{1,0:T(8,128)S(1)}, u32[]{:S(2)}, u32[]{:S(2)}) %collective-permute-start.6) | collective-permute-done | bytes 786464 | tf_op jit(solution)/shard_map/ppermute | solution.py:356
  77.0 1.2 code_y.1
  78.2 4.9 %all-to-all-start.2 = ((s16[8,112,256]{2,1,0:T(8,128)(2,1)}), s16[8,112,256]{2,1,0:T(8,128)(2,1)S(1)}, u32[]{:S(2)}, u32[]{:S(2)}) async-start(s16[8,112,256]{2,1,0:T(8,128)(2,1)} %code_y.1), calls=%async_computation.2 | async-start | bytes 917504 | tf_op jit(solution)/shard_map/all_to_all | solution.py:337
  83.0 2.1 %collective-permute-start.8 = (s16[304,256]{1,0:T(8,128)(2,1)S(1)}, s16[304,256]{1,0:T(8,128)(2,1)S(1)}, u32[]{:S(2)}, u32[]{:S(2)}) collective-permute-start(s16[304,256]{1,0:T(8,128)(2,1)S(1)} %get-tuple-element.56), channel_id=1, source_target_pairs={{0,3},{1,2},{2,1},{3,0},{4,7},{5,6},{6,5},{7,4},{8,11},{9,10},{10,... | collective-permute-start | bytes 466952 | tf_op jit(solution)/shard_map/ppermute | solution.py:333
  85.1 5.6 %collective-permute-done.8.got = s16[304,256]{1,0:T(8,128)(2,1)S(1)} collective-permute-done((s16[304,256]{1,0:T(8,128)(2,1)S(1)}, s16[304,256]{1,0:T(8,128)(2,1)S(1)}, u32[]{:S(2)}, u32[]{:S(2)}) %collective-permute-start.8) | collective-permute-done | bytes 155680 | tf_op jit(solution)/shard_map/ppermute | solution.py:333
  90.7 0.8 sum_x.1
  91.5 7.9 %all-to-all-done.2.coded = s16[8,112,256]{2,1,0:T(8,128)(2,1)S(1)} async-done(((s16[8,112,256]{2,1,0:T(8,128)(2,1)}), s16[8,112,256]{2,1,0:T(8,128)(2,1)S(1)}, u32[]{:S(2)}, u32[]{:S(2)}) %all-to-all-start.2) | async-done | bytes 458784 | tf_op jit(solution)/shard_map/all_to_all | solution.py:337
  99.4 7.5 %all-to-all-start.3 = ((s16[6,64,256]{2,1,0:T(8,128)(2,1)}), s16[6,64,256]{2,1,0:T(8,128)(2,1)S(1)}, u32[]{:S(2)}, u32[]{:S(2)}) async-start(s16[6,64,256]{2,1,0:T(8,128)(2,1)} %sum_x.1), calls=%async_computation.3 | async-start | bytes 393216 | tf_op jit(solution)/shard_map/all_to_all | solution.py:337
  106.9 0.1 sum_y.1
  107.0 5.1 %collective-permute-start.7 = (f32[48,256]{1,0:T(8,128)S(1)}, f32[48,256]{1,0:T(8,128)S(1)}, u32[]{:S(2)}, u32[]{:S(2)}) collective-permute-start(f32[48,256]{1,0:T(8,128)S(1)} %get-tuple-element.54), channel_id=1, source_target_pairs={{0,384},{384,0},{1,385},{385,1},{2,386},{386,2},{3,387},{387,3},{4... | collective-permute-start | bytes 147464 | tf_op jit(solution)/shard_map/ppermute | solution.py:364
  112.1 9.0 %all-to-all-done.3.coded = s16[6,64,256]{2,1,0:T(8,128)(2,1)S(1)} async-done(((s16[6,64,256]{2,1,0:T(8,128)(2,1)}), s16[6,64,256]{2,1,0:T(8,128)(2,1)S(1)}, u32[]{:S(2)}, u32[]{:S(2)}) %all-to-all-start.3) | async-done | bytes 196640 | tf_op jit(solution)/shard_map/all_to_all | solution.py:337
  121.1 0.0 collective-permute-done.7.far
  121.1 0.0 copy-done.3
  121.1 0.7 end.1
  (1 shorter events, 0.0 us)
Async XLA Ops:
  0.0 0.7 copy-start.1
  0.7 30.5 %copy-start.2 = (bf16[48,256]{1,0:T(8,128)(2,1)S(1)}, bf16[48,256]{1,0:T(8,128)(2,1)}, u32[]{:S(2)}) copy-start(bf16[48,256]{1,0:T(8,128)(2,1)} %refs_0_.3) | copy-start | bytes 73732
  1.4 30.6 %all-to-all-start.1 = ((bf16[6,48,256]{2,1,0:T(8,128)(2,1)}), bf16[6,48,256]{2,1,0:T(8,128)(2,1)S(1)}, u32[]{:S(2)}, u32[]{:S(2)}) async-start(bf16[6,48,256]{2,1,0:T(8,128)(2,1)} %copies.3), calls=%async_computation.1 | async-start | bytes 294912 | tf_op jit(solution)/shard_map/all_to_all | solution.py:337
  13.5 17.7 %collective-permute-start = (bf16[48,256]{1,0:T(8,128)(2,1)}, bf16[48,256]{1,0:T(8,128)(2,1)S(1)}, u32[]{:S(2)}, u32[]{:S(2)}) collective-permute-start(bf16[48,256]{1,0:T(8,128)(2,1)} %refs_0_.3), channel_id=1, source_target_pairs={{0,384},{384,0},{1,385},{385,1},{2,386},{386,2},{3,387},{387,3},{4... | collective-permute-start | bytes 73736 | tf_op jit(solution)/shard_map/ppermute | solution.py:341
  32.1 21.2 %all-to-all-start = ((bf16[8,96,256]{2,1,0:T(8,128)(2,1)}), bf16[8,96,256]{2,1,0:T(8,128)(2,1)S(1)}, u32[]{:S(2)}, u32[]{:S(2)}) async-start(bf16[8,96,256]{2,1,0:T(8,128)(2,1)} %copies.2), calls=%async_computation | async-start | bytes 786432 | tf_op jit(solution)/shard_map/all_to_all | solution.py:337
  39.2 16.5 %collective-permute-start.3 = (bf16[6,48,256]{2,1,0:T(8,128)(2,1)S(1)}, bf16[6,48,256]{2,1,0:T(8,128)(2,1)S(1)}, u32[]{:S(2)}, u32[]{:S(2)}) collective-permute-start(bf16[6,48,256]{2,1,0:T(8,128)(2,1)S(1)} %all-to-all-done.1.block), channel_id=1, source_target_pairs={{0,3},{1,2},{2,1},{3,0},{4,7},{5,6},{6,5},{7,4},{8,11},{9,10},{10,... | collective-permute-start | bytes 442376 | tf_op jit(solution)/shard_map/ppermute | solution.py:333
  41.6 14.1 %collective-permute-start.2 = (bf16[6,48,256]{2,1,0:T(8,128)(2,1)S(1)}, bf16[6,48,256]{2,1,0:T(8,128)(2,1)S(1)}, u32[]{:S(2)}, u32[]{:S(2)}) collective-permute-start(bf16[6,48,256]{2,1,0:T(8,128)(2,1)S(1)} %all-to-all-done.1.block), channel_id=1, source_target_pairs={{0,2},{1,3},{2,0},{3,1},{4,6},{5,7},{6,4},{7,5},{8,10},{9,11},{10,... | collective-permute-start | bytes 442376 | tf_op jit(solution)/shard_map/ppermute | solution.py:333
  46.3 9.4 %collective-permute-start.1 = (bf16[6,48,256]{2,1,0:T(8,128)(2,1)S(1)}, bf16[6,48,256]{2,1,0:T(8,128)(2,1)S(1)}, u32[]{:S(2)}, u32[]{:S(2)}) collective-permute-start(bf16[6,48,256]{2,1,0:T(8,128)(2,1)S(1)} %all-to-all-done.1.block), channel_id=1, source_target_pairs={{0,1},{1,0},{2,3},{3,2},{4,5},{5,4},{6,7},{7,6},{8,9},{9,8},{10,11... | collective-permute-start | bytes 442376 | tf_op jit(solution)/shard_map/ppermute | solution.py:333
  53.3 2.3 %copy-start = (bf16[1536,1536]{1,0:T(8,128)(2,1)S(1)}, bf16[1536,1536]{1,0:T(8,128)(2,1)}, u32[]{:S(2)}) copy-start(bf16[1536,1536]{1,0:T(8,128)(2,1)} %place.1.x) | copy-start | bytes 14155780
  55.7 3.6 %collective-permute-start.4 = (bf16[768,256]{1,0:T(8,128)(2,1)S(1)}, bf16[768,256]{1,0:T(8,128)(2,1)S(1)}, u32[]{:S(2)}, u32[]{:S(2)}) collective-permute-start(bf16[768,256]{1,0:T(8,128)(2,1)S(1)} %bitcast.6), channel_id=1, source_target_pairs={{0,24},{24,0},{1,25},{25,1},{2,26},{26,2},{3,27},{27,3},{4,28},{28... | collective-permute-start | bytes 1179656 | tf_op jit(solution)/shard_map/ppermute | solution.py:349
  61.5 11.3 %collective-permute-start.5 = (s16[2,304,256]{2,1,0:T(8,128)(2,1)S(1)}, s16[2,304,256]{2,1,0:T(8,128)(2,1)S(1)}, u32[]{:S(2)}, u32[]{:S(2)}) collective-permute-start(s16[2,304,256]{2,1,0:T(8,128)(2,1)S(1)} %get-tuple-element.45), channel_id=1, source_target_pairs={{0,1},{1,0},{2,3},{3,2},{4,5},{5,4},{6,7},{7,6},{8,9},{9,8},{10,11... | collective-permute-start | bytes 933896 | tf_op jit(solution)/shard_map/ppermute | solution.py:333
  64.6 56.5 %copy-start.3 = (f32[48,256]{1,0:T(8,128)S(1)}, f32[48,256]{1,0:T(8,128)}, u32[]{:S(2)}) copy-start(f32[48,256]{1,0:T(8,128)} %residual.1) | copy-start | bytes 147460
  72.8 4.2 %collective-permute-start.6 = (f32[768,256]{1,0:T(8,128)S(1)}, f32[768,256]{1,0:T(8,128)S(1)}, u32[]{:S(2)}, u32[]{:S(2)}) collective-permute-start(f32[768,256]{1,0:T(8,128)S(1)} %get-tuple-element.46), channel_id=1, source_target_pairs={{0,24},{24,0},{1,25},{25,1},{2,26},{26,2},{3,27},{27,3},{4,28},{28... | collective-permute-start | bytes 2359304 | tf_op jit(solution)/shard_map/ppermute | solution.py:356
  78.2 21.2 %all-to-all-start.2 = ((s16[8,112,256]{2,1,0:T(8,128)(2,1)}), s16[8,112,256]{2,1,0:T(8,128)(2,1)S(1)}, u32[]{:S(2)}, u32[]{:S(2)}) async-start(s16[8,112,256]{2,1,0:T(8,128)(2,1)} %code_y.1), calls=%async_computation.2 | async-start | bytes 917504 | tf_op jit(solution)/shard_map/all_to_all | solution.py:337
  83.0 7.7 %collective-permute-start.8 = (s16[304,256]{1,0:T(8,128)(2,1)S(1)}, s16[304,256]{1,0:T(8,128)(2,1)S(1)}, u32[]{:S(2)}, u32[]{:S(2)}) collective-permute-start(s16[304,256]{1,0:T(8,128)(2,1)S(1)} %get-tuple-element.56), channel_id=1, source_target_pairs={{0,3},{1,2},{2,1},{3,0},{4,7},{5,6},{6,5},{7,4},{8,11},{9,10},{10,... | collective-permute-start | bytes 466952 | tf_op jit(solution)/shard_map/ppermute | solution.py:333
  99.4 21.7 %all-to-all-start.3 = ((s16[6,64,256]{2,1,0:T(8,128)(2,1)}), s16[6,64,256]{2,1,0:T(8,128)(2,1)S(1)}, u32[]{:S(2)}, u32[]{:S(2)}) async-start(s16[6,64,256]{2,1,0:T(8,128)(2,1)} %sum_x.1), calls=%async_computation.3 | async-start | bytes 393216 | tf_op jit(solution)/shard_map/all_to_all | solution.py:337
  107.0 14.1 %collective-permute-start.7 = (f32[48,256]{1,0:T(8,128)S(1)}, f32[48,256]{1,0:T(8,128)S(1)}, u32[]{:S(2)}, u32[]{:S(2)}) collective-permute-start(f32[48,256]{1,0:T(8,128)S(1)} %get-tuple-element.54), channel_id=1, source_target_pairs={{0,384},{384,0},{1,385},{385,1},{2,386},{386,2},{3,387},{387,3},{4... | collective-permute-start | bytes 147464 | tf_op jit(solution)/shard_map/ppermute | solution.py:364

commit v7 on v5

--- a/solution.py
+++ b/solution.py
@@ -127,18 +127,24 @@
     )(*after, *blocks)
 
 
-def meet_kernel(after, x, block, out):
-    out[...] = block[...]
-
-
-def meet(after, x, block):
-    return pl.pallas_call(
-        meet_kernel,
-        in_specs=[pl.BlockSpec(memory_space=pl.ANY), VMEM, VMEM],
-        out_shape=jax.ShapeDtypeStruct(block.shape, block.dtype),
-        compiler_params=params(16),
-        name="meet",
-    )(after, x, block)
+def six_kernel(block, out, sem):
+    moves = [pltpu.make_async_copy(block, out.at[n], sem.at[n]) for n in range(6)]
+    for move in moves:
+        move.start()
+    for move in moves:
+        move.wait()
+
+
+def six(block):
+    return pl.pallas_call(
+        six_kernel,
+        in_specs=[HBM],
+        out_specs=HBM,
+        out_shape=jax.ShapeDtypeStruct((6,) + block.shape, block.dtype),
+        scratch_shapes=[pltpu.SemaphoreType.DMA((6,))],
+        compiler_params=params(60),
+        name="six",
+    )(block)
 
 
 def mirror_kernel(x, a0, a1, a2, a3, own_ref, other_ref, left, right, rows):
@@ -262,13 +268,17 @@
     totals = decode(coded.at[0], 2)
     for n in range(1, 8):
         totals = [a + b for a, b in zip(totals, decode(coded.at[n], 2))]
-    near[...], send[...] = totals
+    near[...] = totals[0]
+    code([totals[1]], send)
 
 
 def sum_y(coded):
     return pl.pallas_call(
         sum_y_kernel,
-        out_shape=(jax.ShapeDtypeStruct((TILE, PAIRS), jnp.float32),) * 2,
+        out_shape=(
+            jax.ShapeDtypeStruct((TILE, PAIRS), jnp.float32),
+            jax.ShapeDtypeStruct((TILE + EXTRA, PAIRS), jnp.int16),
+        ),
         compiler_params=params(4),
         name="sum_y",
     )(coded)
@@ -293,7 +303,7 @@
 def end_kernel(residual, near, far, coded, out):
     line = [decode(coded.at[n], 1)[0] for n in range(6)]
     a = (line[0] + line[1]) + (line[2] + line[3])
-    out[...] = (residual[...] + (near[...] + far[...])) + (a + (line[4] + line[5]))
+    out[...] = (residual[...] + (near[...] + decode(far, 1)[0])) + (a + (line[4] + line[5]))
 
 
 def end(residual, near, far, line):
@@ -318,23 +328,20 @@
 
 def per_device(amplitudes, residual_in, v_tiles, tile_map):
     far = lax.ppermute(amplitudes, "zh", SWAP)
-    line = trade(copies(6, (), amplitudes), "zl")
+    line = trade(six(amplitudes), "zl")
     x = place(tile_map[0, 0].T, v_tiles[0, 0])
     x, far = lax.optimization_barrier((x, far))
     own = trade(copies(8, (), amplitudes, far), "y").reshape(HALF, PAIRS)
     quarters = [swap_x(line, k) for k in (1, 2, 3)]
-    near = meet(own, x, line)
-    quarters = [near] + quarters
-
+    keep, send = mirror(x, line, *quarters)
+    send, own = lax.optimization_barrier((send, own))
     other = lax.ppermute(own, "co", SWAP)
-    keep, send = mirror(x, *quarters)
     got = lax.ppermute(send, "co", SWAP)
+    coded_y = code_y(keep, got)
+    coded_y, other = lax.optimization_barrier((coded_y, other))
+    row_parts = trade(coded_y, "y")
+
     parts = direct(x, own, other)
-    got, *parts = lax.optimization_barrier((got, *parts))
-    coded_y = code_y(keep, got)
-    coded_y, *parts = lax.optimization_barrier((coded_y, *parts))
-    row_parts = trade(coded_y, "y")
-
     col_line = sum_x(parts[0], *(swap_x(parts[k], k) for k in (1, 2, 3)))
     col_line = trade(col_line, "zl")
 

time: 112 us -> 120 us (1.071)
  the two profiles are of different devices: /device:TPU:4 before, /device:TPU:10 now
where the time goes in v7:
time: 120 us; the launch traced here: 119 us
  starting transfers between devices  72.8 us (61%)
  Pallas kernels  21.6 us (18%)
  waiting for transfers between devices  19.5 us (16%)
  local copies, waits for them, and re-layouts  4.68 us (4%)
    all_to_all x4, starting transfers between devices, trade(): return lax.all_to_all(block, axis, split_axis=0, concat_axis=0)  34.4 us
    ppermute x6, starting transfers between devices, swap_x(): return lax.ppermute(block, 'x', [(i, i ^ k) for i in range(4)])  19 us
    ppermute x6, waiting for transfers between devices, swap_x(): return lax.ppermute(block, 'x', [(i, i ^ k) for i in range(4)])  11.9 us
    ppermute x1, starting transfers between devices, per_device(): far = lax.ppermute(amplitudes, 'zh', SWAP)  10 us
    pallas_call x1, Pallas kernels, place(): pl.pallas_call(place_kernel, in_specs=[VMEM, HBM], out_specs=HBM, out_sha...  7.7 us
    all_to_all x4, waiting for transfers between devices, trade(): return lax.all_to_all(block, axis, split_axis=0, concat_axis=0)  7.5 us
    pallas_call x1, Pallas kernels, six(): pl.pallas_call(six_kernel, in_specs=[HBM], out_specs=HBM, out_shape=jax.S...  5.62 us
    ppermute x1, starting transfers between devices, per_device(): row_far = lax.ppermute(row_send, 'zh', SWAP)  5.11 us
  transfers between devices with their start and end apart: 14, of which 6 were waited for; matrix products, arithmetic and copies ran while one was open for 0% of the time, Pallas kernels for 13%

profile of v7, /device:TPU:10, one launch (start us, length us, event | category | flops | bytes accessed | tf_op | source)
XLA Modules:
  0.0 118.8 jit_solution(15900825343341231072)
XLA Ops:
  0.0 0.0 copy-start.2
  0.0 5.6 %six.1 = bf16[6,48,256]{2,1,0:T(8,128)(2,1)} custom-call(bf16[48,256]{1,0:T(8,128)(2,1)} %refs_0_.1), custom_call_target="tpu_custom_call" | custom-call | tf_op jit(solution)/shard_map/six/pallas_call | solution.py:139
  5.6 12.1 %all-to-all-start = ((bf16[6,48,256]{2,1,0:T(8,128)(2,1)}), bf16[6,48,256]{2,1,0:T(8,128)(2,1)S(1)}, u32[]{:S(2)}, u32[]{:S(2)}) async-start(bf16[6,48,256]{2,1,0:T(8,128)(2,1)} %six.1), calls=%async_computation | async-start | bytes 294912 | tf_op jit(solution)/shard_map/all_to_all | solution.py:326
  17.7 10.0 %collective-permute-start = (bf16[48,256]{1,0:T(8,128)(2,1)}, bf16[48,256]{1,0:T(8,128)(2,1)S(1)}, u32[]{:S(2)}, u32[]{:S(2)}) collective-permute-start(bf16[48,256]{1,0:T(8,128)(2,1)} %refs_0_.1), channel_id=1, source_target_pairs={{0,384},{384,0},{1,385},{385,1},{2,386},{386,2},{3,387},{387,3},{4... | collective-permute-start | bytes 73736 | tf_op jit(solution)/shard_map/ppermute | solution.py:330
  27.8 7.7 %place.1.x = bf16[1536,1536]{1,0:T(8,128)(2,1)} custom-call(s32[2,385]{1,0:T(2,128)} %bitcast.8, bf16[385,2304]{1,0:T(8,128)(2,1)} %bitcast.7), custom_call_target="tpu_custom_call" | custom-call | flops 2415919104 | bytes 8388608 | tf_op jit(solution)/shard_map/place/pallas_call | solution.py:89
  35.5 0.0 collective-permute-done.refs_1_
  35.5 0.0 copy-done.2
  35.5 0.8 copies.1
  36.3 0.0 all-to-all-done.a0
  36.3 7.5 %all-to-all-start.1 = ((bf16[8,96,256]{2,1,0:T(8,128)(2,1)}), bf16[8,96,256]{2,1,0:T(8,128)(2,1)S(1)}, u32[]{:S(2)}, u32[]{:S(2)}) async-start(bf16[8,96,256]{2,1,0:T(8,128)(2,1)} %copies.1), calls=%async_computation.1 | async-start | bytes 786432 | tf_op jit(solution)/shard_map/all_to_all | solution.py:326
  43.8 2.4 %collective-permute-start.1 = (bf16[6,48,256]{2,1,0:T(8,128)(2,1)S(1)}, bf16[6,48,256]{2,1,0:T(8,128)(2,1)S(1)}, u32[]{:S(2)}, u32[]{:S(2)}) collective-permute-start(bf16[6,48,256]{2,1,0:T(8,128)(2,1)S(1)} %all-to-all-done.a0), channel_id=1, source_target_pairs={{0,1},{1,0},{2,3},{3,2},{4,5},{5,4},{6,7},{7,6},{8,9},{9,8},{10,11... | collective-permute-start | bytes 442376 | tf_op jit(solution)/shard_map/ppermute | solution.py:322
  46.3 4.3 %collective-permute-start.2 = (bf16[6,48,256]{2,1,0:T(8,128)(2,1)S(1)}, bf16[6,48,256]{2,1,0:T(8,128)(2,1)S(1)}, u32[]{:S(2)}, u32[]{:S(2)}) collective-permute-start(bf16[6,48,256]{2,1,0:T(8,128)(2,1)S(1)} %all-to-all-done.a0), channel_id=1, source_target_pairs={{0,2},{1,3},{2,0},{3,1},{4,6},{5,7},{6,4},{7,5},{8,10},{9,11},{10,... | collective-permute-start | bytes 442376 | tf_op jit(solution)/shard_map/ppermute | solution.py:322
  50.6 2.4 %collective-permute-start.3 = (bf16[6,48,256]{2,1,0:T(8,128)(2,1)S(1)}, bf16[6,48,256]{2,1,0:T(8,128)(2,1)S(1)}, u32[]{:S(2)}, u32[]{:S(2)}) collective-permute-start(bf16[6,48,256]{2,1,0:T(8,128)(2,1)S(1)} %all-to-all-done.a0), channel_id=1, source_target_pairs={{0,3},{1,2},{2,1},{3,0},{4,7},{5,6},{6,5},{7,4},{8,11},{9,10},{10,... | collective-permute-start | bytes 442376 | tf_op jit(solution)/shard_map/ppermute | solution.py:322
  53.1 0.0 collective-permute-done.1.a1
  53.1 2.0 %collective-permute-done.2.a2 = bf16[6,48,256]{2,1,0:T(8,128)(2,1)S(1)} collective-permute-done((bf16[6,48,256]{2,1,0:T(8,128)(2,1)S(1)}, bf16[6,48,256]{2,1,0:T(8,128)(2,1)S(1)}, u32[]{:S(2)}, u32[]{:S(2)}) %collective-permute-start.2) | collective-permute-done | bytes 147488 | tf_op jit(solution)/shard_map/ppermute | solution.py:322
  55.1 3.1 %collective-permute-done.3.a3 = bf16[6,48,256]{2,1,0:T(8,128)(2,1)S(1)} collective-permute-done((bf16[6,48,256]{2,1,0:T(8,128)(2,1)S(1)}, bf16[6,48,256]{2,1,0:T(8,128)(2,1)S(1)}, u32[]{:S(2)}, u32[]{:S(2)}) %collective-permute-start.3) | collective-permute-done | bytes 147488 | tf_op jit(solution)/shard_map/ppermute | solution.py:322
  58.1 0.0 copy-start
  58.1 2.3 %copy-done = bf16[1536,1536]{1,0:T(8,128)(2,1)S(1)} copy-done((bf16[1536,1536]{1,0:T(8,128)(2,1)S(1)}, bf16[1536,1536]{1,0:T(8,128)(2,1)}, u32[]{:S(2)}) %copy-start) | copy-done | bytes 4718616
  60.4 2.5 %mirror.1 = (f32[768,256]{1,0:T(8,128)S(1)}, f32[768,256]{1,0:T(8,128)S(1)}) custom-call(bf16[1536,1536]{1,0:T(8,128)(2,1)S(1)} %copy-done, bf16[6,48,256]{2,1,0:T(8,128)(2,1)S(1)} %all-to-all-done.a0, bf16[6,48,256]{2,1,0:T(8,128)(2,1)S(1)} %collective-permute-done.1.a1, bf16[6,48,256]{2,1,0:T(8,128)(2,1)S(1)} %collective-permute-done.2.a2, ...), custom_call_target="tpu_custom_call" | custom-call | flops 1207959552 | bytes 8388608 | tf_op jit(solution)/shard_map/mirror/pallas_call | solution.py:172
  63.0 0.0 all-to-all-done.1
  63.0 1.9 %collective-permute-start.4 = (f32[768,256]{1,0:T(8,128)S(1)}, f32[768,256]{1,0:T(8,128)S(1)}, u32[]{:S(2)}, u32[]{:S(2)}) collective-permute-start(f32[768,256]{1,0:T(8,128)S(1)} %get-tuple-element.23), channel_id=1, source_target_pairs={{0,24},{24,0},{1,25},{25,1},{2,26},{26,2},{3,27},{27,3},{4,28},{28... | collective-permute-start | bytes 2359304 | tf_op jit(solution)/shard_map/ppermute | solution.py:339
  64.9 2.4 %collective-permute-start.5 = (bf16[768,256]{1,0:T(8,128)(2,1)S(1)}, bf16[768,256]{1,0:T(8,128)(2,1)S(1)}, u32[]{:S(2)}, u32[]{:S(2)}) collective-permute-start(bf16[768,256]{1,0:T(8,128)(2,1)S(1)} %bitcast.5), channel_id=1, source_target_pairs={{0,24},{24,0},{1,25},{25,1},{2,26},{26,2},{3,27},{27,3},{4,28},{28... | collective-permute-start | bytes 1179656 | tf_op jit(solution)/shard_map/ppermute | solution.py:338
  67.3 0.0 collective-permute-done.4.got
  67.3 0.0 copy-start.3
  67.3 1.2 %code_y.1 = s16[8,112,256]{2,1,0:T(8,128)(2,1)} custom-call(f32[768,256]{1,0:T(8,128)S(1)} %get-tuple-element.20.keep, f32[768,256]{1,0:T(8,128)S(1)} %collective-permute-done.4.got), custom_call_target="tpu_custom_call" | custom-call | tf_op jit(solution)/shard_map/code_y/pallas_call | solution.py:259
  68.5 0.1 collective-permute-done.5.other_ref
  68.6 7.2 %all-to-all-start.2 = ((s16[8,112,256]{2,1,0:T(8,128)(2,1)}), s16[8,112,256]{2,1,0:T(8,128)(2,1)S(1)}, u32[]{:S(2)}, u32[]{:S(2)}) async-start(s16[8,112,256]{2,1,0:T(8,128)(2,1)} %code_y.1), calls=%async_computation.2 | async-start | bytes 917504 | tf_op jit(solution)/shard_map/all_to_all | solution.py:326
  75.9 0.0 copy-start.1
  75.9 2.3 %copy-done.1 = bf16[1536,1536]{1,0:T(8,128)(2,1)S(1)} copy-done((bf16[1536,1536]{1,0:T(8,128)(2,1)S(1)}, bf16[1536,1536]{1,0:T(8,128)(2,1)}, u32[]{:S(2)}) %copy-start.1) | copy-done | bytes 4718616
  78.2 2.1 %direct.1 = (f32[288,256]{1,0:T(8,128)S(1)}, s16[304,256]{1,0:T(8,128)(2,1)S(1)}, s16[304,256]{1,0:T(8,128)(2,1)S(1)}, s16[304,256]{1,0:T(8,128)(2,1)S(1)}) custom-call(bf16[1536,1536]{1,0:T(8,128)(2,1)S(1)} %copy-done.1, bf16[768,256]{1,0:T(8,128)(2,1)S(1)} %bitcast.6, bf16[768,256]{1,0:T(8,128)(2,1)S(1)} %collective-permute-done.5.other_ref), custom_call_target="tpu_custom_call" | custom-call | flops 1207959552 | bytes 8388608 | tf_op jit(solution)/shard_map/direct/pallas_call | solution.py:232
  80.3 4.5 %collective-permute-start.7 = (s16[304,256]{1,0:T(8,128)(2,1)S(1)}, s16[304,256]{1,0:T(8,128)(2,1)S(1)}, u32[]{:S(2)}, u32[]{:S(2)}) collective-permute-start(s16[304,256]{1,0:T(8,128)(2,1)S(1)} %get-tuple-element.30), channel_id=1, source_target_pairs={{0,1},{1,0},{2,3},{3,2},{4,5},{5,4},{6,7},{7,6},{8,9},{9,8},{10,11... | collective-permute-start | bytes 466952 | tf_op jit(solution)/shard_map/ppermute | solution.py:322
  84.7 1.9 %collective-permute-start.8 = (s16[304,256]{1,0:T(8,128)(2,1)S(1)}, s16[304,256]{1,0:T(8,128)(2,1)S(1)}, u32[]{:S(2)}, u32[]{:S(2)}) collective-permute-start(s16[304,256]{1,0:T(8,128)(2,1)S(1)} %get-tuple-element.31), channel_id=1, source_target_pairs={{0,2},{1,3},{2,0},{3,1},{4,6},{5,7},{6,4},{7,5},{8,10},{9,11},{10,... | collective-permute-start | bytes 466952 | tf_op jit(solution)/shard_map/ppermute | solution.py:322
  86.7 3.4 %collective-permute-start.9 = (s16[304,256]{1,0:T(8,128)(2,1)S(1)}, s16[304,256]{1,0:T(8,128)(2,1)S(1)}, u32[]{:S(2)}, u32[]{:S(2)}) collective-permute-start(s16[304,256]{1,0:T(8,128)(2,1)S(1)} %get-tuple-element.32), channel_id=1, source_target_pairs={{0,3},{1,2},{2,1},{3,0},{4,7},{5,6},{6,5},{7,4},{8,11},{9,10},{10,... | collective-permute-start | bytes 466952 | tf_op jit(solution)/shard_map/ppermute | solution.py:322
  90.0 0.0 collective-permute-done.7.c1
  90.1 3.6 %collective-permute-done.8.c2 = s16[304,256]{1,0:T(8,128)(2,1)S(1)} collective-permute-done((s16[304,256]{1,0:T(8,128)(2,1)S(1)}, s16[304,256]{1,0:T(8,128)(2,1)S(1)}, u32[]{:S(2)}, u32[]{:S(2)}) %collective-permute-start.8) | collective-permute-done | bytes 155680 | tf_op jit(solution)/shard_map/ppermute | solution.py:322
  93.7 3.2 %collective-permute-done.9.c3 = s16[304,256]{1,0:T(8,128)(2,1)S(1)} collective-permute-done((s16[304,256]{1,0:T(8,128)(2,1)S(1)}, s16[304,256]{1,0:T(8,128)(2,1)S(1)}, u32[]{:S(2)}, u32[]{:S(2)}) %collective-permute-start.9) | collective-permute-done | bytes 155680 | tf_op jit(solution)/shard_map/ppermute | solution.py:322
  96.9 0.9 sum_x.1
  97.8 0.0 all-to-all-done.2.coded
  97.8 7.5 %all-to-all-start.3 = ((s16[6,64,256]{2,1,0:T(8,128)(2,1)}), s16[6,64,256]{2,1,0:T(8,128)(2,1)S(1)}, u32[]{:S(2)}, u32[]{:S(2)}) async-start(s16[6,64,256]{2,1,0:T(8,128)(2,1)} %sum_x.1), calls=%async_computation.3 | async-start | bytes 393216 | tf_op jit(solution)/shard_map/all_to_all | solution.py:326
  105.3 0.1 sum_y.1
  105.5 5.1 %collective-permute-start.6 = (s16[64,256]{1,0:T(8,128)(2,1)S(1)}, s16[64,256]{1,0:T(8,128)(2,1)S(1)}, u32[]{:S(2)}, u32[]{:S(2)}) collective-permute-start(s16[64,256]{1,0:T(8,128)(2,1)S(1)} %get-tuple-element.27), channel_id=1, source_target_pairs={{0,384},{384,0},{1,385},{385,1},{2,386},{386,2},{3,387},{387,3},{4... | collective-permute-start | bytes 98312 | tf_op jit(solution)/shard_map/ppermute | solution.py:349
  110.6 7.5 %all-to-all-done.3.coded = s16[6,64,256]{2,1,0:T(8,128)(2,1)S(1)} async-done(((s16[6,64,256]{2,1,0:T(8,128)(2,1)}), s16[6,64,256]{2,1,0:T(8,128)(2,1)S(1)}, u32[]{:S(2)}, u32[]{:S(2)}) %all-to-all-start.3) | async-done | bytes 196640 | tf_op jit(solution)/shard_map/all_to_all | solution.py:326
  118.1 0.0 collective-permute-done.6.far
  118.1 0.0 copy-done.3
  118.1 0.7 end.1
Async XLA Ops:
  0.0 35.5 %copy-start.2 = (bf16[48,256]{1,0:T(8,128)(2,1)S(1)}, bf16[48,256]{1,0:T(8,128)(2,1)}, u32[]{:S(2)}) copy-start(bf16[48,256]{1,0:T(8,128)(2,1)} %refs_0_.1) | copy-start | bytes 73732
  5.6 30.7 %all-to-all-start = ((bf16[6,48,256]{2,1,0:T(8,128)(2,1)}), bf16[6,48,256]{2,1,0:T(8,128)(2,1)S(1)}, u32[]{:S(2)}, u32[]{:S(2)}) async-start(bf16[6,48,256]{2,1,0:T(8,128)(2,1)} %six.1), calls=%async_computation | async-start | bytes 294912 | tf_op jit(solution)/shard_map/all_to_all | solution.py:326
  17.7 17.7 %collective-permute-start = (bf16[48,256]{1,0:T(8,128)(2,1)}, bf16[48,256]{1,0:T(8,128)(2,1)S(1)}, u32[]{:S(2)}, u32[]{:S(2)}) collective-permute-start(bf16[48,256]{1,0:T(8,128)(2,1)} %refs_0_.1), channel_id=1, source_target_pairs={{0,384},{384,0},{1,385},{385,1},{2,386},{386,2},{3,387},{387,3},{4... | collective-permute-start | bytes 73736 | tf_op jit(solution)/shard_map/ppermute | solution.py:330
  36.3 26.7 %all-to-all-start.1 = ((bf16[8,96,256]{2,1,0:T(8,128)(2,1)}), bf16[8,96,256]{2,1,0:T(8,128)(2,1)S(1)}, u32[]{:S(2)}, u32[]{:S(2)}) async-start(bf16[8,96,256]{2,1,0:T(8,128)(2,1)} %copies.1), calls=%async_computation.1 | async-start | bytes 786432 | tf_op jit(solution)/shard_map/all_to_all | solution.py:326
  43.8 9.2 %collective-permute-start.1 = (bf16[6,48,256]{2,1,0:T(8,128)(2,1)S(1)}, bf16[6,48,256]{2,1,0:T(8,128)(2,1)S(1)}, u32[]{:S(2)}, u32[]{:S(2)}) collective-permute-start(bf16[6,48,256]{2,1,0:T(8,128)(2,1)S(1)} %all-to-all-done.a0), channel_id=1, source_target_pairs={{0,1},{1,0},{2,3},{3,2},{4,5},{5,4},{6,7},{7,6},{8,9},{9,8},{10,11... | collective-permute-start | bytes 442376 | tf_op jit(solution)/shard_map/ppermute | solution.py:322
  46.3 8.8 %collective-permute-start.2 = (bf16[6,48,256]{2,1,0:T(8,128)(2,1)S(1)}, bf16[6,48,256]{2,1,0:T(8,128)(2,1)S(1)}, u32[]{:S(2)}, u32[]{:S(2)}) collective-permute-start(bf16[6,48,256]{2,1,0:T(8,128)(2,1)S(1)} %all-to-all-done.a0), channel_id=1, source_target_pairs={{0,2},{1,3},{2,0},{3,1},{4,6},{5,7},{6,4},{7,5},{8,10},{9,11},{10,... | collective-permute-start | bytes 442376 | tf_op jit(solution)/shard_map/ppermute | solution.py:322
  50.6 7.5 %collective-permute-start.3 = (bf16[6,48,256]{2,1,0:T(8,128)(2,1)S(1)}, bf16[6,48,256]{2,1,0:T(8,128)(2,1)S(1)}, u32[]{:S(2)}, u32[]{:S(2)}) collective-permute-start(bf16[6,48,256]{2,1,0:T(8,128)(2,1)S(1)} %all-to-all-done.a0), channel_id=1, source_target_pairs={{0,3},{1,2},{2,1},{3,0},{4,7},{5,6},{6,5},{7,4},{8,11},{9,10},{10,... | collective-permute-start | bytes 442376 | tf_op jit(solution)/shard_map/ppermute | solution.py:322
  58.1 2.3 %copy-start = (bf16[1536,1536]{1,0:T(8,128)(2,1)S(1)}, bf16[1536,1536]{1,0:T(8,128)(2,1)}, u32[]{:S(2)}) copy-start(bf16[1536,1536]{1,0:T(8,128)(2,1)} %place.1.x) | copy-start | bytes 14155780
  63.0 4.3 %collective-permute-start.4 = (f32[768,256]{1,0:T(8,128)S(1)}, f32[768,256]{1,0:T(8,128)S(1)}, u32[]{:S(2)}, u32[]{:S(2)}) collective-permute-start(f32[768,256]{1,0:T(8,128)S(1)} %get-tuple-element.23), channel_id=1, source_target_pairs={{0,24},{24,0},{1,25},{25,1},{2,26},{26,2},{3,27},{27,3},{4,28},{28... | collective-permute-start | bytes 2359304 | tf_op jit(solution)/shard_map/ppermute | solution.py:339
  64.9 3.7 %collective-permute-start.5 = (bf16[768,256]{1,0:T(8,128)(2,1)S(1)}, bf16[768,256]{1,0:T(8,128)(2,1)S(1)}, u32[]{:S(2)}, u32[]{:S(2)}) collective-permute-start(bf16[768,256]{1,0:T(8,128)(2,1)S(1)} %bitcast.5), channel_id=1, source_target_pairs={{0,24},{24,0},{1,25},{25,1},{2,26},{26,2},{3,27},{27,3},{4,28},{28... | collective-permute-start | bytes 1179656 | tf_op jit(solution)/shard_map/ppermute | solution.py:338
  67.3 50.8 %copy-start.3 = (f32[48,256]{1,0:T(8,128)S(1)}, f32[48,256]{1,0:T(8,128)}, u32[]{:S(2)}) copy-start(f32[48,256]{1,0:T(8,128)} %residual.1) | copy-start | bytes 147460
  68.6 29.2 %all-to-all-start.2 = ((s16[8,112,256]{2,1,0:T(8,128)(2,1)}), s16[8,112,256]{2,1,0:T(8,128)(2,1)S(1)}, u32[]{:S(2)}, u32[]{:S(2)}) async-start(s16[8,112,256]{2,1,0:T(8,128)(2,1)} %code_y.1), calls=%async_computation.2 | async-start | bytes 917504 | tf_op jit(solution)/shard_map/all_to_all | solution.py:326
  75.9 2.3 %copy-start.1 = (bf16[1536,1536]{1,0:T(8,128)(2,1)S(1)}, bf16[1536,1536]{1,0:T(8,128)(2,1)}, u32[]{:S(2)}) copy-start(bf16[1536,1536]{1,0:T(8,128)(2,1)} %place.1.x) | copy-start | bytes 14155780
  80.3 9.8 %collective-permute-start.7 = (s16[304,256]{1,0:T(8,128)(2,1)S(1)}, s16[304,256]{1,0:T(8,128)(2,1)S(1)}, u32[]{:S(2)}, u32[]{:S(2)}) collective-permute-start(s16[304,256]{1,0:T(8,128)(2,1)S(1)} %get-tuple-element.30), channel_id=1, source_target_pairs={{0,1},{1,0},{2,3},{3,2},{4,5},{5,4},{6,7},{7,6},{8,9},{9,8},{10,11... | collective-permute-start | bytes 466952 | tf_op jit(solution)/shard_map/ppermute | solution.py:322
  84.7 9.0 %collective-permute-start.8 = (s16[304,256]{1,0:T(8,128)(2,1)S(1)}, s16[304,256]{1,0:T(8,128)(2,1)S(1)}, u32[]{:S(2)}, u32[]{:S(2)}) collective-permute-start(s16[304,256]{1,0:T(8,128)(2,1)S(1)} %get-tuple-element.31), channel_id=1, source_target_pairs={{0,2},{1,3},{2,0},{3,1},{4,6},{5,7},{6,4},{7,5},{8,10},{9,11},{10,... | collective-permute-start | bytes 466952 | tf_op jit(solution)/shard_map/ppermute | solution.py:322
  86.7 10.3 %collective-permute-start.9 = (s16[304,256]{1,0:T(8,128)(2,1)S(1)}, s16[304,256]{1,0:T(8,128)(2,1)S(1)}, u32[]{:S(2)}, u32[]{:S(2)}) collective-permute-start(s16[304,256]{1,0:T(8,128)(2,1)S(1)} %get-tuple-element.32), channel_id=1, source_target_pairs={{0,3},{1,2},{2,1},{3,0},{4,7},{5,6},{6,5},{7,4},{8,11},{9,10},{10,... | collective-permute-start | bytes 466952 | tf_op jit(solution)/shard_map/ppermute | solution.py:322
  97.8 20.3 %all-to-all-start.3 = ((s16[6,64,256]{2,1,0:T(8,128)(2,1)}), s16[6,64,256]{2,1,0:T(8,128)(2,1)S(1)}, u32[]{:S(2)}, u32[]{:S(2)}) async-start(s16[6,64,256]{2,1,0:T(8,128)(2,1)} %sum_x.1), calls=%async_computation.3 | async-start | bytes 393216 | tf_op jit(solution)/shard_map/all_to_all | solution.py:326
  105.5 12.6 %collective-permute-start.6 = (s16[64,256]{1,0:T(8,128)(2,1)S(1)}, s16[64,256]{1,0:T(8,128)(2,1)S(1)}, u32[]{:S(2)}, u32[]{:S(2)}) collective-permute-start(s16[64,256]{1,0:T(8,128)(2,1)S(1)} %get-tuple-element.27), channel_id=1, source_target_pairs={{0,384},{384,0},{1,385},{385,1},{2,386},{386,2},{3,387},{387,3},{4... | collective-permute-start | bytes 98312 | tf_op jit(solution)/shard_map/ppermute | solution.py:349

commit v8 on v5

--- a/solution.py
+++ b/solution.py
@@ -262,13 +262,17 @@
     totals = decode(coded.at[0], 2)
     for n in range(1, 8):
         totals = [a + b for a, b in zip(totals, decode(coded.at[n], 2))]
-    near[...], send[...] = totals
+    near[...] = totals[0]
+    code([totals[1]], send)
 
 
 def sum_y(coded):
     return pl.pallas_call(
         sum_y_kernel,
-        out_shape=(jax.ShapeDtypeStruct((TILE, PAIRS), jnp.float32),) * 2,
+        out_shape=(
+            jax.ShapeDtypeStruct((TILE, PAIRS), jnp.float32),
+            jax.ShapeDtypeStruct((TILE + EXTRA, PAIRS), jnp.int16),
+        ),
         compiler_params=params(4),
         name="sum_y",
     )(coded)
@@ -293,7 +297,7 @@
 def end_kernel(residual, near, far, coded, out):
     line = [decode(coded.at[n], 1)[0] for n in range(6)]
     a = (line[0] + line[1]) + (line[2] + line[3])
-    out[...] = (residual[...] + (near[...] + far[...])) + (a + (line[4] + line[5]))
+    out[...] = (residual[...] + (near[...] + decode(far, 1)[0])) + (a + (line[4] + line[5]))
 
 
 def end(residual, near, far, line):
@@ -323,11 +327,11 @@
     x, far = lax.optimization_barrier((x, far))
     own = trade(copies(8, (), amplitudes, far), "y").reshape(HALF, PAIRS)
     quarters = [swap_x(line, k) for k in (1, 2, 3)]
+    own, *quarters = lax.optimization_barrier((own, *quarters))
+    other = lax.ppermute(own, "co", SWAP)
     near = meet(own, x, line)
-    quarters = [near] + quarters
-
-    other = lax.ppermute(own, "co", SWAP)
-    keep, send = mirror(x, *quarters)
+    near, other = lax.optimization_barrier((near, other))
+    keep, send = mirror(x, near, *quarters)
     got = lax.ppermute(send, "co", SWAP)
     parts = direct(x, own, other)
     got, *parts = lax.optimization_barrier((got, *parts))

time: 112 us -> 113 us (level)
  the two profiles are of different devices: /device:TPU:4 before, /device:TPU:8 now
where the time goes in v8:
time: 113 us; the launch traced here: 112 us
  starting transfers between devices  73.8 us (65%)
  waiting for transfers between devices  17.8 us (16%)
  Pallas kernels  16.7 us (15%)
  local copies, waits for them, and re-layouts  3.08 us (3%)
    all_to_all x4, starting transfers between devices, trade(): return lax.all_to_all(block, axis, split_axis=0, concat_axis=0)  34.1 us
    ppermute x6, starting transfers between devices, swap_x(): return lax.ppermute(block, 'x', [(i, i ^ k) for i in range(4)])  20.2 us
    ppermute x6, waiting for transfers between devices, swap_x(): return lax.ppermute(block, 'x', [(i, i ^ k) for i in range(4)])  10.2 us
    ppermute x1, starting transfers between devices, per_device(): far = lax.ppermute(amplitudes, 'zh', SWAP)  10 us
    pallas_call x1, Pallas kernels, place(): pl.pallas_call(place_kernel, in_specs=[VMEM, HBM], out_specs=HBM, out_sha...  7.7 us
    all_to_all x4, waiting for transfers between devices, trade(): return lax.all_to_all(block, axis, split_axis=0, concat_axis=0)  5.99 us
    ppermute x1, starting transfers between devices, per_device(): row_far = lax.ppermute(row_send, 'zh', SWAP)  5.05 us
    unnamed x8, local copies, waits for them, and re-layouts  3.08 us
  transfers between devices with their start and end apart: 14, of which 5 were waited for; matrix products, arithmetic and copies ran while one was open for 0% of the time, Pallas kernels for 10%

profile of v8, /device:TPU:8, one launch (start us, length us, event | category | flops | bytes accessed | tf_op | source)
XLA Modules:
  0.0 111.6 jit_solution(15859777026323516526)
XLA Ops:
  0.0 0.0 copy-start.1
  0.0 0.7 copy-done.1
  0.7 0.0 copy-start.2
  0.7 0.7 copies.3
  1.4 12.1 %all-to-all-start.1 = ((bf16[6,48,256]{2,1,0:T(8,128)(2,1)}), bf16[6,48,256]{2,1,0:T(8,128)(2,1)S(1)}, u32[]{:S(2)}, u32[]{:S(2)}) async-start(bf16[6,48,256]{2,1,0:T(8,128)(2,1)} %copies.3), calls=%async_computation.1 | async-start | bytes 294912 | tf_op jit(solution)/shard_map/all_to_all | solution.py:320
  13.5 10.0 %collective-permute-start = (bf16[48,256]{1,0:T(8,128)(2,1)}, bf16[48,256]{1,0:T(8,128)(2,1)S(1)}, u32[]{:S(2)}, u32[]{:S(2)}) collective-permute-start(bf16[48,256]{1,0:T(8,128)(2,1)} %refs_0_.3), channel_id=1, source_target_pairs={{0,384},{384,0},{1,385},{385,1},{2,386},{386,2},{3,387},{387,3},{4... | collective-permute-start | bytes 73736 | tf_op jit(solution)/shard_map/ppermute | solution.py:324
  23.6 7.7 %place.1.x = bf16[1536,1536]{1,0:T(8,128)(2,1)} custom-call(s32[2,385]{1,0:T(2,128)} %bitcast.9, bf16[385,2304]{1,0:T(8,128)(2,1)} %bitcast.8), custom_call_target="tpu_custom_call" | custom-call | flops 2415919104 | bytes 8388608 | tf_op jit(solution)/shard_map/place/pallas_call | solution.py:89
  31.3 0.0 collective-permute-done.refs_1_
  31.3 0.0 copy-done.2
  31.3 0.8 copies.2
  32.1 0.0 all-to-all-done.1.block
  32.1 7.5 %all-to-all-start = ((bf16[8,96,256]{2,1,0:T(8,128)(2,1)}), bf16[8,96,256]{2,1,0:T(8,128)(2,1)S(1)}, u32[]{:S(2)}, u32[]{:S(2)}) async-start(bf16[8,96,256]{2,1,0:T(8,128)(2,1)} %copies.2), calls=%async_computation | async-start | bytes 786432 | tf_op jit(solution)/shard_map/all_to_all | solution.py:320
  39.6 4.7 %collective-permute-start.3 = (bf16[6,48,256]{2,1,0:T(8,128)(2,1)S(1)}, bf16[6,48,256]{2,1,0:T(8,128)(2,1)S(1)}, u32[]{:S(2)}, u32[]{:S(2)}) collective-permute-start(bf16[6,48,256]{2,1,0:T(8,128)(2,1)S(1)} %all-to-all-done.1.block), channel_id=1, source_target_pairs={{0,3},{1,2},{2,1},{3,0},{4,7},{5,6},{6,5},{7,4},{8,11},{9,10},{10,... | collective-permute-start | bytes 442376 | tf_op jit(solution)/shard_map/ppermute | solution.py:316
  44.3 2.7 %collective-permute-start.2 = (bf16[6,48,256]{2,1,0:T(8,128)(2,1)S(1)}, bf16[6,48,256]{2,1,0:T(8,128)(2,1)S(1)}, u32[]{:S(2)}, u32[]{:S(2)}) collective-permute-start(bf16[6,48,256]{2,1,0:T(8,128)(2,1)S(1)} %all-to-all-done.1.block), channel_id=1, source_target_pairs={{0,2},{1,3},{2,0},{3,1},{4,6},{5,7},{6,4},{7,5},{8,10},{9,11},{10,... | collective-permute-start | bytes 442376 | tf_op jit(solution)/shard_map/ppermute | solution.py:316
  47.0 2.4 %collective-permute-start.1 = (bf16[6,48,256]{2,1,0:T(8,128)(2,1)S(1)}, bf16[6,48,256]{2,1,0:T(8,128)(2,1)S(1)}, u32[]{:S(2)}, u32[]{:S(2)}) collective-permute-start(bf16[6,48,256]{2,1,0:T(8,128)(2,1)S(1)} %all-to-all-done.1.block), channel_id=1, source_target_pairs={{0,1},{1,0},{2,3},{3,2},{4,5},{5,4},{6,7},{7,6},{8,9},{9,8},{10,11... | collective-permute-start | bytes 442376 | tf_op jit(solution)/shard_map/ppermute | solution.py:316
  49.5 0.0 collective-permute-done.3.a3
  49.5 4.9 %collective-permute-done.2.a2 = bf16[6,48,256]{2,1,0:T(8,128)(2,1)S(1)} collective-permute-done((bf16[6,48,256]{2,1,0:T(8,128)(2,1)S(1)}, bf16[6,48,256]{2,1,0:T(8,128)(2,1)S(1)}, u32[]{:S(2)}, u32[]{:S(2)}) %collective-permute-start.2) | collective-permute-done | bytes 147488 | tf_op jit(solution)/shard_map/ppermute | solution.py:316
  54.3 0.0 collective-permute-done.1.a1
  54.3 0.0 all-to-all-done
  54.4 1.9 %collective-permute-start.4 = (bf16[768,256]{1,0:T(8,128)(2,1)S(1)}, bf16[768,256]{1,0:T(8,128)(2,1)S(1)}, u32[]{:S(2)}, u32[]{:S(2)}) collective-permute-start(bf16[768,256]{1,0:T(8,128)(2,1)S(1)} %bitcast.5), channel_id=1, source_target_pairs={{0,24},{24,0},{1,25},{25,1},{2,26},{26,2},{3,27},{27,3},{4,28},{28... | collective-permute-start | bytes 1179656 | tf_op jit(solution)/shard_map/ppermute | solution.py:331
  56.3 0.0 copy-start
  56.3 2.3 %copy-done = bf16[1536,1536]{1,0:T(8,128)(2,1)S(1)} copy-done((bf16[1536,1536]{1,0:T(8,128)(2,1)S(1)}, bf16[1536,1536]{1,0:T(8,128)(2,1)}, u32[]{:S(2)}) %copy-start) | copy-done | bytes 4718616
  58.6 0.0 collective-permute-done.4.other_ref
  58.6 2.5 %mirror.1 = (f32[768,256]{1,0:T(8,128)S(1)}, f32[768,256]{1,0:T(8,128)S(1)}) custom-call(bf16[1536,1536]{1,0:T(8,128)(2,1)S(1)} %copy-done, bf16[6,48,256]{2,1,0:T(8,128)(2,1)S(1)} %meet.1.a0, bf16[6,48,256]{2,1,0:T(8,128)(2,1)S(1)} %collective-permute-done.1.a1, bf16[6,48,256]{2,1,0:T(8,128)(2,1)S(1)} %collective-permute-done.2.a2, ...), custom_call_target="tpu_custom_call" | custom-call | flops 1207959552 | bytes 8388608 | tf_op jit(solution)/shard_map/mirror/pallas_call | solution.py:166
  61.1 0.0 copy-start.3
  61.2 2.5 %collective-permute-start.5 = (f32[768,256]{1,0:T(8,128)S(1)}, f32[768,256]{1,0:T(8,128)S(1)}, u32[]{:S(2)}, u32[]{:S(2)}) collective-permute-start(f32[768,256]{1,0:T(8,128)S(1)} %get-tuple-element.39), channel_id=1, source_target_pairs={{0,24},{24,0},{1,25},{25,1},{2,26},{26,2},{3,27},{27,3},{4,28},{28... | collective-permute-start | bytes 2359304 | tf_op jit(solution)/shard_map/ppermute | solution.py:335
  63.7 2.1 %direct.1 = (f32[288,256]{1,0:T(8,128)S(1)}, s16[304,256]{1,0:T(8,128)(2,1)S(1)}, s16[304,256]{1,0:T(8,128)(2,1)S(1)}, s16[304,256]{1,0:T(8,128)(2,1)S(1)}) custom-call(bf16[1536,1536]{1,0:T(8,128)(2,1)S(1)} %copy-done, bf16[768,256]{1,0:T(8,128)(2,1)S(1)} %bitcast.7, bf16[768,256]{1,0:T(8,128)(2,1)S(1)} %collective-permute-done.4.other_ref), custom_call_target="tpu_custom_call" | custom-call | flops 1207959552 | bytes 8388608 | tf_op jit(solution)/shard_map/direct/pallas_call | solution.py:226
  65.8 0.0 collective-permute-done.5.got
  65.8 1.2 %code_y.1 = s16[8,112,256]{2,1,0:T(8,128)(2,1)} custom-call(f32[768,256]{1,0:T(8,128)S(1)} %get-tuple-element.38.keep, f32[768,256]{1,0:T(8,128)S(1)} %collective-permute-done.5.got), custom_call_target="tpu_custom_call" | custom-call | tf_op jit(solution)/shard_map/code_y/pallas_call | solution.py:253
  67.0 7.2 %all-to-all-start.2 = ((s16[8,112,256]{2,1,0:T(8,128)(2,1)}), s16[8,112,256]{2,1,0:T(8,128)(2,1)S(1)}, u32[]{:S(2)}, u32[]{:S(2)}) async-start(s16[8,112,256]{2,1,0:T(8,128)(2,1)} %code_y.1), calls=%async_computation.2 | async-start | bytes 917504 | tf_op jit(solution)/shard_map/all_to_all | solution.py:320
  74.2 2.5 %collective-permute-start.7 = (s16[304,256]{1,0:T(8,128)(2,1)S(1)}, s16[304,256]{1,0:T(8,128)(2,1)S(1)}, u32[]{:S(2)}, u32[]{:S(2)}) collective-permute-start(s16[304,256]{1,0:T(8,128)(2,1)S(1)} %get-tuple-element.54), channel_id=1, source_target_pairs={{0,1},{1,0},{2,3},{3,2},{4,5},{5,4},{6,7},{7,6},{8,9},{9,8},{10,11... | collective-permute-start | bytes 466952 | tf_op jit(solution)/shard_map/ppermute | solution.py:316
  76.7 4.9 %collective-permute-start.8 = (s16[304,256]{1,0:T(8,128)(2,1)S(1)}, s16[304,256]{1,0:T(8,128)(2,1)S(1)}, u32[]{:S(2)}, u32[]{:S(2)}) collective-permute-start(s16[304,256]{1,0:T(8,128)(2,1)S(1)} %get-tuple-element.55), channel_id=1, source_target_pairs={{0,2},{1,3},{2,0},{3,1},{4,6},{5,7},{6,4},{7,5},{8,10},{9,11},{10,... | collective-permute-start | bytes 466952 | tf_op jit(solution)/shard_map/ppermute | solution.py:316
  81.6 3.0 %collective-permute-start.9 = (s16[304,256]{1,0:T(8,128)(2,1)S(1)}, s16[304,256]{1,0:T(8,128)(2,1)S(1)}, u32[]{:S(2)}, u32[]{:S(2)}) collective-permute-start(s16[304,256]{1,0:T(8,128)(2,1)S(1)} %get-tuple-element.56), channel_id=1, source_target_pairs={{0,3},{1,2},{2,1},{3,0},{4,7},{5,6},{6,5},{7,4},{8,11},{9,10},{10,... | collective-permute-start | bytes 466952 | tf_op jit(solution)/shard_map/ppermute | solution.py:316
  84.6 0.0 collective-permute-done.7.c1
  84.7 1.9 %collective-permute-done.8.c2 = s16[304,256]{1,0:T(8,128)(2,1)S(1)} collective-permute-done((s16[304,256]{1,0:T(8,128)(2,1)S(1)}, s16[304,256]{1,0:T(8,128)(2,1)S(1)}, u32[]{:S(2)}, u32[]{:S(2)}) %collective-permute-start.8) | collective-permute-done | bytes 155680 | tf_op jit(solution)/shard_map/ppermute | solution.py:316
  86.6 3.4 %collective-permute-done.9.c3 = s16[304,256]{1,0:T(8,128)(2,1)S(1)} collective-permute-done((s16[304,256]{1,0:T(8,128)(2,1)S(1)}, s16[304,256]{1,0:T(8,128)(2,1)S(1)}, u32[]{:S(2)}, u32[]{:S(2)}) %collective-permute-start.9) | collective-permute-done | bytes 155680 | tf_op jit(solution)/shard_map/ppermute | solution.py:316
  90.0 0.9 sum_x.1
  90.9 0.0 all-to-all-done.2.coded
  90.9 7.2 %all-to-all-start.3 = ((s16[6,64,256]{2,1,0:T(8,128)(2,1)}), s16[6,64,256]{2,1,0:T(8,128)(2,1)S(1)}, u32[]{:S(2)}, u32[]{:S(2)}) async-start(s16[6,64,256]{2,1,0:T(8,128)(2,1)} %sum_x.1), calls=%async_computation.3 | async-start | bytes 393216 | tf_op jit(solution)/shard_map/all_to_all | solution.py:320
  98.1 0.1 sum_y.1
  98.3 5.0 %collective-permute-start.6 = (s16[64,256]{1,0:T(8,128)(2,1)S(1)}, s16[64,256]{1,0:T(8,128)(2,1)S(1)}, u32[]{:S(2)}, u32[]{:S(2)}) collective-permute-start(s16[64,256]{1,0:T(8,128)(2,1)S(1)} %get-tuple-element.52), channel_id=1, source_target_pairs={{0,384},{384,0},{1,385},{385,1},{2,386},{386,2},{3,387},{387,3},{4... | collective-permute-start | bytes 98312 | tf_op jit(solution)/shard_map/ppermute | solution.py:346
  103.3 6.0 %all-to-all-done.3.coded = s16[6,64,256]{2,1,0:T(8,128)(2,1)S(1)} async-done(((s16[6,64,256]{2,1,0:T(8,128)(2,1)}), s16[6,64,256]{2,1,0:T(8,128)(2,1)S(1)}, u32[]{:S(2)}, u32[]{:S(2)}) %all-to-all-start.3) | async-done | bytes 196640 | tf_op jit(solution)/shard_map/all_to_all | solution.py:320
  109.3 1.7 %collective-permute-done.6.far = s16[64,256]{1,0:T(8,128)(2,1)S(1)} collective-permute-done((s16[64,256]{1,0:T(8,128)(2,1)S(1)}, s16[64,256]{1,0:T(8,128)(2,1)S(1)}, u32[]{:S(2)}, u32[]{:S(2)}) %collective-permute-start.6) | collective-permute-done | bytes 32800 | tf_op jit(solution)/shard_map/ppermute | solution.py:346
  110.9 0.0 copy-done.3
  111.0 0.7 end.1
  (1 shorter events, 0.0 us)
Async XLA Ops:
  0.0 0.7 copy-start.1
  0.7 30.5 %copy-start.2 = (bf16[48,256]{1,0:T(8,128)(2,1)S(1)}, bf16[48,256]{1,0:T(8,128)(2,1)}, u32[]{:S(2)}) copy-start(bf16[48,256]{1,0:T(8,128)(2,1)} %refs_0_.3) | copy-start | bytes 73732
  1.4 30.6 %all-to-all-start.1 = ((bf16[6,48,256]{2,1,0:T(8,128)(2,1)}), bf16[6,48,256]{2,1,0:T(8,128)(2,1)S(1)}, u32[]{:S(2)}, u32[]{:S(2)}) async-start(bf16[6,48,256]{2,1,0:T(8,128)(2,1)} %copies.3), calls=%async_computation.1 | async-start | bytes 294912 | tf_op jit(solution)/shard_map/all_to_all | solution.py:320
  13.5 17.7 %collective-permute-start = (bf16[48,256]{1,0:T(8,128)(2,1)}, bf16[48,256]{1,0:T(8,128)(2,1)S(1)}, u32[]{:S(2)}, u32[]{:S(2)}) collective-permute-start(bf16[48,256]{1,0:T(8,128)(2,1)} %refs_0_.3), channel_id=1, source_target_pairs={{0,384},{384,0},{1,385},{385,1},{2,386},{386,2},{3,387},{387,3},{4... | collective-permute-start | bytes 73736 | tf_op jit(solution)/shard_map/ppermute | solution.py:324
  32.1 22.3 %all-to-all-start = ((bf16[8,96,256]{2,1,0:T(8,128)(2,1)}), bf16[8,96,256]{2,1,0:T(8,128)(2,1)S(1)}, u32[]{:S(2)}, u32[]{:S(2)}) async-start(bf16[8,96,256]{2,1,0:T(8,128)(2,1)} %copies.2), calls=%async_computation | async-start | bytes 786432 | tf_op jit(solution)/shard_map/all_to_all | solution.py:320
  39.6 9.8 %collective-permute-start.3 = (bf16[6,48,256]{2,1,0:T(8,128)(2,1)S(1)}, bf16[6,48,256]{2,1,0:T(8,128)(2,1)S(1)}, u32[]{:S(2)}, u32[]{:S(2)}) collective-permute-start(bf16[6,48,256]{2,1,0:T(8,128)(2,1)S(1)} %all-to-all-done.1.block), channel_id=1, source_target_pairs={{0,3},{1,2},{2,1},{3,0},{4,7},{5,6},{6,5},{7,4},{8,11},{9,10},{10,... | collective-permute-start | bytes 442376 | tf_op jit(solution)/shard_map/ppermute | solution.py:316
  44.3 10.1 %collective-permute-start.2 = (bf16[6,48,256]{2,1,0:T(8,128)(2,1)S(1)}, bf16[6,48,256]{2,1,0:T(8,128)(2,1)S(1)}, u32[]{:S(2)}, u32[]{:S(2)}) collective-permute-start(bf16[6,48,256]{2,1,0:T(8,128)(2,1)S(1)} %all-to-all-done.1.block), channel_id=1, source_target_pairs={{0,2},{1,3},{2,0},{3,1},{4,6},{5,7},{6,4},{7,5},{8,10},{9,11},{10,... | collective-permute-start | bytes 442376 | tf_op jit(solution)/shard_map/ppermute | solution.py:316
  47.0 7.3 %collective-permute-start.1 = (bf16[6,48,256]{2,1,0:T(8,128)(2,1)S(1)}, bf16[6,48,256]{2,1,0:T(8,128)(2,1)S(1)}, u32[]{:S(2)}, u32[]{:S(2)}) collective-permute-start(bf16[6,48,256]{2,1,0:T(8,128)(2,1)S(1)} %all-to-all-done.1.block), channel_id=1, source_target_pairs={{0,1},{1,0},{2,3},{3,2},{4,5},{5,4},{6,7},{7,6},{8,9},{9,8},{10,11... | collective-permute-start | bytes 442376 | tf_op jit(solution)/shard_map/ppermute | solution.py:316
  54.4 4.3 %collective-permute-start.4 = (bf16[768,256]{1,0:T(8,128)(2,1)S(1)}, bf16[768,256]{1,0:T(8,128)(2,1)S(1)}, u32[]{:S(2)}, u32[]{:S(2)}) collective-permute-start(bf16[768,256]{1,0:T(8,128)(2,1)S(1)} %bitcast.5), channel_id=1, source_target_pairs={{0,24},{24,0},{1,25},{25,1},{2,26},{26,2},{3,27},{27,3},{4,28},{28... | collective-permute-start | bytes 1179656 | tf_op jit(solution)/shard_map/ppermute | solution.py:331
  56.3 2.3 %copy-start = (bf16[1536,1536]{1,0:T(8,128)(2,1)S(1)}, bf16[1536,1536]{1,0:T(8,128)(2,1)}, u32[]{:S(2)}) copy-start(bf16[1536,1536]{1,0:T(8,128)(2,1)} %place.1.x) | copy-start | bytes 14155780
  61.1 49.8 %copy-start.3 = (f32[48,256]{1,0:T(8,128)S(1)}, f32[48,256]{1,0:T(8,128)}, u32[]{:S(2)}) copy-start(f32[48,256]{1,0:T(8,128)} %residual.1) | copy-start | bytes 147460
  61.2 4.6 %collective-permute-start.5 = (f32[768,256]{1,0:T(8,128)S(1)}, f32[768,256]{1,0:T(8,128)S(1)}, u32[]{:S(2)}, u32[]{:S(2)}) collective-permute-start(f32[768,256]{1,0:T(8,128)S(1)} %get-tuple-element.39), channel_id=1, source_target_pairs={{0,24},{24,0},{1,25},{25,1},{2,26},{26,2},{3,27},{27,3},{4,28},{28... | collective-permute-start | bytes 2359304 | tf_op jit(solution)/shard_map/ppermute | solution.py:335
  67.0 23.9 %all-to-all-start.2 = ((s16[8,112,256]{2,1,0:T(8,128)(2,1)}), s16[8,112,256]{2,1,0:T(8,128)(2,1)S(1)}, u32[]{:S(2)}, u32[]{:S(2)}) async-start(s16[8,112,256]{2,1,0:T(8,128)(2,1)} %code_y.1), calls=%async_computation.2 | async-start | bytes 917504 | tf_op jit(solution)/shard_map/all_to_all | solution.py:320
  74.2 10.4 %collective-permute-start.7 = (s16[304,256]{1,0:T(8,128)(2,1)S(1)}, s16[304,256]{1,0:T(8,128)(2,1)S(1)}, u32[]{:S(2)}, u32[]{:S(2)}) collective-permute-start(s16[304,256]{1,0:T(8,128)(2,1)S(1)} %get-tuple-element.54), channel_id=1, source_target_pairs={{0,1},{1,0},{2,3},{3,2},{4,5},{5,4},{6,7},{7,6},{8,9},{9,8},{10,11... | collective-permute-start | bytes 466952 | tf_op jit(solution)/shard_map/ppermute | solution.py:316
  76.7 9.9 %collective-permute-start.8 = (s16[304,256]{1,0:T(8,128)(2,1)S(1)}, s16[304,256]{1,0:T(8,128)(2,1)S(1)}, u32[]{:S(2)}, u32[]{:S(2)}) collective-permute-start(s16[304,256]{1,0:T(8,128)(2,1)S(1)} %get-tuple-element.55), channel_id=1, source_target_pairs={{0,2},{1,3},{2,0},{3,1},{4,6},{5,7},{6,4},{7,5},{8,10},{9,11},{10,... | collective-permute-start | bytes 466952 | tf_op jit(solution)/shard_map/ppermute | solution.py:316
  81.6 8.3 %collective-permute-start.9 = (s16[304,256]{1,0:T(8,128)(2,1)S(1)}, s16[304,256]{1,0:T(8,128)(2,1)S(1)}, u32[]{:S(2)}, u32[]{:S(2)}) collective-permute-start(s16[304,256]{1,0:T(8,128)(2,1)S(1)} %get-tuple-element.56), channel_id=1, source_target_pairs={{0,3},{1,2},{2,1},{3,0},{4,7},{5,6},{6,5},{7,4},{8,11},{9,10},{10,... | collective-permute-start | bytes 466952 | tf_op jit(solution)/shard_map/ppermute | solution.py:316
  90.9 18.4 %all-to-all-start.3 = ((s16[6,64,256]{2,1,0:T(8,128)(2,1)}), s16[6,64,256]{2,1,0:T(8,128)(2,1)S(1)}, u32[]{:S(2)}, u32[]{:S(2)}) async-start(s16[6,64,256]{2,1,0:T(8,128)(2,1)} %sum_x.1), calls=%async_computation.3 | async-start | bytes 393216 | tf_op jit(solution)/shard_map/all_to_all | solution.py:320
  98.3 12.7 %collective-permute-start.6 = (s16[64,256]{1,0:T(8,128)(2,1)S(1)}, s16[64,256]{1,0:T(8,128)(2,1)S(1)}, u32[]{:S(2)}, u32[]{:S(2)}) collective-permute-start(s16[64,256]{1,0:T(8,128)(2,1)S(1)} %get-tuple-element.52), channel_id=1, source_target_pairs={{0,384},{384,0},{1,385},{385,1},{2,386},{386,2},{3,387},{387,3},{4... | collective-permute-start | bytes 98312 | tf_op jit(solution)/shard_map/ppermute | solution.py:346

commit v9 on v8

--- a/solution.py
+++ b/solution.py
@@ -326,7 +326,8 @@
     x = place(tile_map[0, 0].T, v_tiles[0, 0])
     x, far = lax.optimization_barrier((x, far))
     own = trade(copies(8, (), amplitudes, far), "y").reshape(HALF, PAIRS)
-    quarters = [swap_x(line, k) for k in (1, 2, 3)]
+    left, right = swap_x(line, 1), swap_x(line, 3)
+    quarters = [left, swap_x(left, 3), right]
     own, *quarters = lax.optimization_barrier((own, *quarters))
     other = lax.ppermute(own, "co", SWAP)
     near = meet(own, x, line)

time: 113 us -> 114 us (level)
  starting transfers between devices: 73.8 us -> 76 us
    ppermute x6, starting transfers between devices: 20.2 us -> 22.1 us  [swap_x(): return lax.ppermute(block, 'x', [(i, i ^ k) for i in range(4)])]
  transfers between devices with their start and end apart: 14 -> 14, of which waited for: 5 -> 6; matrix products, arithmetic and copies ran while one was open for 0% -> 0% of each run, Pallas kernels for 10% -> 10%
where the time goes in v9:
time: 114 us; the launch traced here: 113 us
  starting transfers between devices  76 us (67%)
  waiting for transfers between devices  17.1 us (15%)
  Pallas kernels  16.7 us (15%)
  local copies, waits for them, and re-layouts  3.08 us (3%)
    all_to_all x4, starting transfers between devices, trade(): return lax.all_to_all(block, axis, split_axis=0, concat_axis=0)  34.3 us
    ppermute x6, starting transfers between devices, swap_x(): return lax.ppermute(block, 'x', [(i, i ^ k) for i in range(4)])  22.1 us
    ppermute x1, starting transfers between devices, per_device(): far = lax.ppermute(amplitudes, 'zh', SWAP)  10 us
    ppermute x6, waiting for transfers between devices, swap_x(): return lax.ppermute(block, 'x', [(i, i ^ k) for i in range(4)])  9.5 us
    pallas_call x1, Pallas kernels, place(): pl.pallas_call(place_kernel, in_specs=[VMEM, HBM], out_specs=HBM, out_sha...  7.7 us
    all_to_all x4, waiting for transfers between devices, trade(): return lax.all_to_all(block, axis, split_axis=0, concat_axis=0)  5.92 us
    ppermute x1, starting transfers between devices, per_device(): row_far = lax.ppermute(row_send, 'zh', SWAP)  5.12 us
    unnamed x8, local copies, waits for them, and re-layouts  3.08 us
  transfers between devices with their start and end apart: 14, of which 6 were waited for; matrix products, arithmetic and copies ran while one was open for 0% of the time, Pallas kernels for 10%

profile of v9, /device:TPU:8, one launch (start us, length us, event | category | flops | bytes accessed | tf_op | source)
XLA Modules:
  0.0 113.0 jit_solution(14586834006539034004)
XLA Ops:
  0.0 0.0 copy-start.1
  0.0 0.7 copy-done.1
  0.7 0.0 copy-start.2
  0.7 0.7 copies.3
  1.4 12.1 %all-to-all-start.1 = ((bf16[6,48,256]{2,1,0:T(8,128)(2,1)}), bf16[6,48,256]{2,1,0:T(8,128)(2,1)S(1)}, u32[]{:S(2)}, u32[]{:S(2)}) async-start(bf16[6,48,256]{2,1,0:T(8,128)(2,1)} %copies.3), calls=%async_computation.1 | async-start | bytes 294912 | tf_op jit(solution)/shard_map/all_to_all | solution.py:320
  13.5 10.0 %collective-permute-start = (bf16[48,256]{1,0:T(8,128)(2,1)}, bf16[48,256]{1,0:T(8,128)(2,1)S(1)}, u32[]{:S(2)}, u32[]{:S(2)}) collective-permute-start(bf16[48,256]{1,0:T(8,128)(2,1)} %refs_0_.3), channel_id=1, source_target_pairs={{0,384},{384,0},{1,385},{385,1},{2,386},{386,2},{3,387},{387,3},{4... | collective-permute-start | bytes 73736 | tf_op jit(solution)/shard_map/ppermute | solution.py:324
  23.6 7.7 %place.1.x = bf16[1536,1536]{1,0:T(8,128)(2,1)} custom-call(s32[2,385]{1,0:T(2,128)} %bitcast.9, bf16[385,2304]{1,0:T(8,128)(2,1)} %bitcast.8), custom_call_target="tpu_custom_call" | custom-call | flops 2415919104 | bytes 8388608 | tf_op jit(solution)/shard_map/place/pallas_call | solution.py:89
  31.3 0.0 collective-permute-done.refs_1_
  31.3 0.0 copy-done.2
  31.3 0.8 copies.2
  32.1 0.0 all-to-all-done.1.block
  32.1 7.5 %all-to-all-start = ((bf16[8,96,256]{2,1,0:T(8,128)(2,1)}), bf16[8,96,256]{2,1,0:T(8,128)(2,1)S(1)}, u32[]{:S(2)}, u32[]{:S(2)}) async-start(bf16[8,96,256]{2,1,0:T(8,128)(2,1)} %copies.2), calls=%async_computation | async-start | bytes 786432 | tf_op jit(solution)/shard_map/all_to_all | solution.py:320
  39.6 3.4 %collective-permute-start.1 = (bf16[6,48,256]{2,1,0:T(8,128)(2,1)S(1)}, bf16[6,48,256]{2,1,0:T(8,128)(2,1)S(1)}, u32[]{:S(2)}, u32[]{:S(2)}) collective-permute-start(bf16[6,48,256]{2,1,0:T(8,128)(2,1)S(1)} %all-to-all-done.1.block), channel_id=1, source_target_pairs={{0,1},{1,0},{2,3},{3,2},{4,5},{5,4},{6,7},{7,6},{8,9},{9,8},{10,11... | collective-permute-start | bytes 442376 | tf_op jit(solution)/shard_map/ppermute | solution.py:316
  43.0 4.0 %collective-permute-start.3 = (bf16[6,48,256]{2,1,0:T(8,128)(2,1)S(1)}, bf16[6,48,256]{2,1,0:T(8,128)(2,1)S(1)}, u32[]{:S(2)}, u32[]{:S(2)}) collective-permute-start(bf16[6,48,256]{2,1,0:T(8,128)(2,1)S(1)} %all-to-all-done.1.block), channel_id=1, source_target_pairs={{0,3},{1,2},{2,1},{3,0},{4,7},{5,6},{6,5},{7,4},{8,11},{9,10},{10,... | collective-permute-start | bytes 442376 | tf_op jit(solution)/shard_map/ppermute | solution.py:316
  47.0 0.0 collective-permute-done.1.a1
  47.1 4.3 %collective-permute-start.2 = (bf16[6,48,256]{2,1,0:T(8,128)(2,1)S(1)}, bf16[6,48,256]{2,1,0:T(8,128)(2,1)S(1)}, u32[]{:S(2)}, u32[]{:S(2)}) collective-permute-start(bf16[6,48,256]{2,1,0:T(8,128)(2,1)S(1)} %collective-permute-done.1.a1), channel_id=1, source_target_pairs={{0,3},{1,2},{2,1},{3,0},{4,7},{5,6},{6,5},{7,4},{8,11},{9,10},{10,... | collective-permute-start | bytes 442376 | tf_op jit(solution)/shard_map/ppermute | solution.py:316
  51.3 0.3 collective-permute-done.3.a3
  51.6 3.7 %collective-permute-done.2.a2 = bf16[6,48,256]{2,1,0:T(8,128)(2,1)S(1)} collective-permute-done((bf16[6,48,256]{2,1,0:T(8,128)(2,1)S(1)}, bf16[6,48,256]{2,1,0:T(8,128)(2,1)S(1)}, u32[]{:S(2)}, u32[]{:S(2)}) %collective-permute-start.2) | collective-permute-done | bytes 147488 | tf_op jit(solution)/shard_map/ppermute | solution.py:316
  55.3 0.0 all-to-all-done
  55.3 1.9 %collective-permute-start.4 = (bf16[768,256]{1,0:T(8,128)(2,1)S(1)}, bf16[768,256]{1,0:T(8,128)(2,1)S(1)}, u32[]{:S(2)}, u32[]{:S(2)}) collective-permute-start(bf16[768,256]{1,0:T(8,128)(2,1)S(1)} %bitcast.5), channel_id=1, source_target_pairs={{0,24},{24,0},{1,25},{25,1},{2,26},{26,2},{3,27},{27,3},{4,28},{28... | collective-permute-start | bytes 1179656 | tf_op jit(solution)/shard_map/ppermute | solution.py:332
  57.2 0.0 copy-start
  57.2 2.3 %copy-done = bf16[1536,1536]{1,0:T(8,128)(2,1)S(1)} copy-done((bf16[1536,1536]{1,0:T(8,128)(2,1)S(1)}, bf16[1536,1536]{1,0:T(8,128)(2,1)}, u32[]{:S(2)}) %copy-start) | copy-done | bytes 4718616
  59.6 0.0 collective-permute-done.4.other_ref
  59.6 2.5 %mirror.1 = (f32[768,256]{1,0:T(8,128)S(1)}, f32[768,256]{1,0:T(8,128)S(1)}) custom-call(bf16[1536,1536]{1,0:T(8,128)(2,1)S(1)} %copy-done, bf16[6,48,256]{2,1,0:T(8,128)(2,1)S(1)} %meet.1.a0, bf16[6,48,256]{2,1,0:T(8,128)(2,1)S(1)} %collective-permute-done.1.a1, bf16[6,48,256]{2,1,0:T(8,128)(2,1)S(1)} %collective-permute-done.2.a2, ...), custom_call_target="tpu_custom_call" | custom-call | flops 1207959552 | bytes 8388608 | tf_op jit(solution)/shard_map/mirror/pallas_call | solution.py:166
  62.1 0.0 copy-start.3
  62.1 2.5 %collective-permute-start.5 = (f32[768,256]{1,0:T(8,128)S(1)}, f32[768,256]{1,0:T(8,128)S(1)}, u32[]{:S(2)}, u32[]{:S(2)}) collective-permute-start(f32[768,256]{1,0:T(8,128)S(1)} %get-tuple-element.39), channel_id=1, source_target_pairs={{0,24},{24,0},{1,25},{25,1},{2,26},{26,2},{3,27},{27,3},{4,28},{28... | collective-permute-start | bytes 2359304 | tf_op jit(solution)/shard_map/ppermute | solution.py:336
  64.7 2.1 %direct.1 = (f32[288,256]{1,0:T(8,128)S(1)}, s16[304,256]{1,0:T(8,128)(2,1)S(1)}, s16[304,256]{1,0:T(8,128)(2,1)S(1)}, s16[304,256]{1,0:T(8,128)(2,1)S(1)}) custom-call(bf16[1536,1536]{1,0:T(8,128)(2,1)S(1)} %copy-done, bf16[768,256]{1,0:T(8,128)(2,1)S(1)} %bitcast.7, bf16[768,256]{1,0:T(8,128)(2,1)S(1)} %collective-permute-done.4.other_ref), custom_call_target="tpu_custom_call" | custom-call | flops 1207959552 | bytes 8388608 | tf_op jit(solution)/shard_map/direct/pallas_call | solution.py:226
  66.7 0.0 collective-permute-done.5.got
  66.7 1.2 %code_y.1 = s16[8,112,256]{2,1,0:T(8,128)(2,1)} custom-call(f32[768,256]{1,0:T(8,128)S(1)} %get-tuple-element.38.keep, f32[768,256]{1,0:T(8,128)S(1)} %collective-permute-done.5.got), custom_call_target="tpu_custom_call" | custom-call | tf_op jit(solution)/shard_map/code_y/pallas_call | solution.py:253
  67.9 7.2 %all-to-all-start.2 = ((s16[8,112,256]{2,1,0:T(8,128)(2,1)}), s16[8,112,256]{2,1,0:T(8,128)(2,1)S(1)}, u32[]{:S(2)}, u32[]{:S(2)}) async-start(s16[8,112,256]{2,1,0:T(8,128)(2,1)} %code_y.1), calls=%async_computation.2 | async-start | bytes 917504 | tf_op jit(solution)/shard_map/all_to_all | solution.py:320
  75.2 1.9 %collective-permute-start.7 = (s16[304,256]{1,0:T(8,128)(2,1)S(1)}, s16[304,256]{1,0:T(8,128)(2,1)S(1)}, u32[]{:S(2)}, u32[]{:S(2)}) collective-permute-start(s16[304,256]{1,0:T(8,128)(2,1)S(1)} %get-tuple-element.54), channel_id=1, source_target_pairs={{0,1},{1,0},{2,3},{3,2},{4,5},{5,4},{6,7},{7,6},{8,9},{9,8},{10,11... | collective-permute-start | bytes 466952 | tf_op jit(solution)/shard_map/ppermute | solution.py:316
  77.1 5.7 %collective-permute-start.8 = (s16[304,256]{1,0:T(8,128)(2,1)S(1)}, s16[304,256]{1,0:T(8,128)(2,1)S(1)}, u32[]{:S(2)}, u32[]{:S(2)}) collective-permute-start(s16[304,256]{1,0:T(8,128)(2,1)S(1)} %get-tuple-element.55), channel_id=1, source_target_pairs={{0,2},{1,3},{2,0},{3,1},{4,6},{5,7},{6,4},{7,5},{8,10},{9,11},{10,... | collective-permute-start | bytes 466952 | tf_op jit(solution)/shard_map/ppermute | solution.py:316
  82.8 2.8 %collective-permute-start.9 = (s16[304,256]{1,0:T(8,128)(2,1)S(1)}, s16[304,256]{1,0:T(8,128)(2,1)S(1)}, u32[]{:S(2)}, u32[]{:S(2)}) collective-permute-start(s16[304,256]{1,0:T(8,128)(2,1)S(1)} %get-tuple-element.56), channel_id=1, source_target_pairs={{0,3},{1,2},{2,1},{3,0},{4,7},{5,6},{6,5},{7,4},{8,11},{9,10},{10,... | collective-permute-start | bytes 466952 | tf_op jit(solution)/shard_map/ppermute | solution.py:316
  85.6 0.0 collective-permute-done.7.c1
  85.6 2.1 %collective-permute-done.8.c2 = s16[304,256]{1,0:T(8,128)(2,1)S(1)} collective-permute-done((s16[304,256]{1,0:T(8,128)(2,1)S(1)}, s16[304,256]{1,0:T(8,128)(2,1)S(1)}, u32[]{:S(2)}, u32[]{:S(2)}) %collective-permute-start.8) | collective-permute-done | bytes 155680 | tf_op jit(solution)/shard_map/ppermute | solution.py:316
  87.7 3.4 %collective-permute-done.9.c3 = s16[304,256]{1,0:T(8,128)(2,1)S(1)} collective-permute-done((s16[304,256]{1,0:T(8,128)(2,1)S(1)}, s16[304,256]{1,0:T(8,128)(2,1)S(1)}, u32[]{:S(2)}, u32[]{:S(2)}) %collective-permute-start.9) | collective-permute-done | bytes 155680 | tf_op jit(solution)/shard_map/ppermute | solution.py:316
  91.1 0.9 sum_x.1
  92.0 0.0 all-to-all-done.2.coded
  92.0 7.5 %all-to-all-start.3 = ((s16[6,64,256]{2,1,0:T(8,128)(2,1)}), s16[6,64,256]{2,1,0:T(8,128)(2,1)S(1)}, u32[]{:S(2)}, u32[]{:S(2)}) async-start(s16[6,64,256]{2,1,0:T(8,128)(2,1)} %sum_x.1), calls=%async_computation.3 | async-start | bytes 393216 | tf_op jit(solution)/shard_map/all_to_all | solution.py:320
  99.5 0.1 sum_y.1
  99.7 5.1 %collective-permute-start.6 = (s16[64,256]{1,0:T(8,128)(2,1)S(1)}, s16[64,256]{1,0:T(8,128)(2,1)S(1)}, u32[]{:S(2)}, u32[]{:S(2)}) collective-permute-start(s16[64,256]{1,0:T(8,128)(2,1)S(1)} %get-tuple-element.52), channel_id=1, source_target_pairs={{0,384},{384,0},{1,385},{385,1},{2,386},{386,2},{3,387},{387,3},{4... | collective-permute-start | bytes 98312 | tf_op jit(solution)/shard_map/ppermute | solution.py:347
  104.8 5.9 %all-to-all-done.3.coded = s16[6,64,256]{2,1,0:T(8,128)(2,1)S(1)} async-done(((s16[6,64,256]{2,1,0:T(8,128)(2,1)}), s16[6,64,256]{2,1,0:T(8,128)(2,1)S(1)}, u32[]{:S(2)}, u32[]{:S(2)}) %all-to-all-start.3) | async-done | bytes 196640 | tf_op jit(solution)/shard_map/all_to_all | solution.py:320
  110.7 1.6 %collective-permute-done.6.far = s16[64,256]{1,0:T(8,128)(2,1)S(1)} collective-permute-done((s16[64,256]{1,0:T(8,128)(2,1)S(1)}, s16[64,256]{1,0:T(8,128)(2,1)S(1)}, u32[]{:S(2)}, u32[]{:S(2)}) %collective-permute-start.6) | collective-permute-done | bytes 32800 | tf_op jit(solution)/shard_map/ppermute | solution.py:347
  112.4 0.0 copy-done.3
  112.4 0.7 end.1
  (1 shorter events, 0.0 us)
Async XLA Ops:
  0.0 0.7 copy-start.1
  0.7 30.5 %copy-start.2 = (bf16[48,256]{1,0:T(8,128)(2,1)S(1)}, bf16[48,256]{1,0:T(8,128)(2,1)}, u32[]{:S(2)}) copy-start(bf16[48,256]{1,0:T(8,128)(2,1)} %refs_0_.3) | copy-start | bytes 73732
  1.4 30.6 %all-to-all-start.1 = ((bf16[6,48,256]{2,1,0:T(8,128)(2,1)}), bf16[6,48,256]{2,1,0:T(8,128)(2,1)S(1)}, u32[]{:S(2)}, u32[]{:S(2)}) async-start(bf16[6,48,256]{2,1,0:T(8,128)(2,1)} %copies.3), calls=%async_computation.1 | async-start | bytes 294912 | tf_op jit(solution)/shard_map/all_to_all | solution.py:320
  13.5 17.7 %collective-permute-start = (bf16[48,256]{1,0:T(8,128)(2,1)}, bf16[48,256]{1,0:T(8,128)(2,1)S(1)}, u32[]{:S(2)}, u32[]{:S(2)}) collective-permute-start(bf16[48,256]{1,0:T(8,128)(2,1)} %refs_0_.3), channel_id=1, source_target_pairs={{0,384},{384,0},{1,385},{385,1},{2,386},{386,2},{3,387},{387,3},{4... | collective-permute-start | bytes 73736 | tf_op jit(solution)/shard_map/ppermute | solution.py:324
  32.1 23.2 %all-to-all-start = ((bf16[8,96,256]{2,1,0:T(8,128)(2,1)}), bf16[8,96,256]{2,1,0:T(8,128)(2,1)S(1)}, u32[]{:S(2)}, u32[]{:S(2)}) async-start(bf16[8,96,256]{2,1,0:T(8,128)(2,1)} %copies.2), calls=%async_computation | async-start | bytes 786432 | tf_op jit(solution)/shard_map/all_to_all | solution.py:320
  39.6 7.4 %collective-permute-start.1 = (bf16[6,48,256]{2,1,0:T(8,128)(2,1)S(1)}, bf16[6,48,256]{2,1,0:T(8,128)(2,1)S(1)}, u32[]{:S(2)}, u32[]{:S(2)}) collective-permute-start(bf16[6,48,256]{2,1,0:T(8,128)(2,1)S(1)} %all-to-all-done.1.block), channel_id=1, source_target_pairs={{0,1},{1,0},{2,3},{3,2},{4,5},{5,4},{6,7},{7,6},{8,9},{9,8},{10,11... | collective-permute-start | bytes 442376 | tf_op jit(solution)/shard_map/ppermute | solution.py:316
  43.0 8.6 %collective-permute-start.3 = (bf16[6,48,256]{2,1,0:T(8,128)(2,1)S(1)}, bf16[6,48,256]{2,1,0:T(8,128)(2,1)S(1)}, u32[]{:S(2)}, u32[]{:S(2)}) collective-permute-start(bf16[6,48,256]{2,1,0:T(8,128)(2,1)S(1)} %all-to-all-done.1.block), channel_id=1, source_target_pairs={{0,3},{1,2},{2,1},{3,0},{4,7},{5,6},{6,5},{7,4},{8,11},{9,10},{10,... | collective-permute-start | bytes 442376 | tf_op jit(solution)/shard_map/ppermute | solution.py:316
  47.1 8.2 %collective-permute-start.2 = (bf16[6,48,256]{2,1,0:T(8,128)(2,1)S(1)}, bf16[6,48,256]{2,1,0:T(8,128)(2,1)S(1)}, u32[]{:S(2)}, u32[]{:S(2)}) collective-permute-start(bf16[6,48,256]{2,1,0:T(8,128)(2,1)S(1)} %collective-permute-done.1.a1), channel_id=1, source_target_pairs={{0,3},{1,2},{2,1},{3,0},{4,7},{5,6},{6,5},{7,4},{8,11},{9,10},{10,... | collective-permute-start | bytes 442376 | tf_op jit(solution)/shard_map/ppermute | solution.py:316
  55.3 4.3 %collective-permute-start.4 = (bf16[768,256]{1,0:T(8,128)(2,1)S(1)}, bf16[768,256]{1,0:T(8,128)(2,1)S(1)}, u32[]{:S(2)}, u32[]{:S(2)}) collective-permute-start(bf16[768,256]{1,0:T(8,128)(2,1)S(1)} %bitcast.5), channel_id=1, source_target_pairs={{0,24},{24,0},{1,25},{25,1},{2,26},{26,2},{3,27},{27,3},{4,28},{28... | collective-permute-start | bytes 1179656 | tf_op jit(solution)/shard_map/ppermute | solution.py:332
  57.2 2.3 %copy-start = (bf16[1536,1536]{1,0:T(8,128)(2,1)S(1)}, bf16[1536,1536]{1,0:T(8,128)(2,1)}, u32[]{:S(2)}) copy-start(bf16[1536,1536]{1,0:T(8,128)(2,1)} %place.1.x) | copy-start | bytes 14155780
  62.1 50.3 %copy-start.3 = (f32[48,256]{1,0:T(8,128)S(1)}, f32[48,256]{1,0:T(8,128)}, u32[]{:S(2)}) copy-start(f32[48,256]{1,0:T(8,128)} %residual.1) | copy-start | bytes 147460
  62.1 4.6 %collective-permute-start.5 = (f32[768,256]{1,0:T(8,128)S(1)}, f32[768,256]{1,0:T(8,128)S(1)}, u32[]{:S(2)}, u32[]{:S(2)}) collective-permute-start(f32[768,256]{1,0:T(8,128)S(1)} %get-tuple-element.39), channel_id=1, source_target_pairs={{0,24},{24,0},{1,25},{25,1},{2,26},{26,2},{3,27},{27,3},{4,28},{28... | collective-permute-start | bytes 2359304 | tf_op jit(solution)/shard_map/ppermute | solution.py:336
  67.9 24.1 %all-to-all-start.2 = ((s16[8,112,256]{2,1,0:T(8,128)(2,1)}), s16[8,112,256]{2,1,0:T(8,128)(2,1)S(1)}, u32[]{:S(2)}, u32[]{:S(2)}) async-start(s16[8,112,256]{2,1,0:T(8,128)(2,1)} %code_y.1), calls=%async_computation.2 | async-start | bytes 917504 | tf_op jit(solution)/shard_map/all_to_all | solution.py:320
  75.2 10.4 %collective-permute-start.7 = (s16[304,256]{1,0:T(8,128)(2,1)S(1)}, s16[304,256]{1,0:T(8,128)(2,1)S(1)}, u32[]{:S(2)}, u32[]{:S(2)}) collective-permute-start(s16[304,256]{1,0:T(8,128)(2,1)S(1)} %get-tuple-element.54), channel_id=1, source_target_pairs={{0,1},{1,0},{2,3},{3,2},{4,5},{5,4},{6,7},{7,6},{8,9},{9,8},{10,11... | collective-permute-start | bytes 466952 | tf_op jit(solution)/shard_map/ppermute | solution.py:316
  77.1 10.7 %collective-permute-start.8 = (s16[304,256]{1,0:T(8,128)(2,1)S(1)}, s16[304,256]{1,0:T(8,128)(2,1)S(1)}, u32[]{:S(2)}, u32[]{:S(2)}) collective-permute-start(s16[304,256]{1,0:T(8,128)(2,1)S(1)} %get-tuple-element.55), channel_id=1, source_target_pairs={{0,2},{1,3},{2,0},{3,1},{4,6},{5,7},{6,4},{7,5},{8,10},{9,11},{10,... | collective-permute-start | bytes 466952 | tf_op jit(solution)/shard_map/ppermute | solution.py:316
  82.8 8.3 %collective-permute-start.9 = (s16[304,256]{1,0:T(8,128)(2,1)S(1)}, s16[304,256]{1,0:T(8,128)(2,1)S(1)}, u32[]{:S(2)}, u32[]{:S(2)}) collective-permute-start(s16[304,256]{1,0:T(8,128)(2,1)S(1)} %get-tuple-element.56), channel_id=1, source_target_pairs={{0,3},{1,2},{2,1},{3,0},{4,7},{5,6},{6,5},{7,4},{8,11},{9,10},{10,... | collective-permute-start | bytes 466952 | tf_op jit(solution)/shard_map/ppermute | solution.py:316
  92.0 18.7 %all-to-all-start.3 = ((s16[6,64,256]{2,1,0:T(8,128)(2,1)}), s16[6,64,256]{2,1,0:T(8,128)(2,1)S(1)}, u32[]{:S(2)}, u32[]{:S(2)}) async-start(s16[6,64,256]{2,1,0:T(8,128)(2,1)} %sum_x.1), calls=%async_computation.3 | async-start | bytes 393216 | tf_op jit(solution)/shard_map/all_to_all | solution.py:320
  99.7 12.7 %collective-permute-start.6 = (s16[64,256]{1,0:T(8,128)(2,1)S(1)}, s16[64,256]{1,0:T(8,128)(2,1)S(1)}, u32[]{:S(2)}, u32[]{:S(2)}) collective-permute-start(s16[64,256]{1,0:T(8,128)(2,1)S(1)} %get-tuple-element.52), channel_id=1, source_target_pairs={{0,384},{384,0},{1,385},{385,1},{2,386},{386,2},{3,387},{387,3},{4... | collective-permute-start | bytes 98312 | tf_op jit(solution)/shard_map/ppermute | solution.py:347

commit v10 on v5

--- a/solution.py
+++ b/solution.py
@@ -322,9 +322,9 @@
     x = place(tile_map[0, 0].T, v_tiles[0, 0])
     x, far = lax.optimization_barrier((x, far))
     own = trade(copies(8, (), amplitudes, far), "y").reshape(HALF, PAIRS)
-    quarters = [swap_x(line, k) for k in (1, 2, 3)]
+    far_line, left, right = (swap_x(line, k) for k in (2, 1, 3))
     near = meet(own, x, line)
-    quarters = [near] + quarters
+    quarters = [near, left, far_line, right]
 
     other = lax.ppermute(own, "co", SWAP)
     keep, send = mirror(x, *quarters)
@@ -335,7 +335,7 @@
     coded_y, *parts = lax.optimization_barrier((coded_y, *parts))
     row_parts = trade(coded_y, "y")
 
-    col_line = sum_x(parts[0], *(swap_x(parts[k], k) for k in (1, 2, 3)))
+    col_line = sum_x(parts[0], *(swap_x(parts[k], k) for k in (2, 1, 3)))
     col_line = trade(col_line, "zl")
 
     row_near, row_send = sum_y(row_parts)

time: 112 us -> 112 us (level)
    ppermute x6, waiting for transfers between devices: 6.26 us -> 3.74 us  [swap_x(): return lax.ppermute(block, 'x', [(i, i ^ k) for i in range(4)])]
    all_to_all x4, waiting for transfers between devices: 13.6 us -> 15.5 us  [trade(): return lax.all_to_all(block, axis, split_axis=0, concat_axis=0)]
  transfers between devices with their start and end apart: 14 -> 14, of which waited for: 6 -> 7; matrix products, arithmetic and copies ran while one was open for 0% -> 0% of each run, Pallas kernels for 10% -> 10%
where the time goes in v10:
time: 112 us; the launch traced here: 111 us
  starting transfers between devices  70.7 us (63%)
  waiting for transfers between devices  20.6 us (18%)
  Pallas kernels  16.7 us (15%)
  local copies, waits for them, and re-layouts  3.08 us (3%)
    all_to_all x4, starting transfers between devices, trade(): return lax.all_to_all(block, axis, split_axis=0, concat_axis=0)  31.6 us
    ppermute x6, starting transfers between devices, swap_x(): return lax.ppermute(block, 'x', [(i, i ^ k) for i in range(4)])  19.6 us
    all_to_all x4, waiting for transfers between devices, trade(): return lax.all_to_all(block, axis, split_axis=0, concat_axis=0)  15.5 us
    ppermute x1, starting transfers between devices, per_device(): far = lax.ppermute(amplitudes, 'zh', SWAP)  10 us
    pallas_call x1, Pallas kernels, place(): pl.pallas_call(place_kernel, in_specs=[VMEM, HBM], out_specs=HBM, out_sha...  7.7 us
    ppermute x1, starting transfers between devices, per_device(): row_far = lax.ppermute(row_send, 'zh', SWAP)  5.07 us
    ppermute x6, waiting for transfers between devices, swap_x(): return lax.ppermute(block, 'x', [(i, i ^ k) for i in range(4)])  3.74 us
    unnamed x8, local copies, waits for them, and re-layouts  3.08 us
  transfers between devices with their start and end apart: 14, of which 7 were waited for; matrix products, arithmetic and copies ran while one was open for 0% of the time, Pallas kernels for 10%

profile of v10, /device:TPU:4, one launch (start us, length us, event | category | flops | bytes accessed | tf_op | source)
XLA Modules:
  0.0 111.2 jit_solution(8393783489501054923)
XLA Ops:
  0.0 0.0 copy-start.1
  0.0 0.7 copy-done.1
  0.7 0.0 copy-start.2
  0.7 0.7 copies.3
  1.4 12.1 %all-to-all-start.1 = ((bf16[6,48,256]{2,1,0:T(8,128)(2,1)}), bf16[6,48,256]{2,1,0:T(8,128)(2,1)S(1)}, u32[]{:S(2)}, u32[]{:S(2)}) async-start(bf16[6,48,256]{2,1,0:T(8,128)(2,1)} %copies.3), calls=%async_computation.1 | async-start | bytes 294912 | tf_op jit(solution)/shard_map/all_to_all | solution.py:316
  13.5 10.0 %collective-permute-start = (bf16[48,256]{1,0:T(8,128)(2,1)}, bf16[48,256]{1,0:T(8,128)(2,1)S(1)}, u32[]{:S(2)}, u32[]{:S(2)}) collective-permute-start(bf16[48,256]{1,0:T(8,128)(2,1)} %refs_0_.3), channel_id=1, source_target_pairs={{0,384},{384,0},{1,385},{385,1},{2,386},{386,2},{3,387},{387,3},{4... | collective-permute-start | bytes 73736 | tf_op jit(solution)/shard_map/ppermute | solution.py:320
  23.6 7.7 %place.1.x = bf16[1536,1536]{1,0:T(8,128)(2,1)} custom-call(s32[2,385]{1,0:T(2,128)} %bitcast.9, bf16[385,2304]{1,0:T(8,128)(2,1)} %bitcast.8), custom_call_target="tpu_custom_call" | custom-call | flops 2415919104 | bytes 8388608 | tf_op jit(solution)/shard_map/place/pallas_call | solution.py:89
  31.3 0.0 collective-permute-done.refs_1_
  31.3 0.0 copy-done.2
  31.3 0.8 copies.2
  32.1 0.0 all-to-all-done.1.block
  32.1 7.1 %all-to-all-start = ((bf16[8,96,256]{2,1,0:T(8,128)(2,1)}), bf16[8,96,256]{2,1,0:T(8,128)(2,1)S(1)}, u32[]{:S(2)}, u32[]{:S(2)}) async-start(bf16[8,96,256]{2,1,0:T(8,128)(2,1)} %copies.2), calls=%async_computation | async-start | bytes 786432 | tf_op jit(solution)/shard_map/all_to_all | solution.py:316
  39.2 2.4 %collective-permute-start.3 = (bf16[6,48,256]{2,1,0:T(8,128)(2,1)S(1)}, bf16[6,48,256]{2,1,0:T(8,128)(2,1)S(1)}, u32[]{:S(2)}, u32[]{:S(2)}) collective-permute-start(bf16[6,48,256]{2,1,0:T(8,128)(2,1)S(1)} %all-to-all-done.1.block), channel_id=1, source_target_pairs={{0,3},{1,2},{2,1},{3,0},{4,7},{5,6},{6,5},{7,4},{8,11},{9,10},{10,... | collective-permute-start | bytes 442376 | tf_op jit(solution)/shard_map/ppermute | solution.py:312
  41.6 4.6 %collective-permute-start.2 = (bf16[6,48,256]{2,1,0:T(8,128)(2,1)S(1)}, bf16[6,48,256]{2,1,0:T(8,128)(2,1)S(1)}, u32[]{:S(2)}, u32[]{:S(2)}) collective-permute-start(bf16[6,48,256]{2,1,0:T(8,128)(2,1)S(1)} %all-to-all-done.1.block), channel_id=1, source_target_pairs={{0,2},{1,3},{2,0},{3,1},{4,6},{5,7},{6,4},{7,5},{8,10},{9,11},{10,... | collective-permute-start | bytes 442376 | tf_op jit(solution)/shard_map/ppermute | solution.py:312
  46.3 2.7 %collective-permute-start.1 = (bf16[6,48,256]{2,1,0:T(8,128)(2,1)S(1)}, bf16[6,48,256]{2,1,0:T(8,128)(2,1)S(1)}, u32[]{:S(2)}, u32[]{:S(2)}) collective-permute-start(bf16[6,48,256]{2,1,0:T(8,128)(2,1)S(1)} %all-to-all-done.1.block), channel_id=1, source_target_pairs={{0,1},{1,0},{2,3},{3,2},{4,5},{5,4},{6,7},{7,6},{8,9},{9,8},{10,11... | collective-permute-start | bytes 442376 | tf_op jit(solution)/shard_map/ppermute | solution.py:312
  49.0 4.3 %all-to-all-done = bf16[8,96,256]{2,1,0:T(8,128)(2,1)S(1)} async-done(((bf16[8,96,256]{2,1,0:T(8,128)(2,1)}), bf16[8,96,256]{2,1,0:T(8,128)(2,1)S(1)}, u32[]{:S(2)}, u32[]{:S(2)}) %all-to-all-start) | async-done | bytes 393248 | tf_op jit(solution)/shard_map/all_to_all | solution.py:316
  53.3 0.0 copy-start
  53.3 2.3 %copy-done = bf16[1536,1536]{1,0:T(8,128)(2,1)S(1)} copy-done((bf16[1536,1536]{1,0:T(8,128)(2,1)S(1)}, bf16[1536,1536]{1,0:T(8,128)(2,1)}, u32[]{:S(2)}) %copy-start) | copy-done | bytes 4718616
  55.7 0.0 collective-permute-done.3.a3
  55.7 0.0 collective-permute-done.2.a2
  55.7 0.0 collective-permute-done.1.a1
  55.7 2.5 %mirror.1 = (f32[768,256]{1,0:T(8,128)S(1)}, f32[768,256]{1,0:T(8,128)S(1)}) custom-call(bf16[1536,1536]{1,0:T(8,128)(2,1)S(1)} %copy-done, bf16[6,48,256]{2,1,0:T(8,128)(2,1)S(1)} %meet.1.a0, bf16[6,48,256]{2,1,0:T(8,128)(2,1)S(1)} %collective-permute-done.1.a1, bf16[6,48,256]{2,1,0:T(8,128)(2,1)S(1)} %collective-permute-done.2.a2, ...), custom_call_target="tpu_custom_call" | custom-call | flops 1207959552 | bytes 8388608 | tf_op jit(solution)/shard_map/mirror/pallas_call | solution.py:166
  58.2 0.0 copy-start.3
  58.2 2.1 %collective-permute-start.4 = (f32[768,256]{1,0:T(8,128)S(1)}, f32[768,256]{1,0:T(8,128)S(1)}, u32[]{:S(2)}, u32[]{:S(2)}) collective-permute-start(f32[768,256]{1,0:T(8,128)S(1)} %get-tuple-element.28), channel_id=1, source_target_pairs={{0,24},{24,0},{1,25},{25,1},{2,26},{26,2},{3,27},{27,3},{4,28},{28... | collective-permute-start | bytes 2359304 | tf_op jit(solution)/shard_map/ppermute | solution.py:331
  60.3 2.4 %collective-permute-start.5 = (bf16[768,256]{1,0:T(8,128)(2,1)S(1)}, bf16[768,256]{1,0:T(8,128)(2,1)S(1)}, u32[]{:S(2)}, u32[]{:S(2)}) collective-permute-start(bf16[768,256]{1,0:T(8,128)(2,1)S(1)} %bitcast.6), channel_id=1, source_target_pairs={{0,24},{24,0},{1,25},{25,1},{2,26},{26,2},{3,27},{27,3},{4,28},{28... | collective-permute-start | bytes 1179656 | tf_op jit(solution)/shard_map/ppermute | solution.py:329
  62.7 1.3 %collective-permute-done.5.other_ref = bf16[768,256]{1,0:T(8,128)(2,1)S(1)} collective-permute-done((bf16[768,256]{1,0:T(8,128)(2,1)S(1)}, bf16[768,256]{1,0:T(8,128)(2,1)S(1)}, u32[]{:S(2)}, u32[]{:S(2)}) %collective-permute-start.5) | collective-permute-done | bytes 393248 | tf_op jit(solution)/shard_map/ppermute | solution.py:329
  64.0 2.1 %direct.1 = (f32[288,256]{1,0:T(8,128)S(1)}, s16[304,256]{1,0:T(8,128)(2,1)S(1)}, s16[304,256]{1,0:T(8,128)(2,1)S(1)}, s16[304,256]{1,0:T(8,128)(2,1)S(1)}) custom-call(bf16[1536,1536]{1,0:T(8,128)(2,1)S(1)} %copy-done, bf16[768,256]{1,0:T(8,128)(2,1)S(1)} %bitcast.7, bf16[768,256]{1,0:T(8,128)(2,1)S(1)} %collective-permute-done.5.other_ref), custom_call_target="tpu_custom_call" | custom-call | flops 1207959552 | bytes 8388608 | tf_op jit(solution)/shard_map/direct/pallas_call | solution.py:226
  66.1 0.0 collective-permute-done.4.got
  66.1 1.2 %code_y.1 = s16[8,112,256]{2,1,0:T(8,128)(2,1)} custom-call(f32[768,256]{1,0:T(8,128)S(1)} %get-tuple-element.27.keep, f32[768,256]{1,0:T(8,128)S(1)} %collective-permute-done.4.got), custom_call_target="tpu_custom_call" | custom-call | tf_op jit(solution)/shard_map/code_y/pallas_call | solution.py:253
  67.3 4.9 %all-to-all-start.2 = ((s16[8,112,256]{2,1,0:T(8,128)(2,1)}), s16[8,112,256]{2,1,0:T(8,128)(2,1)S(1)}, u32[]{:S(2)}, u32[]{:S(2)}) async-start(s16[8,112,256]{2,1,0:T(8,128)(2,1)} %code_y.1), calls=%async_computation.2 | async-start | bytes 917504 | tf_op jit(solution)/shard_map/all_to_all | solution.py:316
  72.2 2.9 %collective-permute-start.7 = (s16[304,256]{1,0:T(8,128)(2,1)S(1)}, s16[304,256]{1,0:T(8,128)(2,1)S(1)}, u32[]{:S(2)}, u32[]{:S(2)}) collective-permute-start(s16[304,256]{1,0:T(8,128)(2,1)S(1)} %get-tuple-element.42), channel_id=1, source_target_pairs={{0,2},{1,3},{2,0},{3,1},{4,6},{5,7},{6,4},{7,5},{8,10},{9,11},{10,... | collective-permute-start | bytes 466952 | tf_op jit(solution)/shard_map/ppermute | solution.py:312
  75.2 3.1 %collective-permute-start.8 = (s16[304,256]{1,0:T(8,128)(2,1)S(1)}, s16[304,256]{1,0:T(8,128)(2,1)S(1)}, u32[]{:S(2)}, u32[]{:S(2)}) collective-permute-start(s16[304,256]{1,0:T(8,128)(2,1)S(1)} %get-tuple-element.43), channel_id=1, source_target_pairs={{0,1},{1,0},{2,3},{3,2},{4,5},{5,4},{6,7},{7,6},{8,9},{9,8},{10,11... | collective-permute-start | bytes 466952 | tf_op jit(solution)/shard_map/ppermute | solution.py:312
  78.3 3.8 %collective-permute-start.9 = (s16[304,256]{1,0:T(8,128)(2,1)S(1)}, s16[304,256]{1,0:T(8,128)(2,1)S(1)}, u32[]{:S(2)}, u32[]{:S(2)}) collective-permute-start(s16[304,256]{1,0:T(8,128)(2,1)S(1)} %get-tuple-element.44), channel_id=1, source_target_pairs={{0,3},{1,2},{2,1},{3,0},{4,7},{5,6},{6,5},{7,4},{8,11},{9,10},{10,... | collective-permute-start | bytes 466952 | tf_op jit(solution)/shard_map/ppermute | solution.py:312
  82.0 0.4 collective-permute-done.7.c1
  82.5 1.2 %collective-permute-done.8.c2 = s16[304,256]{1,0:T(8,128)(2,1)S(1)} collective-permute-done((s16[304,256]{1,0:T(8,128)(2,1)S(1)}, s16[304,256]{1,0:T(8,128)(2,1)S(1)}, u32[]{:S(2)}, u32[]{:S(2)}) %collective-permute-start.8) | collective-permute-done | bytes 155680 | tf_op jit(solution)/shard_map/ppermute | solution.py:312
  83.6 2.1 %collective-permute-done.9.c3 = s16[304,256]{1,0:T(8,128)(2,1)S(1)} collective-permute-done((s16[304,256]{1,0:T(8,128)(2,1)S(1)}, s16[304,256]{1,0:T(8,128)(2,1)S(1)}, u32[]{:S(2)}, u32[]{:S(2)}) %collective-permute-start.9) | collective-permute-done | bytes 155680 | tf_op jit(solution)/shard_map/ppermute | solution.py:312
  85.8 0.9 sum_x.1
  86.7 2.1 %all-to-all-done.2.coded = s16[8,112,256]{2,1,0:T(8,128)(2,1)S(1)} async-done(((s16[8,112,256]{2,1,0:T(8,128)(2,1)}), s16[8,112,256]{2,1,0:T(8,128)(2,1)S(1)}, u32[]{:S(2)}, u32[]{:S(2)}) %all-to-all-start.2) | async-done | bytes 458784 | tf_op jit(solution)/shard_map/all_to_all | solution.py:316
  88.8 7.5 %all-to-all-start.3 = ((s16[6,64,256]{2,1,0:T(8,128)(2,1)}), s16[6,64,256]{2,1,0:T(8,128)(2,1)S(1)}, u32[]{:S(2)}, u32[]{:S(2)}) async-start(s16[6,64,256]{2,1,0:T(8,128)(2,1)} %sum_x.1), calls=%async_computation.3 | async-start | bytes 393216 | tf_op jit(solution)/shard_map/all_to_all | solution.py:316
  96.3 0.1 sum_y.1
  96.4 5.1 %collective-permute-start.6 = (f32[48,256]{1,0:T(8,128)S(1)}, f32[48,256]{1,0:T(8,128)S(1)}, u32[]{:S(2)}, u32[]{:S(2)}) collective-permute-start(f32[48,256]{1,0:T(8,128)S(1)} %get-tuple-element.40), channel_id=1, source_target_pairs={{0,384},{384,0},{1,385},{385,1},{2,386},{386,2},{3,387},{387,3},{4... | collective-permute-start | bytes 147464 | tf_op jit(solution)/shard_map/ppermute | solution.py:342
  101.5 9.1 %all-to-all-done.3.coded = s16[6,64,256]{2,1,0:T(8,128)(2,1)S(1)} async-done(((s16[6,64,256]{2,1,0:T(8,128)(2,1)}), s16[6,64,256]{2,1,0:T(8,128)(2,1)S(1)}, u32[]{:S(2)}, u32[]{:S(2)}) %all-to-all-start.3) | async-done | bytes 196640 | tf_op jit(solution)/shard_map/all_to_all | solution.py:316
  110.6 0.0 collective-permute-done.6.far
  110.6 0.0 copy-done.3
  110.6 0.7 end.1
  (1 shorter events, 0.0 us)
Async XLA Ops:
  0.0 0.7 copy-start.1
  0.7 30.5 %copy-start.2 = (bf16[48,256]{1,0:T(8,128)(2,1)S(1)}, bf16[48,256]{1,0:T(8,128)(2,1)}, u32[]{:S(2)}) copy-start(bf16[48,256]{1,0:T(8,128)(2,1)} %refs_0_.3) | copy-start | bytes 73732
  1.4 30.6 %all-to-all-start.1 = ((bf16[6,48,256]{2,1,0:T(8,128)(2,1)}), bf16[6,48,256]{2,1,0:T(8,128)(2,1)S(1)}, u32[]{:S(2)}, u32[]{:S(2)}) async-start(bf16[6,48,256]{2,1,0:T(8,128)(2,1)} %copies.3), calls=%async_computation.1 | async-start | bytes 294912 | tf_op jit(solution)/shard_map/all_to_all | solution.py:316
  13.5 17.7 %collective-permute-start = (bf16[48,256]{1,0:T(8,128)(2,1)}, bf16[48,256]{1,0:T(8,128)(2,1)S(1)}, u32[]{:S(2)}, u32[]{:S(2)}) collective-permute-start(bf16[48,256]{1,0:T(8,128)(2,1)} %refs_0_.3), channel_id=1, source_target_pairs={{0,384},{384,0},{1,385},{385,1},{2,386},{386,2},{3,387},{387,3},{4... | collective-permute-start | bytes 73736 | tf_op jit(solution)/shard_map/ppermute | solution.py:320
  32.1 21.2 %all-to-all-start = ((bf16[8,96,256]{2,1,0:T(8,128)(2,1)}), bf16[8,96,256]{2,1,0:T(8,128)(2,1)S(1)}, u32[]{:S(2)}, u32[]{:S(2)}) async-start(bf16[8,96,256]{2,1,0:T(8,128)(2,1)} %copies.2), calls=%async_computation | async-start | bytes 786432 | tf_op jit(solution)/shard_map/all_to_all | solution.py:316
  39.2 16.5 %collective-permute-start.3 = (bf16[6,48,256]{2,1,0:T(8,128)(2,1)S(1)}, bf16[6,48,256]{2,1,0:T(8,128)(2,1)S(1)}, u32[]{:S(2)}, u32[]{:S(2)}) collective-permute-start(bf16[6,48,256]{2,1,0:T(8,128)(2,1)S(1)} %all-to-all-done.1.block), channel_id=1, source_target_pairs={{0,3},{1,2},{2,1},{3,0},{4,7},{5,6},{6,5},{7,4},{8,11},{9,10},{10,... | collective-permute-start | bytes 442376 | tf_op jit(solution)/shard_map/ppermute | solution.py:312
  41.6 14.1 %collective-permute-start.2 = (bf16[6,48,256]{2,1,0:T(8,128)(2,1)S(1)}, bf16[6,48,256]{2,1,0:T(8,128)(2,1)S(1)}, u32[]{:S(2)}, u32[]{:S(2)}) collective-permute-start(bf16[6,48,256]{2,1,0:T(8,128)(2,1)S(1)} %all-to-all-done.1.block), channel_id=1, source_target_pairs={{0,2},{1,3},{2,0},{3,1},{4,6},{5,7},{6,4},{7,5},{8,10},{9,11},{10,... | collective-permute-start | bytes 442376 | tf_op jit(solution)/shard_map/ppermute | solution.py:312
  46.3 9.4 %collective-permute-start.1 = (bf16[6,48,256]{2,1,0:T(8,128)(2,1)S(1)}, bf16[6,48,256]{2,1,0:T(8,128)(2,1)S(1)}, u32[]{:S(2)}, u32[]{:S(2)}) collective-permute-start(bf16[6,48,256]{2,1,0:T(8,128)(2,1)S(1)} %all-to-all-done.1.block), channel_id=1, source_target_pairs={{0,1},{1,0},{2,3},{3,2},{4,5},{5,4},{6,7},{7,6},{8,9},{9,8},{10,11... | collective-permute-start | bytes 442376 | tf_op jit(solution)/shard_map/ppermute | solution.py:312
  53.3 2.3 %copy-start = (bf16[1536,1536]{1,0:T(8,128)(2,1)S(1)}, bf16[1536,1536]{1,0:T(8,128)(2,1)}, u32[]{:S(2)}) copy-start(bf16[1536,1536]{1,0:T(8,128)(2,1)} %place.1.x) | copy-start | bytes 14155780
  58.2 52.4 %copy-start.3 = (f32[48,256]{1,0:T(8,128)S(1)}, f32[48,256]{1,0:T(8,128)}, u32[]{:S(2)}) copy-start(f32[48,256]{1,0:T(8,128)} %residual.1) | copy-start | bytes 147460
  58.2 7.9 %collective-permute-start.4 = (f32[768,256]{1,0:T(8,128)S(1)}, f32[768,256]{1,0:T(8,128)S(1)}, u32[]{:S(2)}, u32[]{:S(2)}) collective-permute-start(f32[768,256]{1,0:T(8,128)S(1)} %get-tuple-element.28), channel_id=1, source_target_pairs={{0,24},{24,0},{1,25},{25,1},{2,26},{26,2},{3,27},{27,3},{4,28},{28... | collective-permute-start | bytes 2359304 | tf_op jit(solution)/shard_map/ppermute | solution.py:331
  60.3 3.7 %collective-permute-start.5 = (bf16[768,256]{1,0:T(8,128)(2,1)S(1)}, bf16[768,256]{1,0:T(8,128)(2,1)S(1)}, u32[]{:S(2)}, u32[]{:S(2)}) collective-permute-start(bf16[768,256]{1,0:T(8,128)(2,1)S(1)} %bitcast.6), channel_id=1, source_target_pairs={{0,24},{24,0},{1,25},{25,1},{2,26},{26,2},{3,27},{27,3},{4,28},{28... | collective-permute-start | bytes 1179656 | tf_op jit(solution)/shard_map/ppermute | solution.py:329
  67.3 21.5 %all-to-all-start.2 = ((s16[8,112,256]{2,1,0:T(8,128)(2,1)}), s16[8,112,256]{2,1,0:T(8,128)(2,1)S(1)}, u32[]{:S(2)}, u32[]{:S(2)}) async-start(s16[8,112,256]{2,1,0:T(8,128)(2,1)} %code_y.1), calls=%async_computation.2 | async-start | bytes 917504 | tf_op jit(solution)/shard_map/all_to_all | solution.py:316
  72.2 10.3 %collective-permute-start.7 = (s16[304,256]{1,0:T(8,128)(2,1)S(1)}, s16[304,256]{1,0:T(8,128)(2,1)S(1)}, u32[]{:S(2)}, u32[]{:S(2)}) collective-permute-start(s16[304,256]{1,0:T(8,128)(2,1)S(1)} %get-tuple-element.42), channel_id=1, source_target_pairs={{0,2},{1,3},{2,0},{3,1},{4,6},{5,7},{6,4},{7,5},{8,10},{9,11},{10,... | collective-permute-start | bytes 466952 | tf_op jit(solution)/shard_map/ppermute | solution.py:312
  75.2 8.5 %collective-permute-start.8 = (s16[304,256]{1,0:T(8,128)(2,1)S(1)}, s16[304,256]{1,0:T(8,128)(2,1)S(1)}, u32[]{:S(2)}, u32[]{:S(2)}) collective-permute-start(s16[304,256]{1,0:T(8,128)(2,1)S(1)} %get-tuple-element.43), channel_id=1, source_target_pairs={{0,1},{1,0},{2,3},{3,2},{4,5},{5,4},{6,7},{7,6},{8,9},{9,8},{10,11... | collective-permute-start | bytes 466952 | tf_op jit(solution)/shard_map/ppermute | solution.py:312
  78.3 7.5 %collective-permute-start.9 = (s16[304,256]{1,0:T(8,128)(2,1)S(1)}, s16[304,256]{1,0:T(8,128)(2,1)S(1)}, u32[]{:S(2)}, u32[]{:S(2)}) collective-permute-start(s16[304,256]{1,0:T(8,128)(2,1)S(1)} %get-tuple-element.44), channel_id=1, source_target_pairs={{0,3},{1,2},{2,1},{3,0},{4,7},{5,6},{6,5},{7,4},{8,11},{9,10},{10,... | collective-permute-start | bytes 466952 | tf_op jit(solution)/shard_map/ppermute | solution.py:312
  88.8 21.7 %all-to-all-start.3 = ((s16[6,64,256]{2,1,0:T(8,128)(2,1)}), s16[6,64,256]{2,1,0:T(8,128)(2,1)S(1)}, u32[]{:S(2)}, u32[]{:S(2)}) async-start(s16[6,64,256]{2,1,0:T(8,128)(2,1)} %sum_x.1), calls=%async_computation.3 | async-start | bytes 393216 | tf_op jit(solution)/shard_map/all_to_all | solution.py:316
  96.4 14.1 %collective-permute-start.6 = (f32[48,256]{1,0:T(8,128)S(1)}, f32[48,256]{1,0:T(8,128)S(1)}, u32[]{:S(2)}, u32[]{:S(2)}) collective-permute-start(f32[48,256]{1,0:T(8,128)S(1)} %get-tuple-element.40), channel_id=1, source_target_pairs={{0,384},{384,0},{1,385},{385,1},{2,386},{386,2},{3,387},{387,3},{4... | collective-permute-start | bytes 147464 | tf_op jit(solution)/shard_map/ppermute | solution.py:342

commit v11 on v8

--- a/solution.py
+++ b/solution.py
@@ -339,7 +339,7 @@
     coded_y, *parts = lax.optimization_barrier((coded_y, *parts))
     row_parts = trade(coded_y, "y")
 
-    col_line = sum_x(parts[0], *(swap_x(parts[k], k) for k in (1, 2, 3)))
+    col_line = sum_x(parts[0], *(swap_x(parts[k], k) for k in (2, 1, 3)))
     col_line = trade(col_line, "zl")
 
     row_near, row_send = sum_y(row_parts)

time: 113 us -> 112 us (level)
  no operation moved by 1% of the time
where the time goes in v11:
time: 112 us; the launch traced here: 111 us
  starting transfers between devices  73.2 us (65%)
  waiting for transfers between devices  17.9 us (16%)
  Pallas kernels  16.7 us (15%)
  local copies, waits for them, and re-layouts  3.08 us (3%)
    all_to_all x4, starting transfers between devices, trade(): return lax.all_to_all(block, axis, split_axis=0, concat_axis=0)  34.1 us
    ppermute x6, starting transfers between devices, swap_x(): return lax.ppermute(block, 'x', [(i, i ^ k) for i in range(4)])  19.6 us
    ppermute x6, waiting for transfers between devices, swap_x(): return lax.ppermute(block, 'x', [(i, i ^ k) for i in range(4)])  10.2 us
    ppermute x1, starting transfers between devices, per_device(): far = lax.ppermute(amplitudes, 'zh', SWAP)  10 us
    pallas_call x1, Pallas kernels, place(): pl.pallas_call(place_kernel, in_specs=[VMEM, HBM], out_specs=HBM, out_sha...  7.7 us
    all_to_all x4, waiting for transfers between devices, trade(): return lax.all_to_all(block, axis, split_axis=0, concat_axis=0)  5.99 us
    ppermute x1, starting transfers between devices, per_device(): row_far = lax.ppermute(row_send, 'zh', SWAP)  5.05 us
    unnamed x8, local copies, waits for them, and re-layouts  3.08 us
  transfers between devices with their start and end apart: 14, of which 5 were waited for; matrix products, arithmetic and copies ran while one was open for 0% of the time, Pallas kernels for 10%

profile of v11, /device:TPU:8, one launch (start us, length us, event | category | flops | bytes accessed | tf_op | source)
XLA Modules:
  0.0 111.1 jit_solution(11560659742484412575)
XLA Ops:
  0.0 0.0 copy-start.1
  0.0 0.7 copy-done.1
  0.7 0.0 copy-start.2
  0.7 0.7 copies.3
  1.4 12.1 %all-to-all-start.1 = ((bf16[6,48,256]{2,1,0:T(8,128)(2,1)}), bf16[6,48,256]{2,1,0:T(8,128)(2,1)S(1)}, u32[]{:S(2)}, u32[]{:S(2)}) async-start(bf16[6,48,256]{2,1,0:T(8,128)(2,1)} %copies.3), calls=%async_computation.1 | async-start | bytes 294912 | tf_op jit(solution)/shard_map/all_to_all | solution.py:320
  13.5 10.0 %collective-permute-start = (bf16[48,256]{1,0:T(8,128)(2,1)}, bf16[48,256]{1,0:T(8,128)(2,1)S(1)}, u32[]{:S(2)}, u32[]{:S(2)}) collective-permute-start(bf16[48,256]{1,0:T(8,128)(2,1)} %refs_0_.3), channel_id=1, source_target_pairs={{0,384},{384,0},{1,385},{385,1},{2,386},{386,2},{3,387},{387,3},{4... | collective-permute-start | bytes 73736 | tf_op jit(solution)/shard_map/ppermute | solution.py:324
  23.6 7.7 %place.1.x = bf16[1536,1536]{1,0:T(8,128)(2,1)} custom-call(s32[2,385]{1,0:T(2,128)} %bitcast.9, bf16[385,2304]{1,0:T(8,128)(2,1)} %bitcast.8), custom_call_target="tpu_custom_call" | custom-call | flops 2415919104 | bytes 8388608 | tf_op jit(solution)/shard_map/place/pallas_call | solution.py:89
  31.3 0.0 collective-permute-done.refs_1_
  31.3 0.0 copy-done.2
  31.3 0.8 copies.2
  32.1 0.0 all-to-all-done.1.block
  32.1 7.5 %all-to-all-start = ((bf16[8,96,256]{2,1,0:T(8,128)(2,1)}), bf16[8,96,256]{2,1,0:T(8,128)(2,1)S(1)}, u32[]{:S(2)}, u32[]{:S(2)}) async-start(bf16[8,96,256]{2,1,0:T(8,128)(2,1)} %copies.2), calls=%async_computation | async-start | bytes 786432 | tf_op jit(solution)/shard_map/all_to_all | solution.py:320
  39.6 4.7 %collective-permute-start.3 = (bf16[6,48,256]{2,1,0:T(8,128)(2,1)S(1)}, bf16[6,48,256]{2,1,0:T(8,128)(2,1)S(1)}, u32[]{:S(2)}, u32[]{:S(2)}) collective-permute-start(bf16[6,48,256]{2,1,0:T(8,128)(2,1)S(1)} %all-to-all-done.1.block), channel_id=1, source_target_pairs={{0,3},{1,2},{2,1},{3,0},{4,7},{5,6},{6,5},{7,4},{8,11},{9,10},{10,... | collective-permute-start | bytes 442376 | tf_op jit(solution)/shard_map/ppermute | solution.py:316
  44.3 2.7 %collective-permute-start.2 = (bf16[6,48,256]{2,1,0:T(8,128)(2,1)S(1)}, bf16[6,48,256]{2,1,0:T(8,128)(2,1)S(1)}, u32[]{:S(2)}, u32[]{:S(2)}) collective-permute-start(bf16[6,48,256]{2,1,0:T(8,128)(2,1)S(1)} %all-to-all-done.1.block), channel_id=1, source_target_pairs={{0,2},{1,3},{2,0},{3,1},{4,6},{5,7},{6,4},{7,5},{8,10},{9,11},{10,... | collective-permute-start | bytes 442376 | tf_op jit(solution)/shard_map/ppermute | solution.py:316
  47.0 2.4 %collective-permute-start.1 = (bf16[6,48,256]{2,1,0:T(8,128)(2,1)S(1)}, bf16[6,48,256]{2,1,0:T(8,128)(2,1)S(1)}, u32[]{:S(2)}, u32[]{:S(2)}) collective-permute-start(bf16[6,48,256]{2,1,0:T(8,128)(2,1)S(1)} %all-to-all-done.1.block), channel_id=1, source_target_pairs={{0,1},{1,0},{2,3},{3,2},{4,5},{5,4},{6,7},{7,6},{8,9},{9,8},{10,11... | collective-permute-start | bytes 442376 | tf_op jit(solution)/shard_map/ppermute | solution.py:316
  49.5 0.0 collective-permute-done.3.a3
  49.5 4.9 %collective-permute-done.2.a2 = bf16[6,48,256]{2,1,0:T(8,128)(2,1)S(1)} collective-permute-done((bf16[6,48,256]{2,1,0:T(8,128)(2,1)S(1)}, bf16[6,48,256]{2,1,0:T(8,128)(2,1)S(1)}, u32[]{:S(2)}, u32[]{:S(2)}) %collective-permute-start.2) | collective-permute-done | bytes 147488 | tf_op jit(solution)/shard_map/ppermute | solution.py:316
  54.3 0.0 collective-permute-done.1.a1
  54.3 0.0 all-to-all-done
  54.4 1.9 %collective-permute-start.4 = (bf16[768,256]{1,0:T(8,128)(2,1)S(1)}, bf16[768,256]{1,0:T(8,128)(2,1)S(1)}, u32[]{:S(2)}, u32[]{:S(2)}) collective-permute-start(bf16[768,256]{1,0:T(8,128)(2,1)S(1)} %bitcast.5), channel_id=1, source_target_pairs={{0,24},{24,0},{1,25},{25,1},{2,26},{26,2},{3,27},{27,3},{4,28},{28... | collective-permute-start | bytes 1179656 | tf_op jit(solution)/shard_map/ppermute | solution.py:331
  56.3 0.0 copy-start
  56.3 2.3 %copy-done = bf16[1536,1536]{1,0:T(8,128)(2,1)S(1)} copy-done((bf16[1536,1536]{1,0:T(8,128)(2,1)S(1)}, bf16[1536,1536]{1,0:T(8,128)(2,1)}, u32[]{:S(2)}) %copy-start) | copy-done | bytes 4718616
  58.6 0.0 collective-permute-done.4.other_ref
  58.6 2.5 %mirror.1 = (f32[768,256]{1,0:T(8,128)S(1)}, f32[768,256]{1,0:T(8,128)S(1)}) custom-call(bf16[1536,1536]{1,0:T(8,128)(2,1)S(1)} %copy-done, bf16[6,48,256]{2,1,0:T(8,128)(2,1)S(1)} %meet.1.a0, bf16[6,48,256]{2,1,0:T(8,128)(2,1)S(1)} %collective-permute-done.1.a1, bf16[6,48,256]{2,1,0:T(8,128)(2,1)S(1)} %collective-permute-done.2.a2, ...), custom_call_target="tpu_custom_call" | custom-call | flops 1207959552 | bytes 8388608 | tf_op jit(solution)/shard_map/mirror/pallas_call | solution.py:166
  61.1 0.0 copy-start.3
  61.2 2.5 %collective-permute-start.5 = (f32[768,256]{1,0:T(8,128)S(1)}, f32[768,256]{1,0:T(8,128)S(1)}, u32[]{:S(2)}, u32[]{:S(2)}) collective-permute-start(f32[768,256]{1,0:T(8,128)S(1)} %get-tuple-element.39), channel_id=1, source_target_pairs={{0,24},{24,0},{1,25},{25,1},{2,26},{26,2},{3,27},{27,3},{4,28},{28... | collective-permute-start | bytes 2359304 | tf_op jit(solution)/shard_map/ppermute | solution.py:335
  63.7 2.1 %direct.1 = (f32[288,256]{1,0:T(8,128)S(1)}, s16[304,256]{1,0:T(8,128)(2,1)S(1)}, s16[304,256]{1,0:T(8,128)(2,1)S(1)}, s16[304,256]{1,0:T(8,128)(2,1)S(1)}) custom-call(bf16[1536,1536]{1,0:T(8,128)(2,1)S(1)} %copy-done, bf16[768,256]{1,0:T(8,128)(2,1)S(1)} %bitcast.7, bf16[768,256]{1,0:T(8,128)(2,1)S(1)} %collective-permute-done.4.other_ref), custom_call_target="tpu_custom_call" | custom-call | flops 1207959552 | bytes 8388608 | tf_op jit(solution)/shard_map/direct/pallas_call | solution.py:226
  65.8 0.0 collective-permute-done.5.got
  65.8 1.2 %code_y.1 = s16[8,112,256]{2,1,0:T(8,128)(2,1)} custom-call(f32[768,256]{1,0:T(8,128)S(1)} %get-tuple-element.38.keep, f32[768,256]{1,0:T(8,128)S(1)} %collective-permute-done.5.got), custom_call_target="tpu_custom_call" | custom-call | tf_op jit(solution)/shard_map/code_y/pallas_call | solution.py:253
  67.0 7.2 %all-to-all-start.2 = ((s16[8,112,256]{2,1,0:T(8,128)(2,1)}), s16[8,112,256]{2,1,0:T(8,128)(2,1)S(1)}, u32[]{:S(2)}, u32[]{:S(2)}) async-start(s16[8,112,256]{2,1,0:T(8,128)(2,1)} %code_y.1), calls=%async_computation.2 | async-start | bytes 917504 | tf_op jit(solution)/shard_map/all_to_all | solution.py:320
  74.2 4.4 %collective-permute-start.7 = (s16[304,256]{1,0:T(8,128)(2,1)S(1)}, s16[304,256]{1,0:T(8,128)(2,1)S(1)}, u32[]{:S(2)}, u32[]{:S(2)}) collective-permute-start(s16[304,256]{1,0:T(8,128)(2,1)S(1)} %get-tuple-element.54), channel_id=1, source_target_pairs={{0,2},{1,3},{2,0},{3,1},{4,6},{5,7},{6,4},{7,5},{8,10},{9,11},{10,... | collective-permute-start | bytes 466952 | tf_op jit(solution)/shard_map/ppermute | solution.py:316
  78.6 2.4 %collective-permute-start.8 = (s16[304,256]{1,0:T(8,128)(2,1)S(1)}, s16[304,256]{1,0:T(8,128)(2,1)S(1)}, u32[]{:S(2)}, u32[]{:S(2)}) collective-permute-start(s16[304,256]{1,0:T(8,128)(2,1)S(1)} %get-tuple-element.55), channel_id=1, source_target_pairs={{0,1},{1,0},{2,3},{3,2},{4,5},{5,4},{6,7},{7,6},{8,9},{9,8},{10,11... | collective-permute-start | bytes 466952 | tf_op jit(solution)/shard_map/ppermute | solution.py:316
  81.0 3.0 %collective-permute-start.9 = (s16[304,256]{1,0:T(8,128)(2,1)S(1)}, s16[304,256]{1,0:T(8,128)(2,1)S(1)}, u32[]{:S(2)}, u32[]{:S(2)}) collective-permute-start(s16[304,256]{1,0:T(8,128)(2,1)S(1)} %get-tuple-element.56), channel_id=1, source_target_pairs={{0,3},{1,2},{2,1},{3,0},{4,7},{5,6},{6,5},{7,4},{8,11},{9,10},{10,... | collective-permute-start | bytes 466952 | tf_op jit(solution)/shard_map/ppermute | solution.py:316
  84.0 0.0 collective-permute-done.7.c1
  84.0 1.9 %collective-permute-done.8.c2 = s16[304,256]{1,0:T(8,128)(2,1)S(1)} collective-permute-done((s16[304,256]{1,0:T(8,128)(2,1)S(1)}, s16[304,256]{1,0:T(8,128)(2,1)S(1)}, u32[]{:S(2)}, u32[]{:S(2)}) %collective-permute-start.8) | collective-permute-done | bytes 155680 | tf_op jit(solution)/shard_map/ppermute | solution.py:316
  85.9 3.4 %collective-permute-done.9.c3 = s16[304,256]{1,0:T(8,128)(2,1)S(1)} collective-permute-done((s16[304,256]{1,0:T(8,128)(2,1)S(1)}, s16[304,256]{1,0:T(8,128)(2,1)S(1)}, u32[]{:S(2)}, u32[]{:S(2)}) %collective-permute-start.9) | collective-permute-done | bytes 155680 | tf_op jit(solution)/shard_map/ppermute | solution.py:316
  89.4 0.9 sum_x.1
  90.3 0.0 all-to-all-done.2.coded
  90.3 7.2 %all-to-all-start.3 = ((s16[6,64,256]{2,1,0:T(8,128)(2,1)}), s16[6,64,256]{2,1,0:T(8,128)(2,1)S(1)}, u32[]{:S(2)}, u32[]{:S(2)}) async-start(s16[6,64,256]{2,1,0:T(8,128)(2,1)} %sum_x.1), calls=%async_computation.3 | async-start | bytes 393216 | tf_op jit(solution)/shard_map/all_to_all | solution.py:320
  97.5 0.1 sum_y.1
  97.6 5.0 %collective-permute-start.6 = (s16[64,256]{1,0:T(8,128)(2,1)S(1)}, s16[64,256]{1,0:T(8,128)(2,1)S(1)}, u32[]{:S(2)}, u32[]{:S(2)}) collective-permute-start(s16[64,256]{1,0:T(8,128)(2,1)S(1)} %get-tuple-element.52), channel_id=1, source_target_pairs={{0,384},{384,0},{1,385},{385,1},{2,386},{386,2},{3,387},{387,3},{4... | collective-permute-start | bytes 98312 | tf_op jit(solution)/shard_map/ppermute | solution.py:346
  102.7 6.0 %all-to-all-done.3.coded = s16[6,64,256]{2,1,0:T(8,128)(2,1)S(1)} async-done(((s16[6,64,256]{2,1,0:T(8,128)(2,1)}), s16[6,64,256]{2,1,0:T(8,128)(2,1)S(1)}, u32[]{:S(2)}, u32[]{:S(2)}) %all-to-all-start.3) | async-done | bytes 196640 | tf_op jit(solution)/shard_map/all_to_all | solution.py:320
  108.7 1.7 %collective-permute-done.6.far = s16[64,256]{1,0:T(8,128)(2,1)S(1)} collective-permute-done((s16[64,256]{1,0:T(8,128)(2,1)S(1)}, s16[64,256]{1,0:T(8,128)(2,1)S(1)}, u32[]{:S(2)}, u32[]{:S(2)}) %collective-permute-start.6) | collective-permute-done | bytes 32800 | tf_op jit(solution)/shard_map/ppermute | solution.py:346
  110.4 0.0 copy-done.3
  110.4 0.7 end.1
  (1 shorter events, 0.0 us)
Async XLA Ops:
  0.0 0.7 copy-start.1
  0.7 30.5 %copy-start.2 = (bf16[48,256]{1,0:T(8,128)(2,1)S(1)}, bf16[48,256]{1,0:T(8,128)(2,1)}, u32[]{:S(2)}) copy-start(bf16[48,256]{1,0:T(8,128)(2,1)} %refs_0_.3) | copy-start | bytes 73732
  1.4 30.6 %all-to-all-start.1 = ((bf16[6,48,256]{2,1,0:T(8,128)(2,1)}), bf16[6,48,256]{2,1,0:T(8,128)(2,1)S(1)}, u32[]{:S(2)}, u32[]{:S(2)}) async-start(bf16[6,48,256]{2,1,0:T(8,128)(2,1)} %copies.3), calls=%async_computation.1 | async-start | bytes 294912 | tf_op jit(solution)/shard_map/all_to_all | solution.py:320
  13.5 17.7 %collective-permute-start = (bf16[48,256]{1,0:T(8,128)(2,1)}, bf16[48,256]{1,0:T(8,128)(2,1)S(1)}, u32[]{:S(2)}, u32[]{:S(2)}) collective-permute-start(bf16[48,256]{1,0:T(8,128)(2,1)} %refs_0_.3), channel_id=1, source_target_pairs={{0,384},{384,0},{1,385},{385,1},{2,386},{386,2},{3,387},{387,3},{4... | collective-permute-start | bytes 73736 | tf_op jit(solution)/shard_map/ppermute | solution.py:324
  32.1 22.3 %all-to-all-start = ((bf16[8,96,256]{2,1,0:T(8,128)(2,1)}), bf16[8,96,256]{2,1,0:T(8,128)(2,1)S(1)}, u32[]{:S(2)}, u32[]{:S(2)}) async-start(bf16[8,96,256]{2,1,0:T(8,128)(2,1)} %copies.2), calls=%async_computation | async-start | bytes 786432 | tf_op jit(solution)/shard_map/all_to_all | solution.py:320
  39.6 9.8 %collective-permute-start.3 = (bf16[6,48,256]{2,1,0:T(8,128)(2,1)S(1)}, bf16[6,48,256]{2,1,0:T(8,128)(2,1)S(1)}, u32[]{:S(2)}, u32[]{:S(2)}) collective-permute-start(bf16[6,48,256]{2,1,0:T(8,128)(2,1)S(1)} %all-to-all-done.1.block), channel_id=1, source_target_pairs={{0,3},{1,2},{2,1},{3,0},{4,7},{5,6},{6,5},{7,4},{8,11},{9,10},{10,... | collective-permute-start | bytes 442376 | tf_op jit(solution)/shard_map/ppermute | solution.py:316
  44.3 10.1 %collective-permute-start.2 = (bf16[6,48,256]{2,1,0:T(8,128)(2,1)S(1)}, bf16[6,48,256]{2,1,0:T(8,128)(2,1)S(1)}, u32[]{:S(2)}, u32[]{:S(2)}) collective-permute-start(bf16[6,48,256]{2,1,0:T(8,128)(2,1)S(1)} %all-to-all-done.1.block), channel_id=1, source_target_pairs={{0,2},{1,3},{2,0},{3,1},{4,6},{5,7},{6,4},{7,5},{8,10},{9,11},{10,... | collective-permute-start | bytes 442376 | tf_op jit(solution)/shard_map/ppermute | solution.py:316
  47.0 7.3 %collective-permute-start.1 = (bf16[6,48,256]{2,1,0:T(8,128)(2,1)S(1)}, bf16[6,48,256]{2,1,0:T(8,128)(2,1)S(1)}, u32[]{:S(2)}, u32[]{:S(2)}) collective-permute-start(bf16[6,48,256]{2,1,0:T(8,128)(2,1)S(1)} %all-to-all-done.1.block), channel_id=1, source_target_pairs={{0,1},{1,0},{2,3},{3,2},{4,5},{5,4},{6,7},{7,6},{8,9},{9,8},{10,11... | collective-permute-start | bytes 442376 | tf_op jit(solution)/shard_map/ppermute | solution.py:316
  54.4 4.3 %collective-permute-start.4 = (bf16[768,256]{1,0:T(8,128)(2,1)S(1)}, bf16[768,256]{1,0:T(8,128)(2,1)S(1)}, u32[]{:S(2)}, u32[]{:S(2)}) collective-permute-start(bf16[768,256]{1,0:T(8,128)(2,1)S(1)} %bitcast.5), channel_id=1, source_target_pairs={{0,24},{24,0},{1,25},{25,1},{2,26},{26,2},{3,27},{27,3},{4,28},{28... | collective-permute-start | bytes 1179656 | tf_op jit(solution)/shard_map/ppermute | solution.py:331
  56.3 2.3 %copy-start = (bf16[1536,1536]{1,0:T(8,128)(2,1)S(1)}, bf16[1536,1536]{1,0:T(8,128)(2,1)}, u32[]{:S(2)}) copy-start(bf16[1536,1536]{1,0:T(8,128)(2,1)} %place.1.x) | copy-start | bytes 14155780
  61.1 49.2 %copy-start.3 = (f32[48,256]{1,0:T(8,128)S(1)}, f32[48,256]{1,0:T(8,128)}, u32[]{:S(2)}) copy-start(f32[48,256]{1,0:T(8,128)} %residual.1) | copy-start | bytes 147460
  61.2 4.6 %collective-permute-start.5 = (f32[768,256]{1,0:T(8,128)S(1)}, f32[768,256]{1,0:T(8,128)S(1)}, u32[]{:S(2)}, u32[]{:S(2)}) collective-permute-start(f32[768,256]{1,0:T(8,128)S(1)} %get-tuple-element.39), channel_id=1, source_target_pairs={{0,24},{24,0},{1,25},{25,1},{2,26},{26,2},{3,27},{27,3},{4,28},{28... | collective-permute-start | bytes 2359304 | tf_op jit(solution)/shard_map/ppermute | solution.py:335
  67.0 23.3 %all-to-all-start.2 = ((s16[8,112,256]{2,1,0:T(8,128)(2,1)}), s16[8,112,256]{2,1,0:T(8,128)(2,1)S(1)}, u32[]{:S(2)}, u32[]{:S(2)}) async-start(s16[8,112,256]{2,1,0:T(8,128)(2,1)} %code_y.1), calls=%async_computation.2 | async-start | bytes 917504 | tf_op jit(solution)/shard_map/all_to_all | solution.py:320
  74.2 9.8 %collective-permute-start.7 = (s16[304,256]{1,0:T(8,128)(2,1)S(1)}, s16[304,256]{1,0:T(8,128)(2,1)S(1)}, u32[]{:S(2)}, u32[]{:S(2)}) collective-permute-start(s16[304,256]{1,0:T(8,128)(2,1)S(1)} %get-tuple-element.54), channel_id=1, source_target_pairs={{0,2},{1,3},{2,0},{3,1},{4,6},{5,7},{6,4},{7,5},{8,10},{9,11},{10,... | collective-permute-start | bytes 466952 | tf_op jit(solution)/shard_map/ppermute | solution.py:316
  78.6 7.4 %collective-permute-start.8 = (s16[304,256]{1,0:T(8,128)(2,1)S(1)}, s16[304,256]{1,0:T(8,128)(2,1)S(1)}, u32[]{:S(2)}, u32[]{:S(2)}) collective-permute-start(s16[304,256]{1,0:T(8,128)(2,1)S(1)} %get-tuple-element.55), channel_id=1, source_target_pairs={{0,1},{1,0},{2,3},{3,2},{4,5},{5,4},{6,7},{7,6},{8,9},{9,8},{10,11... | collective-permute-start | bytes 466952 | tf_op jit(solution)/shard_map/ppermute | solution.py:316
  81.0 8.3 %collective-permute-start.9 = (s16[304,256]{1,0:T(8,128)(2,1)S(1)}, s16[304,256]{1,0:T(8,128)(2,1)S(1)}, u32[]{:S(2)}, u32[]{:S(2)}) collective-permute-start(s16[304,256]{1,0:T(8,128)(2,1)S(1)} %get-tuple-element.56), channel_id=1, source_target_pairs={{0,3},{1,2},{2,1},{3,0},{4,7},{5,6},{6,5},{7,4},{8,11},{9,10},{10,... | collective-permute-start | bytes 466952 | tf_op jit(solution)/shard_map/ppermute | solution.py:316
  90.3 18.4 %all-to-all-start.3 = ((s16[6,64,256]{2,1,0:T(8,128)(2,1)}), s16[6,64,256]{2,1,0:T(8,128)(2,1)S(1)}, u32[]{:S(2)}, u32[]{:S(2)}) async-start(s16[6,64,256]{2,1,0:T(8,128)(2,1)} %sum_x.1), calls=%async_computation.3 | async-start | bytes 393216 | tf_op jit(solution)/shard_map/all_to_all | solution.py:320
  97.6 12.7 %collective-permute-start.6 = (s16[64,256]{1,0:T(8,128)(2,1)S(1)}, s16[64,256]{1,0:T(8,128)(2,1)S(1)}, u32[]{:S(2)}, u32[]{:S(2)}) collective-permute-start(s16[64,256]{1,0:T(8,128)(2,1)S(1)} %get-tuple-element.52), channel_id=1, source_target_pairs={{0,384},{384,0},{1,385},{385,1},{2,386},{386,2},{3,387},{387,3},{4... | collective-permute-start | bytes 98312 | tf_op jit(solution)/shard_map/ppermute | solution.py:346
